TPU v7x, 256 devices: a whole 4x4x8 slice. The times are simulated.
256 devices in a mesh: blk: 8 (over z_hi, x), group: 2 (over core), tp: 16 (over y, z_lo).
Axes of the slice: x: 4, y: 4, z: 8 (z_hi: 2, z_lo: 4; z = z_hi * 4 + z_lo), core: 2. Of those that a mesh axis runs over, the one named last changes fastest.
Arguments:
- prompt_query: bfloat16 [2, 2048, 8192], P('group', 'blk', 'tp'), may hold values from -9 to 9
- context_cache: bfloat16 [2, 2, 2048, 1024], P('group', None, 'blk', 'tp'), may hold values from -4 to 4
- new_block_cache: bfloat16 [2, 2, 2048, 1024], P('group', None, 'blk', 'tp'), may hold values from -4 to 4
- block_offset: int32 [2], replicated, may hold values from 512 to 2048
- page_owner: int32 [2, 128, 1], P('group', 'blk'), may hold values from 0 to 15; in each aligned block of 16 rows (0 to 15, 16 to 31, ..., all dimensions but the last counted through in order) at most 2 rows name the same one
- step_query: bfloat16 [16, 4, 16, 8192], P(('blk', 'group'), None, None, 'tp'), may hold values from -9 to 9
- step_cache: bfloat16 [16, 4, 2, 16, 2048], P(('blk', 'group'), None, None, None, 'tp'), may hold values from -4 to 4
- row_cache: bfloat16 [16, 2, 16, 256, 2048], P(('blk', 'group'), None, None, None, 'tp'), may hold values from -4 to 4
- row_lengths: int32 [16, 16], P(('blk', 'group')), may hold values from 2 to 256
- out_weight: bfloat16 [8192, 8192], P('tp'), may hold values from -0.0625 to 0.0625
- residual: bfloat16 [16, 4, 16, 8192], P(('blk', 'group'), None, None, 'tp'), may hold values from -48 to 48
- norm_gain: bfloat16 [8192], P('tp'), may hold values from 0.5 to 1.5
Outputs:
- prefill_out: bfloat16 [2, 2048, 8192], P('group', 'blk', 'tp')
- page_pool: bfloat16 [16, 32, 2, 16, 2048], P(('blk', 'group'), None, None, None, 'tp')
- decode_out: bfloat16 [16, 4, 16, 8192], P(('blk', 'group'), None, None, 'tp')
Inputs may be any that keep to these rules, and one draw needn't show every extreme that they name: `page_owner`: among the 16 pages of one blk index of a prompt, each instance is named at most 2 times.
All inputs are finite; a program needn't handle non-finite values.
Results may differ from a plain program's by a relative error of at most 0.0029.
Values may be sent and summed in bfloat16 or wider, within the bound.
No kernel may reach another device: no remote copies, remote signals or barrier semaphores. Data moves between devices by JAX's collectives and lax.ppermute only.
A program may use at most 64 MiB of HBM per device.

v0:
```python
import math

import jax
import jax.numpy as jnp
from jax import lax
from jax.sharding import PartitionSpec as P

HEAD_SIZE = 128
PAGE_TOKENS = 16
STEPS = 4


LOW_SCORE = -1e30
EPSILON = 1e-05


def from_partner(x, axis, stride):
    return lax.ppermute(x, axis, [(i, i ^ 1 << stride) for i in range(lax.axis_size(axis))])


def join_halves(mine, partner, is_odd):
    first_order = jnp.concatenate([mine, partner], axis=-1)
    second_order = jnp.concatenate([partner, mine], axis=-1)
    return jnp.where(is_odd, second_order, first_order)


def pick_entry(table, position):
    places = lax.iota(jnp.int32, table.shape[0])
    return jnp.sum(jnp.where(places == position, table, 0))


def fold_slab(state_now, queries, query_pos, context_slab, block_slab, key_start, offset):
    maxima, totals, accumulated = state_now
    slab_width = context_slab.shape[1]
    key_pos = key_start + lax.iota(jnp.int32, slab_width)
    scaling = queries.shape[-1] ** (-0.5)
    score_context = (
        jnp.einsum("qhd,kd->qhk", queries, context_slab[0], preferred_element_type=jnp.float32)
        * scaling
    )
    score_block = (
        jnp.einsum("qhd,kd->qhk", queries, block_slab[0], preferred_element_type=jnp.float32)
        * scaling
    )
    open_context = (key_pos < offset)[None, None, :]
    open_block = (key_pos[None, :] <= query_pos[:, None])[:, None, :]
    score_context = jnp.where(open_context, score_context, LOW_SCORE)
    score_block = jnp.where(open_block, score_block, LOW_SCORE)
    highest = jnp.maximum(
        maxima, jnp.maximum(jnp.max(score_context, axis=-1), jnp.max(score_block, axis=-1))
    )
    weight_context = jnp.where(open_context, jnp.exp(score_context - highest[..., None]), 0.0)
    weight_block = jnp.where(open_block, jnp.exp(score_block - highest[..., None]), 0.0)
    shrink = jnp.exp(maxima - highest)
    totals = totals * shrink + jnp.sum(weight_context, axis=-1) + jnp.sum(weight_block, axis=-1)
    accumulated = accumulated * shrink[..., None]
    accumulated = accumulated + jnp.einsum(
        "qhk,kd->qhd",
        weight_context,
        context_slab[1].astype(jnp.float32),
        precision=lax.Precision.HIGHEST,
        preferred_element_type=jnp.float32,
    )
    accumulated = accumulated + jnp.einsum(
        "qhk,kd->qhd",
        weight_block,
        block_slab[1].astype(jnp.float32),
        precision=lax.Precision.HIGHEST,
        preferred_element_type=jnp.float32,
    )
    return (highest, totals, accumulated)


def finish_rows(partials, residual_part, norm_gain):
    share_width = residual_part.shape[-1]
    corner = lax.axis_index("tp") * share_width
    placed = lax.dynamic_update_slice_in_dim(
        jnp.zeros_like(partials), residual_part.astype(jnp.float32), corner, 2
    )
    whole = lax.psum(partials + placed, "tp")
    mean_square = jnp.mean(whole * whole, axis=-1)
    hidden = lax.dynamic_slice_in_dim(whole, corner, share_width, 2)
    scaled = hidden * lax.rsqrt(mean_square + EPSILON)[..., None]
    return (scaled * norm_gain.astype(jnp.float32)).astype(jnp.bfloat16)


def body(
    prompt_query,
    context_cache,
    new_block_cache,
    block_offset,
    page_owner,
    step_query,
    step_cache,
    row_cache,
    row_lengths,
    out_weight,
    residual,
    norm_gain,
):
    is_odd = lax.axis_index("tp") % 2 == 1
    other_context, other_block = from_partner((context_cache, new_block_cache), "tp", 0)
    context_full = join_halves(context_cache, other_context, is_odd)[0]
    block_full = join_halves(new_block_cache, other_block, is_odd)[0]
    offset = pick_entry(block_offset, lax.axis_index("group"))
    rows_here = prompt_query.shape[1]
    heads_here = prompt_query.shape[2] // HEAD_SIZE
    queries = prompt_query[0].reshape(rows_here, heads_here, HEAD_SIZE)
    query_pos = lax.axis_index("blk") * rows_here + lax.iota(jnp.int32, rows_here)
    initial = (
        jnp.full((rows_here, heads_here), LOW_SCORE, jnp.float32),
        jnp.zeros((rows_here, heads_here), jnp.float32),
        jnp.zeros((rows_here, heads_here, HEAD_SIZE), jnp.float32),
    )
    state_now = initial
    anchor = jnp.int32(0)
    context_piece = lax.all_gather(context_full, "blk", axis=1, tiled=True)
    block_piece = lax.all_gather(block_full, "blk", axis=1, tiled=True)
    key_count = context_piece.shape[1]
    slab_width = math.gcd(key_count, rows_here)
    for first_key in range(0, key_count, slab_width):
        state_now = fold_slab(
            state_now,
            queries,
            query_pos,
            context_piece[:, first_key : first_key + slab_width],
            block_piece[:, first_key : first_key + slab_width],
            anchor + first_key,
            offset,
        )
    maxima, totals, accumulated = state_now
    prefill_out = (
        (accumulated / totals[..., None])
        .astype(jnp.bfloat16)
        .reshape(1, rows_here, heads_here * HEAD_SIZE)
    )
    owners = page_owner[0, :, 0]
    page_count = owners.shape[0]
    instances = lax.axis_size(("blk", "group"))
    capacity = 2 * page_count // instances
    page_order = lax.iota(jnp.int32, page_count)
    earlier = (owners[None, :] == owners[:, None]) & (page_order[None, :] < page_order[:, None])
    ranks = jnp.sum(earlier.astype(jnp.int32), axis=1)
    targets = owners * capacity + ranks
    chooser = (lax.iota(jnp.int32, instances * capacity)[:, None] == targets[None, :]).astype(
        jnp.bfloat16
    )
    columns = block_full.shape[-1]
    paged_cache = block_full.reshape(2, page_count, PAGE_TOKENS, columns)
    packed = jnp.einsum(
        "sp,kptc->sktc", chooser, paged_cache, preferred_element_type=jnp.float32
    ).astype(jnp.bfloat16)
    packed = packed.reshape(instances, capacity, 2, PAGE_TOKENS, columns)
    arrived = lax.all_to_all(packed, ("blk", "group"), split_axis=0, concat_axis=0, tiled=True)
    arrived = arrived.reshape(instances * capacity, 2, PAGE_TOKENS, columns)
    page_pool = arrived[None]
    step_queries = step_query[0]
    step_pairs = step_cache[0]
    cache_pair = row_cache[0]
    lengths = row_lengths[0]
    decode_rows = step_queries.shape[1]
    cache_len = cache_pair.shape[2]
    per_tensor = step_queries.shape[2] // HEAD_SIZE
    scaling = HEAD_SIZE ** (-0.5)
    live = (lax.iota(jnp.int32, cache_len)[None, :] < lengths[:, None])[:, None, :]
    outputs = []
    for number in range(STEPS):
        query_now = step_queries[number].reshape(decode_rows, per_tensor, HEAD_SIZE)
        new_keys = step_pairs[: number + 1, 0]
        new_values = step_pairs[: number + 1, 1]
        score_old = (
            jnp.einsum("rhd,rld->rhl", query_now, cache_pair[0], preferred_element_type=jnp.float32)
            * scaling
        )
        score_old = jnp.where(live, score_old, LOW_SCORE)
        score_new = (
            jnp.einsum("rhd,srd->rhs", query_now, new_keys, preferred_element_type=jnp.float32)
            * scaling
        )
        highest = jnp.maximum(jnp.max(score_old, axis=-1), jnp.max(score_new, axis=-1))[..., None]
        weight_old = jnp.where(live, jnp.exp(score_old - highest), 0.0)
        weight_new = jnp.exp(score_new - highest)
        row_totals = jnp.sum(weight_old, axis=-1) + jnp.sum(weight_new, axis=-1)
        mixed = jnp.einsum(
            "rhl,rld->rhd",
            weight_old.astype(jnp.bfloat16),
            cache_pair[1],
            preferred_element_type=jnp.float32,
        )
        mixed = mixed + jnp.einsum(
            "rhs,srd->rhd",
            weight_new.astype(jnp.bfloat16),
            new_values,
            preferred_element_type=jnp.float32,
        )
        attended = (
            (mixed / row_totals[..., None])
            .astype(jnp.bfloat16)
            .reshape(decode_rows, per_tensor * HEAD_SIZE)
        )
        partial_value = jnp.dot(attended, out_weight, preferred_element_type=jnp.float32)
        outputs.append(
            finish_rows(partial_value[None], residual[0, number : number + 1], norm_gain)
        )
    decode_out = jnp.concatenate(outputs, axis=0)
    return (prefill_out, page_pool, decode_out[None])


def solution(mesh):
    placed = (
        P("group", "blk", "tp"),
        P("group", None, "blk", "tp"),
        P("group", None, "blk", "tp"),
        P(),
        P("group", "blk", None),
        P(("blk", "group"), None, None, "tp"),
        P(("blk", "group"), None, None, None, "tp"),
        P(("blk", "group"), None, None, None, "tp"),
        P(("blk", "group"), None),
        P("tp", None),
        P(("blk", "group"), None, None, "tp"),
        P("tp"),
    )
    return jax.shard_map(
        body,
        mesh=mesh,
        in_specs=placed,
        out_specs=(
            P("group", "blk", "tp"),
            P(("blk", "group"), None, None, None, "tp"),
            P(("blk", "group"), None, None, "tp"),
        ),
        check_vma=False,
    )
```

profile of v0, /device:TPU:6, one launch (start us, length us, event | category | flops | bytes accessed | tf_op | source)
XLA Modules:
  0.0 260.5 jit_solution(879450844509725244)
XLA Ops:
  8.1 1.1 copy.254
  9.2 2.0 collective-permute-start
  11.2 1.0 copy.257
  12.3 0.8 fusion.236
  13.1 0.7 iota_compare_fusion.1
  13.8 0.8 copy.454
  14.8 1.7 fusion.253
  16.5 1.7 fusion.254
  18.3 0.5 fusion.256
  19.0 0.5 fusion.258
  21.0 0.8 maximum_select_fusion
  22.2 4.6 %fusion.184 = f32[16,8192]{1,0:T(8,128)S(1)} fusion(bf16[512,8192]{1,0:T(8,128)(2,1)} %param.21, bf16[2,8,4,128]{3,2,1,0:T(4,128)(2,1)S(1)} %bitcast.395), kind=kOutput, calls=%fused_computation.301 | convolution fusion | flops 134217728 | bytes 8929280 | tf_op jit(solution)/shard_map/dot_general | solution.py:201
  26.7 4.6 %fusion.178 = f32[16,8192]{1,0:T(8,128)S(1)} fusion(bf16[512,8192]{1,0:T(8,128)(2,1)} %param.21, bf16[2,8,4,128]{3,2,1,0:T(4,128)(2,1)S(1)} %bitcast.393), kind=kOutput, calls=%fused_computation.295 | convolution fusion | flops 134217728 | bytes 8929280 | tf_op jit(solution)/shard_map/dot_general | solution.py:201
  31.7 0.8 maximum_select_fusion.1
  32.6 4.7 %fusion.175 = f32[16,8192]{1,0:T(8,128)S(1)} fusion(bf16[512,8192]{1,0:T(8,128)(2,1)} %param.21, bf16[2,8,4,128]{3,2,1,0:T(4,128)(2,1)S(1)} %bitcast.394), kind=kOutput, calls=%fused_computation.292 | convolution fusion | flops 134217728 | bytes 8929280 | tf_op jit(solution)/shard_map/dot_general | solution.py:201
  37.3 0.8 copy.457
  38.7 0.6 slice-done.1
  39.3 1.2 fusion.181
  40.5 0.8 copy.458
  41.4 0.7 fusion.156
  42.0 0.8 copy-done
  43.1 0.6 fusion.199
  43.7 0.7 iota_compare_fusion.4
  44.4 1.2 broadcast_compare_fusion.8
  45.6 1.2 broadcast_compare_fusion.10
  47.5 1.0 copy.308
  48.5 11.4 %all-to-all-start = ((bf16[16,2,2,16,128]{4,1,3,2,0:T(2,128)(2,1)}), bf16[16,2,2,16,128]{4,1,3,2,0:T(2,128)(2,1)S(1)}, u32[]{:S(2)}, u32[]{:S(2)}) async-start(bf16[16,2,2,16,128]{4,1,3,2,0:T(2,128)(2,1)} %copy.308), calls=%async_computation | async-start | bytes 524288 | tf_op jit(solution)/shard_map/all_to_all | solution.py:154
  59.9 1.2 broadcast_compare_fusion.12
  61.3 1.0 iota_compare_fusion
  62.3 9.9 %all-to-all-done = bf16[16,2,2,16,128]{4,1,3,2,0:T(2,128)(2,1)S(1)} async-done(((bf16[16,2,2,16,128]{4,1,3,2,0:T(2,128)(2,1)}), bf16[16,2,2,16,128]{4,1,3,2,0:T(2,128)(2,1)S(1)}, u32[]{:S(2)}, u32[]{:S(2)}) %all-to-all-start) | async-done | bytes 262176 | tf_op jit(solution)/shard_map/all_to_all | solution.py:154
  72.2 0.8 copy.309
  72.9 10.3 %all-gather.3.cloned.1.call-done = bf16[2,2048,128]{2,1,0:T(8,128)(2,1)} async-done(((bf16[2,256,128]{2,1,0:T(8,128)(2,1)}), bf16[2,2048,128]{2,1,0:T(8,128)(2,1)}) %all-gather.3.cloned.1.call-update) | async-done | bytes 1048592 | tf_op jit(solution)/shard_map/all_gather | solution.py:117
  83.2 1.2 fusion.251
  84.4 1.2 fusion.237
  85.5 1.2 fusion.239
  86.7 68.7 %all-gather.5.cloned.1.call-done = bf16[2,2048,128]{2,1,0:T(8,128)(2,1)} async-done(((bf16[2,256,128]{2,1,0:T(8,128)(2,1)}), bf16[2,2048,128]{2,1,0:T(8,128)(2,1)}) %all-gather.5.cloned.1.call-update) | async-done | bytes 1048592 | tf_op jit(solution)/shard_map/all_gather | solution.py:118
  155.4 1.4 fusion.238
  156.8 1.2 fusion.240
  158.0 1.0 fusion.241
  162.9 0.4 fusion.78
  163.4 0.4 fusion.76
  163.8 0.4 fusion.74
  165.8 0.7 convolution_add_fusion.15
  166.5 0.7 fusion.39
  167.2 0.7 convolution_add_fusion.13
  167.9 0.7 fusion.38
  168.6 0.7 convolution_add_fusion.11
  169.3 0.9 fusion.37
  170.2 0.7 convolution_add_fusion.9
  170.9 0.7 fusion.36
  171.6 0.7 convolution_add_fusion.7
  172.3 0.7 fusion.35
  172.9 0.7 convolution_add_fusion.5
  173.6 0.7 fusion.34
  174.3 0.7 convolution_add_fusion.3
  175.0 0.7 fusion.33
  175.7 0.7 convolution_add_fusion.1
  176.4 0.7 fusion.40
  177.1 0.8 copy.313
  177.9 70.8 %all-reduce.3.cloned.1.call-done = (f32[1,16,8192]{2,1,0:T(8,128)}, f32[1,16,8192]{2,1,0:T(8,128)}, f32[1,16,8192]{2,1,0:T(8,128)}, f32[1,16,8192]{2,1,0:T(8,128)}) async-done(((f32[1,16,8192]{2,1,0:T(8,128)}, f32[1,16,8192]{2,1,0:T(8,128)}, f32[1,16,8192]{2,1,0:T(8,128)}, f32[1,16,8192]{2,1,0:T(8,128)}), (f32[1,16,8192]{2,1,0:T(8,128)}, f32[1,16,8192]{2,1,0:T(8,128)}, f32[1,16,8192]{2,1,0:T(8,128)}, ...) | async-done | bytes 2097168 | tf_op jit(solution)/shard_map/psum | solution.py:80
  248.7 1.4 multiply_reduce_fusion.2
  250.1 1.4 multiply_reduce_fusion
  251.5 0.9 multiply_convert_fusion.3
  252.4 0.6 maximum_bitcast_fusion
  (128 shorter events, 9.8 us)
Async XLA Ops:
  8.0 10.3 %copy-start.23 = (bf16[1,2,16,256,128]{4,3,2,1,0:T(8,128)(2,1)S(1)}, bf16[1,2,16,256,128]{4,3,2,1,0:T(8,128)(2,1)}, u32[]{:S(2)}) copy-start(bf16[1,2,16,256,128]{4,3,2,1,0:T(8,128)(2,1)} %param.19) | copy-start | bytes 6291460
  8.0 75.2 %all-gather.3.cloned.1.call-start = ((), (), s32[]{:S(2)}) async-start(), calls=%async_computation.1 | async-start | bytes 1179648 | tf_op jit(solution)/shard_map/all_gather | solution.py:117
  9.2 11.8 %collective-permute-start = (bf16[1,2,256,64]{3,2,1,0:T(8,128)(2,1)S(1)}, bf16[1,2,256,64]{3,2,1,0:T(8,128)(2,1)S(1)}, u32[]{:S(2)}, u32[]{:S(2)}) collective-permute-start(bf16[1,2,256,64]{3,2,1,0:T(8,128)(2,1)S(1)} %copy.254), channel_id=1, source_target_pairs={{0,1},{1,0},{2,3},{3,2},{4,5},{5,4},{6,7},{7,6},{8,9},{9,8},{10,11... | collective-permute-start | bytes 196616 | tf_op jit(solution)/shard_map/ppermute | solution.py:18
  12.1 19.5 %collective-permute-start.1 = (bf16[1,2,256,64]{3,2,1,0:T(8,128)(2,1)S(1)}, bf16[1,2,256,64]{3,2,1,0:T(8,128)(2,1)S(1)}, u32[]{:S(2)}, u32[]{:S(2)}) collective-permute-start(bf16[1,2,256,64]{3,2,1,0:T(8,128)(2,1)S(1)} %copy.257), channel_id=1, source_target_pairs={{0,1},{1,0},{2,3},{3,2},{4,5},{5,4},{6,7},{7,6},{8,9},{9,8},{10,11... | collective-permute-start | bytes 196616 | tf_op jit(solution)/shard_map/ppermute | solution.py:18
  21.8 133.6 %all-gather.5.cloned.1.call-start = ((), (), s32[]{:S(2)}) async-start(), calls=%async_computation.2 | async-start | bytes 1179648 | tf_op jit(solution)/shard_map/all_gather | solution.py:118
  32.5 216.2 %all-reduce.3.cloned.1.call-start = ((), (), s32[]{:S(2)}) async-start(), calls=%async_computation.3 | async-start | bytes 4194304 | tf_op jit(solution)/shard_map/psum | solution.py:80
  32.5 6.2 %slice-start = ((s8[8388608]{0:T(1024)(128)(4,1)}), s8[4194304]{0:T(1024)(128)(4,1)S(1)}, s32[]{:S(2)}) async-start(s8[8388608]{0:T(1024)(128)(4,1)} %bitcast.370), calls=%async_computation.4 | async-start | bytes 8388608
  32.6 5.6 %copy-start.24 = (bf16[1,2,16,256,128]{4,3,2,1,0:T(8,128)(2,1)S(1)}, bf16[1,2,16,256,128]{4,3,2,1,0:T(8,128)(2,1)}, u32[]{:S(2)}) copy-start(bf16[1,2,16,256,128]{4,3,2,1,0:T(8,128)(2,1)} %param.19) | copy-start | bytes 6291460
  32.6 6.8 %slice-start.1 = ((s8[8388608]{0:T(1024)(128)(4,1)}), s8[4194304]{0:T(1024)(128)(4,1)S(1)}, s32[]{:S(2)}) async-start(s8[8388608]{0:T(1024)(128)(4,1)} %bitcast.370), calls=%async_computation.5 | async-start | bytes 8388608
  39.3 2.0 copy-start.11
  40.5 2.5 copy-start.25
  40.5 6.3 %copy-start.26 = (s32[1,16,1]{1,2,0:T(1,128)S(1)}, s32[1,16,1]{1,2,0:T(1,128)}, u32[]{:S(2)}) copy-start(s32[1,16,1]{1,2,0:T(1,128)} %param.16) | copy-start | bytes 196
  42.0 0.8 copy-start
  42.0 1.0 copy-start.1
  42.0 19.1 %copy-start.10 = (bf16[1,256,512]{2,1,0:T(8,128)(2,1)S(1)}, bf16[1,256,512]{2,1,0:T(8,128)(2,1)}, u32[]{:S(2)}) copy-start(bf16[1,256,512]{2,1,0:T(8,128)(2,1)} %param.12) | copy-start | bytes 786436
  42.0 19.2 %copy-start.22 = (bf16[512]{0:T(512)(128)(2,1)S(1)}, bf16[512]{0:T(512)(128)(2,1)}, u32[]{:S(2)}) copy-start(bf16[512]{0:T(512)(128)(2,1)} %param.23) | copy-start | bytes 3076
  44.4 40.0 %copy-start.18 = (pred[256]{0:T(512)(128)(4,1)}, pred[256]{0:T(512)(128)(4,1)S(1)}, u32[]{:S(2)}) copy-start(pred[256]{0:T(512)(128)(4,1)S(1)} %get-tuple-element.126) | copy-start | bytes 772
  44.4 40.0 %copy-start.12 = (pred[256]{0:T(512)(128)(4,1)}, pred[256]{0:T(512)(128)(4,1)S(1)}, u32[]{:S(2)}) copy-start(pred[256]{0:T(512)(128)(4,1)S(1)} %get-tuple-element.127) | copy-start | bytes 772
  48.5 23.7 %all-to-all-start = ((bf16[16,2,2,16,128]{4,1,3,2,0:T(2,128)(2,1)}), bf16[16,2,2,16,128]{4,1,3,2,0:T(2,128)(2,1)S(1)}, u32[]{:S(2)}, u32[]{:S(2)}) async-start(bf16[16,2,2,16,128]{4,1,3,2,0:T(2,128)(2,1)} %copy.308), calls=%async_computation | async-start | bytes 524288 | tf_op jit(solution)/shard_map/all_to_all | solution.py:154
  155.4 2.5 copy-start.2
  155.4 3.6 %copy-start.8 = (bf16[2,2048,128]{2,1,0:T(8,128)(2,1)S(1)}, bf16[2,2048,128]{2,1,0:T(8,128)(2,1)}, u32[]{:S(2)}) copy-start(bf16[2,2048,128]{2,1,0:T(8,128)(2,1)} %all-gather.5.cloned.1.call-done) | copy-start | bytes 3145732
  156.8 2.6 copy-start.16
  158.0 1.7 copy-start.3
  159.0 1.0 copy-start.17
  159.4 1.0 copy-start.4
  159.7 1.0 copy-start.20
  160.1 1.0 copy-start.5
  160.4 1.0 copy-start.21
  160.7 1.0 copy-start.6
  161.1 1.0 copy-start.7
  161.4 1.1 copy-start.19
  162.1 0.8 copy-start.9
  162.1 0.8 copy-start.13
  162.5 0.8 copy-start.14
  162.9 0.8 copy-start.15
Sparse Core Ops, SparseCore 0:
  21.9 61.2 all-gather.2
  85.8 69.5 all-gather.4
Sparse Core Ops, SparseCore 1:
  43.1 205.5 all-reduce.2
where the time goes:
time: 262 us; the launch traced here: 260 us
  waiting for transfers between devices  160 us (61%)
  matrix products  43.6 us (17%)
  other arithmetic  17.4 us (7%)
  between operations  16.3 us (6%)
  starting transfers between devices  13.8 us (5%)
  local copies, waits for them, and re-layouts  9.69 us (4%)
    psum x1, waiting for transfers between devices, finish_rows(): whole = lax.psum(partials + placed, 'tp')  70.8 us
    all_gather x1, waiting for transfers between devices, body(): block_piece = lax.all_gather(block_full, 'blk', axis=1, tiled=True)  68.7 us
    dot_general x4, matrix products, body(): jnp.dot(attended, out_weight, preferred_element_type=jnp.float32)  15.1 us
    all_to_all x1, starting transfers between devices, body(): lax.all_to_all(packed, ('blk', 'group'), split_axis=0, concat_axis=0, til...  11.4 us
    all_gather x1, waiting for transfers between devices, body(): context_piece = lax.all_gather(context_full, 'blk', axis=1, tiled=True)  10.3 us
    all_to_all x1, waiting for transfers between devices, body(): lax.all_to_all(packed, ('blk', 'group'), split_axis=0, concat_axis=0, til...  9.86 us
    unnamed x66, local copies, waits for them, and re-layouts  7.09 us
    dot_general x8, matrix products, fold_slab(): jnp.einsum('qhd,kd->qhk', queries, context_slab[0], preferred_element_typ...  5.73 us
  transfers between devices with their start and end apart: 6, of which 4 were waited for; matrix products, arithmetic and copies ran while one was open for 24% of the time, Pallas kernels for 0%

commit v1 on v0

v1 whole, which is shorter than its diff:
```python
import functools
import math

import jax
import jax.numpy as jnp
from jax import lax
from jax.experimental import pallas as pl
from jax.experimental.pallas import tpu as pltpu
from jax.sharding import PartitionSpec as P

HEAD_SIZE = 128
PAGE_TOKENS = 16
STEPS = 4
ROWS = 16
LEN = 256
HEADS = 4
TOKENS = 256
PAGES = TOKENS // PAGE_TOKENS
HALF = HEAD_SIZE // 2
PACKED = 4 * TOKENS // 2
CHUNK = 4 * TOKENS
TAIL = 16
COLUMNS = 8192
QUARTER = COLUMNS // 4
SHARE = COLUMNS // 16
LOW_SCORE = -1e30
EPSILON = 1e-05
F32 = jnp.float32
BF16 = jnp.bfloat16
LOG2_SCALE = math.log2(math.e) * HEAD_SIZE**-0.5
VMEM = pltpu.VMEM
SMEM = pltpu.SMEM
PARAMS = pltpu.CompilerParams(vmem_limit_bytes=48 * 1024 * 1024)


def spec(space=VMEM):
    return pl.BlockSpec(memory_space=space)


def shape(dims, dtype):
    return jax.ShapeDtypeStruct(dims, dtype)


def dot_t(a, b):
    return lax.dot_general(a, b, (((1,), (1,)), ((), ())), preferred_element_type=F32)


def dot(a, b):
    return lax.dot_general(a, b, (((1,), (0,)), ((), ())), preferred_element_type=F32)


def pack_kernel(owner_ref, context_ref, block_ref, out_ref):
    half = TOKENS // 2
    for number in range(4):
        source = context_ref if number < 2 else block_ref
        piece = source[0, number % 2]
        out_ref[number * half : (number + 1) * half, :] = jnp.concatenate(
            [piece[:half], piece[half:]], axis=1
        )
    owners = [owner_ref[p] for p in range(PAGES)]
    page = lax.broadcasted_iota(jnp.int32, (TAIL, HEAD_SIZE), 1) // PAGE_TOKENS
    page = page + lax.broadcasted_iota(jnp.int32, (TAIL, HEAD_SIZE), 0) * (HEAD_SIZE // PAGE_TOKENS)
    codes = jnp.full((TAIL, HEAD_SIZE), -1, jnp.int32)
    for p in range(PAGES):
        rank = jnp.int32(0)
        for q in range(p):
            rank = rank + (owners[q] == owners[p]).astype(jnp.int32)
        codes = jnp.where(page == p, owners[p] * 2 + rank, codes)
    out_ref[PACKED:, :] = codes.astype(F32).astype(BF16)


def pack(page_owner, context_cache, new_block_cache):
    return pl.pallas_call(
        pack_kernel,
        out_shape=shape((PACKED + TAIL, HEAD_SIZE), BF16),
        in_specs=[spec(SMEM), spec(), spec()],
        out_specs=spec(),
        name="pack",
    )(page_owner, context_cache, new_block_cache)


def join_kernel(mine_ref, other_ref, out_ref):
    odd = lax.axis_index("tp") % 2
    half = TOKENS // 2

    def write(first_ref, second_ref):
        for number in range(4):
            rows = slice(number * half, (number + 1) * half)
            first, second = first_ref[rows, :], second_ref[rows, :]
            out_ref[number * TOKENS : number * TOKENS + half, :] = jnp.concatenate(
                [first[:, :HALF], second[:, :HALF]], axis=1
            )
            out_ref[number * TOKENS + half : (number + 1) * TOKENS, :] = jnp.concatenate(
                [first[:, HALF:], second[:, HALF:]], axis=1
            )

    @pl.when(odd == 0)
    def _():
        write(mine_ref, other_ref)

    @pl.when(odd == 1)
    def _():
        write(other_ref, mine_ref)

    out_ref[CHUNK:, :] = mine_ref[PACKED:, :]


def join(mine, other):
    return pl.pallas_call(
        join_kernel,
        out_shape=shape((CHUNK + TAIL, HEAD_SIZE), BF16),
        in_specs=[spec(), spec()],
        out_specs=spec(),
        name="join",
    )(mine, other)


def attend_kernel(offsets, first, last, *refs):
    offset_ref, query_ref = refs[:2]
    count = len(offsets)
    chunks = refs[2 : 2 + count]
    refs = refs[2 + count :]
    if not first:
        top_in, sum_in = refs[:2]
        refs = refs[2:]
    if last:
        (out_ref,) = refs
    else:
        top_out, sum_out = refs
    blk = lax.axis_index("blk")
    offset = offset_ref[lax.axis_index("group")]
    lane = lax.broadcasted_iota(jnp.int32, (1, TOKENS), 1)
    ones = jnp.ones((2 * TOKENS, HEAD_SIZE), BF16)
    rows_causal = lax.broadcasted_iota(jnp.int32, (TOKENS, TOKENS), 0)
    keys_causal = lax.broadcasted_iota(jnp.int32, (TOKENS, TOKENS), 1)
    keys, values, bias = [], [], []
    for (flip, turn), chunk in zip(offsets, chunks):
        source = (blk // 4 + flip) % 2 * 4 + (blk % 4 + turn + 4) % 4
        bias.append(jnp.where(source * TOKENS + lane < offset, 0.0, LOW_SCORE))
        bias.append(jnp.where(source * TOKENS + 0 * lane <= blk * TOKENS, 0.0, LOW_SCORE))
        keys += [chunk[:TOKENS, :], chunk[2 * TOKENS : 3 * TOKENS, :]]
        values += [chunk[TOKENS : 2 * TOKENS, :], chunk[3 * TOKENS : 4 * TOKENS, :]]
    for head in range(HEADS):
        query = query_ref[0, :, head * HEAD_SIZE : (head + 1) * HEAD_SIZE]
        rows = slice(head * TOKENS, (head + 1) * TOKENS)
        if first:
            top = jnp.full((TOKENS, 1), LOW_SCORE, F32)
            total = jnp.zeros((TOKENS, 2 * HEAD_SIZE), F32)
        else:
            top = top_in[rows, :1]
            total = sum_in[rows, :]
        for number in range(count):
            scores = []
            for part in (2 * number, 2 * number + 1):
                score = dot_t(query, keys[part]) * LOG2_SCALE + bias[part]
                if offsets[number] == (0, 0) and part % 2 == 1:
                    score = jnp.where(keys_causal <= rows_causal, score, LOW_SCORE)
                scores.append(score)
            score = jnp.concatenate(scores, axis=1)
            top_now = jnp.maximum(top, jnp.max(score, axis=1, keepdims=True))
            weight = jnp.exp2(score - top_now)
            high = weight.astype(BF16)
            low = (weight - high.astype(F32)).astype(BF16)
            value = jnp.concatenate(
                [jnp.concatenate(values[2 * number : 2 * number + 2], axis=0), ones], axis=1
            )
            fresh = dot(high, value) + dot(low, value)
            if first and number == 0:
                total = fresh
            else:
                total = total * jnp.exp2(top - top_now) + fresh
            top = top_now
        if last:
            out_ref[0, :, head * HEAD_SIZE : (head + 1) * HEAD_SIZE] = (
                total[:, :HEAD_SIZE] / total[:, HEAD_SIZE:]
            ).astype(BF16)
        else:
            top_out[rows, :] = jnp.broadcast_to(top, (TOKENS, HEAD_SIZE))
            sum_out[rows, :] = total


def attend(block_offset, queries, chunks, offsets, state, last):
    first = state is None
    operands = [block_offset, queries, *chunks] + ([] if first else list(state))
    rows = HEADS * TOKENS
    if last:
        out = shape((1, TOKENS, HEADS * HEAD_SIZE), BF16)
    else:
        out = (shape((rows, HEAD_SIZE), F32), shape((rows, 2 * HEAD_SIZE), F32))
    pairs = rows * len(chunks) * 2 * TOKENS
    return pl.pallas_call(
        functools.partial(attend_kernel, offsets, first, last),
        out_shape=out,
        in_specs=[spec(SMEM)] + [spec()] * (len(operands) - 1),
        out_specs=spec() if last else (spec(), spec()),
        compiler_params=PARAMS,
        cost_estimate=pl.CostEstimate(
            flops=pairs * HEAD_SIZE * 10, bytes_accessed=2 << 20, transcendentals=pairs
        ),
        name="attend",
    )(*operands)


def pages_kernel(offsets, *refs):
    chunks, (mine_ref, other_ref) = refs[:-2], refs[-2:]
    blk = lax.axis_index("blk")
    instance = blk * 2 + lax.axis_index("group")
    other = blk * 2 + 1 - lax.axis_index("group")
    slots = 4 * PAGE_TOKENS
    row = lax.broadcasted_iota(jnp.int32, (slots, TOKENS), 0)
    token = lax.broadcasted_iota(jnp.int32, (slots, TOKENS), 1)
    wanted = jnp.where(row < 2 * PAGE_TOKENS, instance * 2, other * 2) + row // PAGE_TOKENS % 2
    wanted = jnp.where(row % PAGE_TOKENS == token % PAGE_TOKENS, wanted, -2).astype(F32)
    for (flip, turn), chunk in zip(offsets, chunks):
        source = (blk // 4 + flip) % 2 * 4 + (blk % 4 + turn + 4) % 4
        codes = chunk[CHUNK : CHUNK + TAIL, :].astype(F32)
        codes = jnp.concatenate([codes[0:1], codes[1:2]], axis=1)
        chooser = (wanted == codes).astype(BF16)
        for part in range(2):
            cache = chunk[(2 + part) * TOKENS : (3 + part) * TOKENS, :]
            found = dot(chooser, cache).astype(BF16)
            for rank in range(2):
                mine_ref[source, rank, part] = found[rank * PAGE_TOKENS : (rank + 1) * PAGE_TOKENS]
                other_ref[source, rank, part] = found[
                    (2 + rank) * PAGE_TOKENS : (3 + rank) * PAGE_TOKENS
                ]


def select_pages(chunks, offsets):
    out = shape((8, 2, 2, PAGE_TOKENS, HEAD_SIZE), BF16)
    return pl.pallas_call(
        functools.partial(pages_kernel, offsets),
        out_shape=(out, out),
        in_specs=[spec()] * len(chunks),
        out_specs=(spec(), spec()),
        compiler_params=PARAMS,
        name="pages",
    )(*chunks)


def pool_kernel(mine_ref, came_ref, out_ref):
    group = lax.axis_index("group")
    out_ref[:, group] = mine_ref[...]
    out_ref[:, 1 - group] = came_ref[...]


def pool(mine, came):
    return pl.pallas_call(
        pool_kernel,
        out_shape=shape((8, 2, 2, 2, PAGE_TOKENS, HEAD_SIZE), BF16),
        in_specs=[spec(), spec()],
        out_specs=spec(),
        name="pool",
    )(mine, came)


def attend_rows(length_ref, query_ref, step_ref, cache_ref, attended_ref, score_ref, mixed_ref):
    count = HEADS * STEPS * ROWS
    query = jnp.concatenate(
        [
            query_ref[0, :, :, h * HEAD_SIZE : (h + 1) * HEAD_SIZE].reshape(STEPS * ROWS, HEAD_SIZE)
            for h in range(HEADS)
        ],
        axis=0,
    )
    scaling = HEAD_SIZE**-0.5

    def row_of(width):
        return lax.broadcasted_iota(jnp.int32, (count, width), 0) % ROWS

    row_wide, row_head = row_of(LEN), row_of(HEAD_SIZE)
    lengths = jnp.zeros((count, LEN), jnp.int32)
    for r in range(ROWS):
        score = dot_t(query, cache_ref[0, 0, r])
        if r == 0:
            score_ref[...] = score
        else:
            score_ref[...] = jnp.where(row_wide == r, score, score_ref[...])
        lengths = jnp.where(row_wide == r, length_ref[r], lengths)
    live = lax.broadcasted_iota(jnp.int32, (count, LEN), 1) < lengths
    score_old = jnp.where(live, score_ref[...] * scaling, LOW_SCORE)
    new_keys = step_ref[0, :, 0].reshape(STEPS * ROWS, HEAD_SIZE)
    new_values = step_ref[0, :, 1].reshape(STEPS * ROWS, HEAD_SIZE)
    lane = lax.broadcasted_iota(jnp.int32, (count, STEPS * ROWS), 1)
    place = lax.broadcasted_iota(jnp.int32, (count, STEPS * ROWS), 0)
    open_new = (lane % ROWS == place % ROWS) & (lane // ROWS <= place // ROWS % STEPS)
    score_new = jnp.where(open_new, dot_t(query, new_keys) * scaling, LOW_SCORE)
    top = jnp.maximum(
        jnp.max(score_old, axis=1, keepdims=True), jnp.max(score_new, axis=1, keepdims=True)
    )
    weight_old = jnp.where(live, jnp.exp(score_old - top), 0.0)
    weight_new = jnp.where(open_new, jnp.exp(score_new - top), 0.0)
    totals = jnp.sum(weight_old, axis=1, keepdims=True) + jnp.sum(weight_new, axis=1, keepdims=True)
    rounded = weight_old.astype(BF16)
    for r in range(ROWS):
        mixed = dot(rounded, cache_ref[0, 1, r])
        if r == 0:
            mixed_ref[...] = mixed
        else:
            mixed_ref[...] = jnp.where(row_head == r, mixed, mixed_ref[...])
    mixed = mixed_ref[...] + dot(weight_new.astype(BF16), new_values)
    attended = (mixed / totals).astype(BF16)
    for h in range(HEADS):
        attended_ref[:, h * HEAD_SIZE : (h + 1) * HEAD_SIZE] = attended[
            h * STEPS * ROWS : (h + 1) * STEPS * ROWS
        ]


TILES = 2


def decode_kernel(
    y_ref, length_ref, query_ref, step_ref, cache_ref, weight_ref, *refs
):
    outs, (attended_ref, score_ref, mixed_ref) = refs[:4], refs[4:]
    number = pl.program_id(0)

    @pl.when(number == 0)
    def _():
        attend_rows(length_ref, query_ref, step_ref, cache_ref, attended_ref, score_ref, mixed_ref)

    part = dot(attended_ref[...], weight_ref[...])
    for place, out in enumerate(outs):

        @pl.when(number // TILES == place)
        def _(out=out):
            out[...] = part.astype(out.dtype)


TURNS = (2, 1, 3, 0)


def decode(place, row_lengths, step_query, step_cache, row_cache, out_weight):
    width = QUARTER // TILES
    rows = STEPS * ROWS

    def weight_block(j, y):
        slot = j // TILES
        turn = jnp.where(slot == 0, 2, jnp.where(slot == 1, 1, jnp.where(slot == 2, 3, 0)))
        return (0, (y[0] + turn) % 4 * TILES + j % TILES)

    def whole(a):
        dims = a.shape
        return pl.BlockSpec(dims, lambda j, y: (0,) * len(dims))

    def out_block(slot):
        return pl.BlockSpec(
            (rows, width), lambda j, y: (0, jnp.clip(j - slot * TILES, 0, TILES - 1))
        )

    return pl.pallas_call(
        decode_kernel,
        out_shape=tuple(shape((rows, QUARTER), BF16 if t else F32) for t in TURNS),
        grid_spec=pltpu.PrefetchScalarGridSpec(
            num_scalar_prefetch=2,
            grid=(4 * TILES,),
            in_specs=[
                whole(step_query),
                whole(step_cache),
                whole(row_cache),
                pl.BlockSpec((out_weight.shape[0], width), lambda j, y, l: weight_block(j, y)),
            ]
            if False
            else [
                pl.BlockSpec(step_query.shape, lambda j, y, l: (0,) * 4),
                pl.BlockSpec(step_cache.shape, lambda j, y, l: (0,) * 5),
                pl.BlockSpec(row_cache.shape, lambda j, y, l: (0,) * 5),
                pl.BlockSpec((out_weight.shape[0], width), lambda j, y, l: weight_block(j, y)),
            ],
            out_specs=tuple(
                pl.BlockSpec(
                    (rows, width),
                    lambda j, y, l, s=s: (0, jnp.clip(j - s * TILES, 0, TILES - 1)),
                )
                for s in range(4)
            ),
            scratch_shapes=[
                pltpu.VMEM((rows, HEADS * HEAD_SIZE), BF16),
                pltpu.VMEM((HEADS * rows, LEN), F32),
                pltpu.VMEM((HEADS * rows, HEAD_SIZE), F32),
            ],
        ),
        compiler_params=PARAMS,
        cost_estimate=pl.CostEstimate(
            flops=2 * rows * 512 * COLUMNS, bytes_accessed=12 << 20, transcendentals=1 << 16
        ),
        name="decode",
    )(place, row_lengths, step_query, step_cache, row_cache, out_weight)


def quarter_kernel(own_ref, a_ref, b_ref, c_ref, *outs):
    z = lax.axis_index("tp") % 4
    for out, turn in zip(outs, TURNS):
        columns = pl.ds(pl.multiple_of((z + turn) % 4 * SHARE, SHARE), SHARE)
        out[...] = (
            own_ref[:, columns]
            + a_ref[:, columns].astype(F32)
            + b_ref[:, columns].astype(F32)
            + c_ref[:, columns].astype(F32)
        )


def sum_quarters(own, came):
    return pl.pallas_call(
        quarter_kernel,
        out_shape=tuple(shape((STEPS * ROWS, SHARE), F32) for _ in TURNS),
        in_specs=[spec()] * 4,
        out_specs=(spec(),) * 4,
        name="quarters",
    )(own, *came)


def hidden_kernel(residual_ref, own_ref, a_ref, b_ref, c_ref, hidden_ref, square_ref):
    residual = residual_ref[0].reshape(STEPS * ROWS, SHARE).astype(F32)
    hidden = residual + (own_ref[...] + a_ref[...] + b_ref[...] + c_ref[...])
    hidden_ref[...] = hidden
    square_ref[...] = jnp.broadcast_to(
        jnp.sum(hidden * hidden, axis=1, keepdims=True), square_ref.shape
    )


def sum_shares(residual, own, came):
    return pl.pallas_call(
        hidden_kernel,
        out_shape=(shape((STEPS * ROWS, SHARE), F32), shape((STEPS * ROWS, HEAD_SIZE), F32)),
        in_specs=[spec()] * 5,
        out_specs=(spec(), spec()),
        name="hidden",
    )(residual, own, *came)


def squares_kernel(own_ref, a_ref, b_ref, c_ref, out_ref):
    out_ref[...] = own_ref[...] + a_ref[...] + b_ref[...] + c_ref[...]


def sum_squares(own, came):
    return pl.pallas_call(
        squares_kernel,
        out_shape=shape((STEPS * ROWS, HEAD_SIZE), F32),
        in_specs=[spec()] * 4,
        out_specs=spec(),
        name="squares",
    )(own, *came)


def finish_kernel(hidden_ref, gain_ref, own_ref, a_ref, b_ref, c_ref, out_ref):
    square = own_ref[...] + a_ref[...] + b_ref[...] + c_ref[...]
    scale = lax.rsqrt(square * (1.0 / COLUMNS) + EPSILON)
    scale = jnp.concatenate([scale] * (SHARE // HEAD_SIZE), axis=1)
    out = hidden_ref[...] * scale * gain_ref[...].astype(F32)
    out_ref[0] = out.astype(BF16).reshape(STEPS, ROWS, SHARE)


def finish(hidden, gain, own, came):
    return pl.pallas_call(
        finish_kernel,
        out_shape=shape((1, STEPS, ROWS, SHARE), BF16),
        in_specs=[spec()] * 6,
        out_specs=spec(),
        name="finish",
    )(hidden, gain, own, *came)


def move_x(a, turn):
    return lax.ppermute(a, "blk", [(i, i // 4 * 4 + (i + turn) % 4) for i in range(8)])


def move_y(a, turn):
    return lax.ppermute(a, "tp", [(i, (i + 4 * turn) % 16) for i in range(16)])


def move_z(a, turn):
    return lax.ppermute(a, "tp", [(i, i // 4 * 4 + (i + turn) % 4) for i in range(16)])


def body(
    prompt_query,
    context_cache,
    new_block_cache,
    block_offset,
    page_owner,
    step_query,
    step_cache,
    row_cache,
    row_lengths,
    out_weight,
    residual,
    norm_gain,
):
    packed = pack(page_owner.reshape(PAGES), context_cache, new_block_cache)
    near = lax.ppermute(packed, "tp", [(i, i ^ 1) for i in range(16)])
    far = lax.ppermute(packed, "blk", [(i, i ^ 4) for i in range(8)])
    far_near = lax.ppermute(
        packed,
        ("blk", "tp"),
        [(b * 16 + t, (b ^ 4) * 16 + (t ^ 1)) for b in range(8) for t in range(16)],
    )
    place = (lax.axis_index("tp") // 4).astype(jnp.int32).reshape(1)
    parts = decode(
        place, row_lengths.reshape(ROWS), step_query, step_cache, row_cache, out_weight
    )
    came = [move_y(a, turn) for a, turn in zip(parts[:3], TURNS)]

    chunk = join(packed, near)
    chunk_far = join(far, far_near)
    up = move_x(chunk, 1)
    down = move_x(chunk, 3)
    far_up = move_x(chunk_far, 1)
    far_down = move_x(chunk_far, 3)
    up_two = move_x(up, 1)
    far_down_two = move_x(far_down, 3)

    state = attend(block_offset, prompt_query, [chunk, chunk_far], [(0, 0), (1, 0)], None, False)

    shares = sum_quarters(parts[3], came)
    came = [move_z(a, turn) for a, turn in zip(shares[:3], TURNS)]

    state = attend(
        block_offset,
        prompt_query,
        [up, down, far_up, far_down],
        [(0, -1), (0, 1), (1, -1), (1, 1)],
        state,
        False,
    )

    hidden, square = sum_shares(residual, shares[3], came)
    came = [move_y(square, turn) for turn in TURNS[:3]]
    square = sum_squares(square, came)
    came = [move_z(square, turn) for turn in TURNS[:3]]

    chunks = [chunk, chunk_far, up, down, far_up, far_down, up_two, far_down_two]
    offsets = [(0, 0), (1, 0), (0, -1), (0, 1), (1, -1), (1, 1), (0, 2), (1, 2)]
    mine, other = select_pages(chunks, offsets)
    other = lax.ppermute(other, "group", [(0, 1), (1, 0)])
    prefill_out = attend(
        block_offset, prompt_query, [up_two, far_down_two], [(0, 2), (1, 2)], state, True
    )
    page_pool = pool(mine, other).reshape(1, 32, 2, PAGE_TOKENS, HEAD_SIZE)
    decode_out = finish(hidden, norm_gain.reshape(1, SHARE), square, came)
    return (prefill_out, page_pool, decode_out)


def solution(mesh):
    placed = (
        P("group", "blk", "tp"),
        P("group", None, "blk", "tp"),
        P("group", None, "blk", "tp"),
        P(),
        P("group", "blk", None),
        P(("blk", "group"), None, None, "tp"),
        P(("blk", "group"), None, None, None, "tp"),
        P(("blk", "group"), None, None, None, "tp"),
        P(("blk", "group"), None),
        P("tp", None),
        P(("blk", "group"), None, None, "tp"),
        P("tp"),
    )
    return jax.shard_map(
        body,
        mesh=mesh,
        in_specs=placed,
        out_specs=(
            P("group", "blk", "tp"),
            P(("blk", "group"), None, None, None, "tp"),
            P(("blk", "group"), None, None, "tp"),
        ),
        check_vma=False,
    )
```

time: 262 us -> 116 us (0.44)
  the two profiles are of different devices: /device:TPU:6 before, /device:TPU:1 now
where the time goes in v1:
time: 116 us
  starting transfers between devices  39.8 us (34%)
  Pallas kernels  38.2 us (33%)
  local copies, waits for them, and re-layouts  22.8 us (20%)
  waiting for transfers between devices  14 us (12%)
    unnamed x72, local copies, waits for them, and re-layouts  22.3 us
    pallas_call x3, Pallas kernels, attend(): pl.pallas_call(functools.partial(attend_kernel, offsets, first, last), ou...  14.5 us
    ppermute x6, starting transfers between devices, move_y(): return lax.ppermute(a, 'tp', [(i, (i + 4 * turn) % 16) for i in range(16)])  9.88 us
    pallas_call x1, Pallas kernels, decode(): pl.pallas_call(decode_kernel, out_shape=tuple((shape((rows, QUARTER), BF1...  9.31 us
    ppermute x6, starting transfers between devices, move_x(): lax.ppermute(a, 'blk', [(i, i // 4 * 4 + (i + turn) % 4) for i in range(8)])  8.56 us
    ppermute x6, starting transfers between devices, move_z(): lax.ppermute(a, 'tp', [(i, i // 4 * 4 + (i + turn) % 4) for i in range(16)])  8.52 us
    ppermute x6, waiting for transfers between devices, move_z(): lax.ppermute(a, 'tp', [(i, i // 4 * 4 + (i + turn) % 4) for i in range(16)])  7.24 us
    ppermute x6, waiting for transfers between devices, move_y(): return lax.ppermute(a, 'tp', [(i, (i + 4 * turn) % 16) for i in range(16)])  6.69 us
  transfers between devices with their start and end apart: 22, of which 4 were waited for; matrix products, arithmetic and copies ran while one was open for 0% of the time, Pallas kernels for 30%

profile of v1, /device:TPU:1, one launch (start us, length us, event | category | flops | bytes accessed | tf_op | source)
XLA Modules:
  0.0 115.6 jit_solution(7839407023428801180)
XLA Ops:
  0.7 1.6 %copy.15.context_ref = bf16[1,2,256,64]{3,2,1,0:T(8,128)(2,1)} copy(bf16[1,2,256,64]{2,3,1,0:T(8,128)(2,1)} %param.13) | data formatting | bytes 131072 | tf_op args[1]
  2.3 1.6 %copy.16.block_ref = bf16[1,2,256,64]{3,2,1,0:T(8,128)(2,1)} copy(bf16[1,2,256,64]{2,3,1,0:T(8,128)(2,1)} %param.14) | data formatting | bytes 131072 | tf_op args[2]
  3.9 1.8 %pack.1.mine_ref = bf16[528,128]{1,0:T(8,128)(2,1)} custom-call(s32[16]{0:T(128)} %bitcast.6, bf16[1,2,256,64]{3,2,1,0:T(8,128)(2,1)} %copy.15.context_ref, bf16[1,2,256,64]{3,2,1,0:T(8,128)(2,1)} %copy.16.block_ref), custom_call_target="tpu_custom_call" | custom-call | tf_op jit(solution)/shard_map/pack/pallas_call | solution.py:73
  5.7 2.5 %collective-permute-start = (bf16[528,128]{1,0:T(8,128)(2,1)}, bf16[528,128]{1,0:T(8,128)(2,1)S(1)}, u32[]{:S(2)}, u32[]{:S(2)}) collective-permute-start(bf16[528,128]{1,0:T(8,128)(2,1)} %pack.1.mine_ref), channel_id=1, source_target_pairs={{0,1},{1,0},{2,3},{3,2},{4,5},{5,4},{6,7},{7,6},{8,9},{9,8},{10,11... | collective-permute-start | bytes 405512 | tf_op jit(solution)/shard_map/ppermute | solution.py:491
  8.1 5.6 %collective-permute-start.4 = (bf16[528,128]{1,0:T(8,128)(2,1)}, bf16[528,128]{1,0:T(8,128)(2,1)S(1)}, u32[]{:S(2)}, u32[]{:S(2)}) collective-permute-start(bf16[528,128]{1,0:T(8,128)(2,1)} %pack.1.mine_ref), channel_id=1, source_target_pairs={{0,129},{1,128},{2,131},{3,130},{4,133},{5,132},{6,135},{7,134},{8... | collective-permute-start | bytes 405512 | tf_op jit(solution)/shard_map/ppermute | solution.py:493
  13.7 0.5 collective-permute-start.3
  14.2 1.6 %copy-done = bf16[1,2,16,256,128]{4,3,2,1,0:T(8,128)(2,1)S(1)} copy-done((bf16[1,2,16,256,128]{4,3,2,1,0:T(8,128)(2,1)S(1)}, bf16[1,2,16,256,128]{4,3,2,1,0:T(8,128)(2,1)}, u32[]{:S(2)}) %copy-start) | copy-done | bytes 2097176
  15.8 0.8 copy-done.7
  16.6 0.8 copy-done.8
  17.4 0.7 copy-done.9
  18.0 9.3 %decode.1 = (bf16[64,2048]{1,0:T(8,128)(2,1)S(1)}, bf16[64,2048]{1,0:T(8,128)(2,1)S(1)}, bf16[64,2048]{1,0:T(8,128)(2,1)S(1)}, f32[64,2048]{1,0:T(8,128)S(1)}) custom-call(s32[1]{0:T(128)} %bitcast.2.y_ref, s32[16]{0:T(128)S(1)} %bitcast.4, bf16[1,4,16,512]{3,2,1,0:T(8,128)(2,1)S(1)} %copy-done.7, bf16[1,4,2,16,128]{4,3,2,1,0:T(8,128)(2,1)S(1)} %copy-done.8, ...), custom_call_target="tpu_custom_call" | custom-call | flops 536870912 | bytes 12582912 | tf_op jit(solution)/shard_map/decode/pallas_call | solution.py:351
  27.3 0.8 copy-done.5
  28.1 2.9 %collective-permute-start.10 = (bf16[64,2048]{1,0:T(8,128)(2,1)S(1)}, bf16[64,2048]{1,0:T(8,128)(2,1)S(1)}, u32[]{:S(2)}, u32[]{:S(2)}) collective-permute-start(bf16[64,2048]{1,0:T(8,128)(2,1)S(1)} %get-tuple-element.26), channel_id=1, source_target_pairs={{0,8},{1,9},{2,10},{3,11},{4,12},{5,13},{6,14},{7,15},{8,0},{9,1},... | collective-permute-start | bytes 786440 | tf_op jit(solution)/shard_map/ppermute | solution.py:469
  31.1 0.4 collective-permute-start.11
  31.5 2.3 %collective-permute-start.12 = (bf16[64,2048]{1,0:T(8,128)(2,1)S(1)}, bf16[64,2048]{1,0:T(8,128)(2,1)S(1)}, u32[]{:S(2)}, u32[]{:S(2)}) collective-permute-start(bf16[64,2048]{1,0:T(8,128)(2,1)S(1)} %get-tuple-element.28), channel_id=1, source_target_pairs={{0,12},{1,13},{2,14},{3,15},{4,0},{5,1},{6,2},{7,3},{8,4},{9,5},{1... | collective-permute-start | bytes 786440 | tf_op jit(solution)/shard_map/ppermute | solution.py:469
  33.7 1.8 %join.2.refs_2_.refs_0_ = bf16[1040,128]{1,0:T(8,128)(2,1)} custom-call(bf16[528,128]{1,0:T(8,128)(2,1)} %pack.1.mine_ref, bf16[528,128]{1,0:T(8,128)(2,1)} %copy-done.23), custom_call_target="tpu_custom_call" | custom-call | tf_op jit(solution)/shard_map/join/pallas_call | solution.py:109
  35.6 1.2 %collective-permute-start.1 = (bf16[1040,128]{1,0:T(8,128)(2,1)}, bf16[1040,128]{1,0:T(8,128)(2,1)S(1)}, u32[]{:S(2)}, u32[]{:S(2)}) collective-permute-start(bf16[1040,128]{1,0:T(8,128)(2,1)} %join.2.refs_2_.refs_0_), channel_id=1, source_target_pairs={{0,32},{32,64},{64,96},{96,0},{128,160},{160,192},{192,224},{224,1... | collective-permute-start | bytes 798728 | tf_op jit(solution)/shard_map/ppermute | solution.py:465
  36.8 0.7 copy-done.22
  37.4 1.8 %join.3.refs_3_.refs_1_ = bf16[1040,128]{1,0:T(8,128)(2,1)} custom-call(bf16[528,128]{1,0:T(8,128)(2,1)} %copy-done.22, bf16[528,128]{1,0:T(8,128)(2,1)} %copy-done.21), custom_call_target="tpu_custom_call" | custom-call | tf_op jit(solution)/shard_map/join/pallas_call | solution.py:109
  39.3 1.9 %collective-permute-start.5 = (bf16[1040,128]{1,0:T(8,128)(2,1)}, bf16[1040,128]{1,0:T(8,128)(2,1)S(1)}, u32[]{:S(2)}, u32[]{:S(2)}) collective-permute-start(bf16[1040,128]{1,0:T(8,128)(2,1)} %join.3.refs_3_.refs_1_), channel_id=1, source_target_pairs={{0,96},{32,0},{64,32},{96,64},{128,224},{160,128},{192,160},{224,1... | collective-permute-start | bytes 798728 | tf_op jit(solution)/shard_map/ppermute | solution.py:465
  41.2 2.0 %collective-permute-done.11.b_ref = bf16[64,2048]{1,0:T(8,128)(2,1)S(1)} collective-permute-done((bf16[64,2048]{1,0:T(8,128)(2,1)S(1)}, bf16[64,2048]{1,0:T(8,128)(2,1)S(1)}, u32[]{:S(2)}, u32[]{:S(2)}) %collective-permute-start.11) | collective-permute-done | bytes 262176 | tf_op jit(solution)/shard_map/ppermute | solution.py:469
  43.1 0.7 copy-done.19
  43.8 0.1 copy-done.20
  43.9 2.1 %quarters.1 = (f32[64,512]{1,0:T(8,128)}, f32[64,512]{1,0:T(8,128)}, f32[64,512]{1,0:T(8,128)}, f32[64,512]{1,0:T(8,128)}) custom-call(f32[64,2048]{1,0:T(8,128)} %copy-done.5, bf16[64,2048]{1,0:T(8,128)(2,1)} %copy-done.18, bf16[64,2048]{1,0:T(8,128)(2,1)} %copy-done.19, bf16[64,2048]{1,0:T(8,128)(2,1)} %copy-done.20), custom_call_target="tpu_custom_call" | custom-call | tf_op jit(solution)/shard_map/quarters/pallas_call | solution.py:404
  46.1 1.1 collective-permute-start.13
  47.2 1.2 %collective-permute-start.14 = (f32[64,512]{1,0:T(8,128)}, f32[64,512]{1,0:T(8,128)S(1)}, u32[]{:S(2)}, u32[]{:S(2)}) collective-permute-start(f32[64,512]{1,0:T(8,128)} %get-tuple-element.31), channel_id=1, source_target_pairs={{0,1},{1,2},{2,3},{3,0},{4,5},{5,6},{6,7},{7,4},{8,9},{9,10},{10,1... | collective-permute-start | bytes 393224 | tf_op jit(solution)/shard_map/ppermute | solution.py:473
  48.4 2.0 %collective-permute-start.15 = (f32[64,512]{1,0:T(8,128)}, f32[64,512]{1,0:T(8,128)S(1)}, u32[]{:S(2)}, u32[]{:S(2)}) collective-permute-start(f32[64,512]{1,0:T(8,128)} %get-tuple-element.32), channel_id=1, source_target_pairs={{0,3},{1,0},{2,1},{3,2},{4,7},{5,4},{6,5},{7,6},{8,11},{9,8},{10,9... | collective-permute-start | bytes 393224 | tf_op jit(solution)/shard_map/ppermute | solution.py:473
  50.4 7.2 %collective-permute-done.13.a_ref = f32[64,512]{1,0:T(8,128)S(1)} collective-permute-done((f32[64,512]{1,0:T(8,128)}, f32[64,512]{1,0:T(8,128)S(1)}, u32[]{:S(2)}, u32[]{:S(2)}) %collective-permute-start.13) | collective-permute-done | bytes 131104 | tf_op jit(solution)/shard_map/ppermute | solution.py:473
  57.7 2.5 %collective-permute-start.7 = (bf16[1040,128]{1,0:T(8,128)(2,1)}, bf16[1040,128]{1,0:T(8,128)(2,1)S(1)}, u32[]{:S(2)}, u32[]{:S(2)}) collective-permute-start(bf16[1040,128]{1,0:T(8,128)(2,1)} %join.2.refs_2_.refs_0_), channel_id=1, source_target_pairs={{0,96},{32,0},{64,32},{96,64},{128,224},{160,128},{192,160},{224,1... | collective-permute-start | bytes 798728 | tf_op jit(solution)/shard_map/ppermute | solution.py:465
  60.2 0.3 collective-permute-start.2
  60.5 2.7 %collective-permute-start.6 = (bf16[1040,128]{1,0:T(8,128)(2,1)S(1)}, bf16[1040,128]{1,0:T(8,128)(2,1)S(1)}, u32[]{:S(2)}, u32[]{:S(2)}) collective-permute-start(bf16[1040,128]{1,0:T(8,128)(2,1)S(1)} %collective-permute-done.5.refs_5_), channel_id=1, source_target_pairs={{0,96},{32,0},{64,32},{96,64},{128,224},{160,128},{192,160},{224,1... | collective-permute-start | bytes 798728 | tf_op jit(solution)/shard_map/ppermute | solution.py:465
  63.2 0.7 copy-done.26
  63.8 1.9 %hidden.1 = (f32[64,512]{1,0:T(8,128)}, f32[64,128]{1,0:T(8,128)}) custom-call(bf16[1,4,16,512]{3,2,1,0:T(8,128)(2,1)} %residual_ref.1, f32[64,512]{1,0:T(8,128)} %get-tuple-element.29.own_ref, f32[64,512]{1,0:T(8,128)} %copy-done.24, f32[64,512]{1,0:T(8,128)} %copy-done.25, f32[64,512]{1,0:T(8,128)} %copy-done.26), custom_call_target="tpu_custom_call" | custom-call | tf_op jit(solution)/shard_map/hidden/pallas_call | solution.py:423
  65.7 2.6 %collective-permute-start.18 = (f32[64,128]{1,0:T(8,128)}, f32[64,128]{1,0:T(8,128)S(1)}, u32[]{:S(2)}, u32[]{:S(2)}) collective-permute-start(f32[64,128]{1,0:T(8,128)} %get-tuple-element.34.own_ref), channel_id=1, source_target_pairs={{0,12},{1,13},{2,14},{3,15},{4,0},{5,1},{6,2},{7,3},{8,4},{9,5},{1... | collective-permute-start | bytes 98312 | tf_op jit(solution)/shard_map/ppermute | solution.py:469
  68.3 1.3 %collective-permute-done.18.c_ref = f32[64,128]{1,0:T(8,128)S(1)} collective-permute-done((f32[64,128]{1,0:T(8,128)}, f32[64,128]{1,0:T(8,128)S(1)}, u32[]{:S(2)}, u32[]{:S(2)}) %collective-permute-start.18) | collective-permute-done | bytes 32800 | tf_op jit(solution)/shard_map/ppermute | solution.py:469
  69.6 1.0 collective-permute-start.17
  70.6 0.6 reshape.25.gain_ref
  71.2 3.4 %collective-permute-done.17.b_ref = f32[64,128]{1,0:T(8,128)S(1)} collective-permute-done((f32[64,128]{1,0:T(8,128)}, f32[64,128]{1,0:T(8,128)S(1)}, u32[]{:S(2)}, u32[]{:S(2)}) %collective-permute-start.17) | collective-permute-done | bytes 32800 | tf_op jit(solution)/shard_map/ppermute | solution.py:469
  74.6 0.7 collective-permute-start.16
  75.3 1.0 copy-done.1
  76.2 0.9 copy-done.3
  77.2 3.2 %attend.3 = (f32[1024,128]{1,0:T(8,128)S(1)}, f32[1024,256]{1,0:T(8,128)S(1)}) custom-call(s32[2]{0:T(128)S(1)} %copy-done.11, bf16[1,256,512]{2,1,0:T(8,128)(2,1)S(1)} %copy-done.10, bf16[1040,128]{1,0:T(8,128)(2,1)S(1)} %copy-done.1, bf16[1040,128]{1,0:T(8,128)(2,1)S(1)} %copy-done.3), custom_call_target="tpu_custom_call" | custom-call | flops 1342177280 | bytes 2097152 | tf_op jit(solution)/shard_map/attend/pallas_call | solution.py:191
  80.4 1.0 copy-done.14
  81.5 0.8 copy-done.16
  82.3 0.6 copy-done.33
  82.9 1.4 %squares.1.own_ref = f32[64,128]{1,0:T(8,128)} custom-call(f32[64,128]{1,0:T(8,128)} %get-tuple-element.34.own_ref, f32[64,128]{1,0:T(8,128)} %copy-done.33, f32[64,128]{1,0:T(8,128)} %copy-done.32, f32[64,128]{1,0:T(8,128)} %copy-done.31), custom_call_target="tpu_custom_call" | custom-call | tf_op jit(solution)/shard_map/squares/pallas_call | solution.py:437
  84.3 0.8 collective-permute-start.21
  85.1 0.7 collective-permute-start.20
  85.8 2.7 %collective-permute-start.19 = (f32[64,128]{1,0:T(8,128)}, f32[64,128]{1,0:T(8,128)S(1)}, u32[]{:S(2)}, u32[]{:S(2)}) collective-permute-start(f32[64,128]{1,0:T(8,128)} %squares.1.own_ref), channel_id=1, source_target_pairs={{0,2},{1,3},{2,0},{3,1},{4,6},{5,7},{6,4},{7,5},{8,10},{9,11},{10,... | collective-permute-start | bytes 98312 | tf_op jit(solution)/shard_map/ppermute | solution.py:473
  88.5 0.9 copy-done.2
  89.4 0.9 copy-done.4
  90.4 0.3 pages.1
  90.7 0.6 copy-done.6
  91.3 4.3 %collective-permute-start.9 = (bf16[8,2,2,16,128]{4,3,2,1,0:T(8,128)(2,1)S(1)}, bf16[8,2,2,16,128]{4,3,2,1,0:T(8,128)(2,1)S(1)}, u32[]{:S(2)}, u32[]{:S(2)}) collective-permute-start(bf16[8,2,2,16,128]{4,3,2,1,0:T(8,128)(2,1)S(1)} %get-tuple-element.24), channel_id=1, source_target_pairs={{0,16},{16,0},{1,17},{17,1},{2,18},{18,2},{3,19},{19,3},{4,20},{20... | collective-permute-start | bytes 393224 | tf_op jit(solution)/shard_map/ppermute | solution.py:535
  95.6 1.2 %copy-done.15 = f32[1024,256]{1,0:T(8,128)S(1)} copy-done((f32[1024,256]{1,0:T(8,128)S(1)}, f32[1024,256]{1,0:T(8,128)}, u32[]{:S(2)}) %copy-start.15) | copy-done | bytes 1048600
  96.9 1.0 copy-done.17
  97.9 6.8 %attend.4 = (f32[1024,128]{1,0:T(8,128)S(1)}, f32[1024,256]{1,0:T(8,128)S(1)}) custom-call(s32[2]{0:T(128)S(1)} %copy-done.11, bf16[1,256,512]{2,1,0:T(8,128)(2,1)S(1)} %copy-done.10, bf16[1040,128]{1,0:T(8,128)(2,1)S(1)} %collective-permute-done.1.refs_2_, bf16[1040,128]{1,0:T(8,128)(2,1)S(1)} %collective-permute-done.7.refs_3_, ...), custom_call_target="tpu_custom_call" | custom-call | flops 2684354560 | bytes 2097152 | tf_op jit(solution)/shard_map/attend/pallas_call | solution.py:191
  104.7 0.8 copy-done.12
  105.5 0.6 copy-done.28
  106.1 1.6 %finish.1 = bf16[1,4,16,512]{3,2,1,0:T(8,128)(2,1)} custom-call(f32[64,512]{1,0:T(8,128)} %get-tuple-element.33.hidden_ref, bf16[1,512]{1,0:T(2,128)(2,1)} %reshape.25.gain_ref, f32[64,128]{1,0:T(8,128)} %squares.1.own_ref, f32[64,128]{1,0:T(8,128)} %copy-done.30, f32[64,128]{1,0:T(8,128)} %copy-done.29, f32[64,128]{1,0:T(8,128)} %copy-done.28), custom_call_target="tpu_custom_call" | custom-call | tf_op jit(solution)/shard_map/finish/pallas_call | solution.py:455
  107.7 1.0 copy-done.13
  108.8 4.5 %attend.5 = bf16[1,256,512]{2,1,0:T(8,128)(2,1)} custom-call(s32[2]{0:T(128)S(1)} %copy-done.11, bf16[1,256,512]{2,1,0:T(8,128)(2,1)S(1)} %copy-done.10, bf16[1040,128]{1,0:T(8,128)(2,1)S(1)} %collective-permute-done.2.refs_2_.refs_6_, bf16[1040,128]{1,0:T(8,128)(2,1)S(1)} %collective-permute-done.6.refs_3_.refs_7_, f32[1024,128]{1,0:T(8,128)S(1)} %copy-done.13, ...), custom_call_target="tpu_custom_call" | custom-call | flops 1342177280 | bytes 2097152 | tf_op jit(solution)/shard_map/attend/pallas_call | solution.py:191
  113.2 0.6 copy-done.27
  113.9 1.7 %pool.1 = bf16[8,2,2,2,16,128]{5,4,3,2,1,0:T(8,128)(2,1)} custom-call(bf16[8,2,2,16,128]{4,3,2,1,0:T(8,128)(2,1)} %copy-done.6, bf16[8,2,2,16,128]{4,3,2,1,0:T(8,128)(2,1)} %copy-done.27), custom_call_target="tpu_custom_call" | custom-call | tf_op jit(solution)/shard_map/pool/pallas_call | solution.py:248
  (66 shorter events, 0.2 us)
Async XLA Ops:
  0.6 70.0 %copy-start.34 = (bf16[512]{0:T(512)(128)(2,1)S(1)}, bf16[512]{0:T(512)(128)(2,1)}, u32[]{:S(2)}) copy-start(bf16[512]{0:T(512)(128)(2,1)} %param.23) | copy-start | bytes 3076
  0.6 74.6 %copy-start.11 = (s32[2]{0:T(128)S(1)}, s32[2]{0:T(128)}, u32[]{:S(2)}) copy-start(s32[2]{0:T(128)} %refs_0_.5) | copy-start | bytes 28
  0.7 74.6 %copy-start.10 = (bf16[1,256,512]{2,1,0:T(8,128)(2,1)S(1)}, bf16[1,256,512]{2,1,0:T(8,128)(2,1)}, u32[]{:S(2)}) copy-start(bf16[1,256,512]{2,1,0:T(8,128)(2,1)} %refs_1_.5) | copy-start | bytes 786436
  5.7 25.8 %collective-permute-start = (bf16[528,128]{1,0:T(8,128)(2,1)}, bf16[528,128]{1,0:T(8,128)(2,1)S(1)}, u32[]{:S(2)}, u32[]{:S(2)}) collective-permute-start(bf16[528,128]{1,0:T(8,128)(2,1)} %pack.1.mine_ref), channel_id=1, source_target_pairs={{0,1},{1,0},{2,3},{3,2},{4,5},{5,4},{6,7},{7,6},{8,9},{9,8},{10,11... | collective-permute-start | bytes 405512 | tf_op jit(solution)/shard_map/ppermute | solution.py:491
  8.1 27.4 %collective-permute-start.4 = (bf16[528,128]{1,0:T(8,128)(2,1)}, bf16[528,128]{1,0:T(8,128)(2,1)S(1)}, u32[]{:S(2)}, u32[]{:S(2)}) collective-permute-start(bf16[528,128]{1,0:T(8,128)(2,1)} %pack.1.mine_ref), channel_id=1, source_target_pairs={{0,129},{1,128},{2,131},{3,130},{4,133},{5,132},{6,135},{7,134},{8... | collective-permute-start | bytes 405512 | tf_op jit(solution)/shard_map/ppermute | solution.py:493
  13.7 23.1 %collective-permute-start.3 = (bf16[528,128]{1,0:T(8,128)(2,1)}, bf16[528,128]{1,0:T(8,128)(2,1)S(1)}, u32[]{:S(2)}, u32[]{:S(2)}) collective-permute-start(bf16[528,128]{1,0:T(8,128)(2,1)} %pack.1.mine_ref), channel_id=1, source_target_pairs={{0,128},{32,160},{64,192},{96,224},{128,0},{160,32},{192,64},{224,... | collective-permute-start | bytes 405512 | tf_op jit(solution)/shard_map/ppermute | solution.py:492
  14.2 1.6 %copy-start = (bf16[1,2,16,256,128]{4,3,2,1,0:T(8,128)(2,1)S(1)}, bf16[1,2,16,256,128]{4,3,2,1,0:T(8,128)(2,1)}, u32[]{:S(2)}) copy-start(bf16[1,2,16,256,128]{4,3,2,1,0:T(8,128)(2,1)} %cache_ref.1) | copy-start | bytes 6291460
  15.8 0.8 copy-start.7
  16.6 0.8 copy-start.8
  17.4 0.7 copy-start.9
  27.3 0.8 copy-start.5
  28.1 13.0 %collective-permute-start.10 = (bf16[64,2048]{1,0:T(8,128)(2,1)S(1)}, bf16[64,2048]{1,0:T(8,128)(2,1)S(1)}, u32[]{:S(2)}, u32[]{:S(2)}) collective-permute-start(bf16[64,2048]{1,0:T(8,128)(2,1)S(1)} %get-tuple-element.26), channel_id=1, source_target_pairs={{0,8},{1,9},{2,10},{3,11},{4,12},{5,13},{6,14},{7,15},{8,0},{9,1},... | collective-permute-start | bytes 786440 | tf_op jit(solution)/shard_map/ppermute | solution.py:469
  31.1 12.1 %collective-permute-start.11 = (bf16[64,2048]{1,0:T(8,128)(2,1)S(1)}, bf16[64,2048]{1,0:T(8,128)(2,1)S(1)}, u32[]{:S(2)}, u32[]{:S(2)}) collective-permute-start(bf16[64,2048]{1,0:T(8,128)(2,1)S(1)} %get-tuple-element.27), channel_id=1, source_target_pairs={{0,4},{1,5},{2,6},{3,7},{4,8},{5,9},{6,10},{7,11},{8,12},{9,13},{1... | collective-permute-start | bytes 786440 | tf_op jit(solution)/shard_map/ppermute | solution.py:469
  31.5 2.3 %copy-start.23 = (bf16[528,128]{1,0:T(8,128)(2,1)}, bf16[528,128]{1,0:T(8,128)(2,1)S(1)}, u32[]{:S(2)}) copy-start(bf16[528,128]{1,0:T(8,128)(2,1)S(1)} %collective-permute-done.other_ref) | copy-start | bytes 405508
  31.5 11.7 %collective-permute-start.12 = (bf16[64,2048]{1,0:T(8,128)(2,1)S(1)}, bf16[64,2048]{1,0:T(8,128)(2,1)S(1)}, u32[]{:S(2)}, u32[]{:S(2)}) collective-permute-start(bf16[64,2048]{1,0:T(8,128)(2,1)S(1)} %get-tuple-element.28), channel_id=1, source_target_pairs={{0,12},{1,13},{2,14},{3,15},{4,0},{5,1},{6,2},{7,3},{8,4},{9,5},{1... | collective-permute-start | bytes 786440 | tf_op jit(solution)/shard_map/ppermute | solution.py:469
  35.6 1.2 %copy-start.21 = (bf16[528,128]{1,0:T(8,128)(2,1)}, bf16[528,128]{1,0:T(8,128)(2,1)S(1)}, u32[]{:S(2)}) copy-start(bf16[528,128]{1,0:T(8,128)(2,1)S(1)} %collective-permute-done.4.other_ref) | copy-start | bytes 405508
  35.6 24.6 %collective-permute-start.1 = (bf16[1040,128]{1,0:T(8,128)(2,1)}, bf16[1040,128]{1,0:T(8,128)(2,1)S(1)}, u32[]{:S(2)}, u32[]{:S(2)}) collective-permute-start(bf16[1040,128]{1,0:T(8,128)(2,1)} %join.2.refs_2_.refs_0_), channel_id=1, source_target_pairs={{0,32},{32,64},{64,96},{96,0},{128,160},{160,192},{192,224},{224,1... | collective-permute-start | bytes 798728 | tf_op jit(solution)/shard_map/ppermute | solution.py:465
  36.8 0.7 copy-start.22
  39.3 21.2 %collective-permute-start.5 = (bf16[1040,128]{1,0:T(8,128)(2,1)}, bf16[1040,128]{1,0:T(8,128)(2,1)S(1)}, u32[]{:S(2)}, u32[]{:S(2)}) collective-permute-start(bf16[1040,128]{1,0:T(8,128)(2,1)} %join.3.refs_3_.refs_1_), channel_id=1, source_target_pairs={{0,96},{32,0},{64,32},{96,64},{128,224},{160,128},{192,160},{224,1... | collective-permute-start | bytes 798728 | tf_op jit(solution)/shard_map/ppermute | solution.py:465
  41.2 2.0 %copy-start.18 = (bf16[64,2048]{1,0:T(8,128)(2,1)}, bf16[64,2048]{1,0:T(8,128)(2,1)S(1)}, u32[]{:S(2)}) copy-start(bf16[64,2048]{1,0:T(8,128)(2,1)S(1)} %collective-permute-done.10.a_ref) | copy-start | bytes 786436
  43.1 0.7 copy-start.19
  43.1 0.8 copy-start.20
  46.1 11.6 %collective-permute-start.13 = (f32[64,512]{1,0:T(8,128)}, f32[64,512]{1,0:T(8,128)S(1)}, u32[]{:S(2)}, u32[]{:S(2)}) collective-permute-start(f32[64,512]{1,0:T(8,128)} %get-tuple-element.30), channel_id=1, source_target_pairs={{0,2},{1,3},{2,0},{3,1},{4,6},{5,7},{6,4},{7,5},{8,10},{9,11},{10,... | collective-permute-start | bytes 393224 | tf_op jit(solution)/shard_map/ppermute | solution.py:473
  47.2 13.0 %collective-permute-start.14 = (f32[64,512]{1,0:T(8,128)}, f32[64,512]{1,0:T(8,128)S(1)}, u32[]{:S(2)}, u32[]{:S(2)}) collective-permute-start(f32[64,512]{1,0:T(8,128)} %get-tuple-element.31), channel_id=1, source_target_pairs={{0,1},{1,2},{2,3},{3,0},{4,5},{5,6},{6,7},{7,4},{8,9},{9,10},{10,1... | collective-permute-start | bytes 393224 | tf_op jit(solution)/shard_map/ppermute | solution.py:473
  48.4 14.7 %collective-permute-start.15 = (f32[64,512]{1,0:T(8,128)}, f32[64,512]{1,0:T(8,128)S(1)}, u32[]{:S(2)}, u32[]{:S(2)}) collective-permute-start(f32[64,512]{1,0:T(8,128)} %get-tuple-element.32), channel_id=1, source_target_pairs={{0,3},{1,0},{2,1},{3,2},{4,7},{5,4},{6,5},{7,6},{8,11},{9,8},{10,9... | collective-permute-start | bytes 393224 | tf_op jit(solution)/shard_map/ppermute | solution.py:473
  57.7 5.5 %copy-start.24 = (f32[64,512]{1,0:T(8,128)}, f32[64,512]{1,0:T(8,128)S(1)}, u32[]{:S(2)}) copy-start(f32[64,512]{1,0:T(8,128)S(1)} %collective-permute-done.13.a_ref) | copy-start | bytes 393220
  57.7 27.4 %collective-permute-start.7 = (bf16[1040,128]{1,0:T(8,128)(2,1)}, bf16[1040,128]{1,0:T(8,128)(2,1)S(1)}, u32[]{:S(2)}, u32[]{:S(2)}) collective-permute-start(bf16[1040,128]{1,0:T(8,128)(2,1)} %join.2.refs_2_.refs_0_), channel_id=1, source_target_pairs={{0,96},{32,0},{64,32},{96,64},{128,224},{160,128},{192,160},{224,1... | collective-permute-start | bytes 798728 | tf_op jit(solution)/shard_map/ppermute | solution.py:465
  60.2 3.0 %copy-start.25 = (f32[64,512]{1,0:T(8,128)}, f32[64,512]{1,0:T(8,128)S(1)}, u32[]{:S(2)}) copy-start(f32[64,512]{1,0:T(8,128)S(1)} %collective-permute-done.14.b_ref) | copy-start | bytes 393220
  60.2 25.6 %collective-permute-start.8 = (bf16[1040,128]{1,0:T(8,128)(2,1)}, bf16[1040,128]{1,0:T(8,128)(2,1)S(1)}, u32[]{:S(2)}, u32[]{:S(2)}) collective-permute-start(bf16[1040,128]{1,0:T(8,128)(2,1)} %join.3.refs_3_.refs_1_), channel_id=1, source_target_pairs={{0,32},{32,64},{64,96},{96,0},{128,160},{160,192},{192,224},{224,1... | collective-permute-start | bytes 798728 | tf_op jit(solution)/shard_map/ppermute | solution.py:465
  60.2 28.2 %collective-permute-start.2 = (bf16[1040,128]{1,0:T(8,128)(2,1)S(1)}, bf16[1040,128]{1,0:T(8,128)(2,1)S(1)}, u32[]{:S(2)}, u32[]{:S(2)}) collective-permute-start(bf16[1040,128]{1,0:T(8,128)(2,1)S(1)} %collective-permute-done.1.refs_2_), channel_id=1, source_target_pairs={{0,32},{32,64},{64,96},{96,0},{128,160},{160,192},{192,224},{224,1... | collective-permute-start | bytes 798728 | tf_op jit(solution)/shard_map/ppermute | solution.py:465
  60.5 28.0 %collective-permute-start.6 = (bf16[1040,128]{1,0:T(8,128)(2,1)S(1)}, bf16[1040,128]{1,0:T(8,128)(2,1)S(1)}, u32[]{:S(2)}, u32[]{:S(2)}) collective-permute-start(bf16[1040,128]{1,0:T(8,128)(2,1)S(1)} %collective-permute-done.5.refs_5_), channel_id=1, source_target_pairs={{0,96},{32,0},{64,32},{96,64},{128,224},{160,128},{192,160},{224,1... | collective-permute-start | bytes 798728 | tf_op jit(solution)/shard_map/ppermute | solution.py:465
  63.2 0.7 copy-start.26
  65.7 3.9 %collective-permute-start.18 = (f32[64,128]{1,0:T(8,128)}, f32[64,128]{1,0:T(8,128)S(1)}, u32[]{:S(2)}, u32[]{:S(2)}) collective-permute-start(f32[64,128]{1,0:T(8,128)} %get-tuple-element.34.own_ref), channel_id=1, source_target_pairs={{0,12},{1,13},{2,14},{3,15},{4,0},{5,1},{6,2},{7,3},{8,4},{9,5},{1... | collective-permute-start | bytes 98312 | tf_op jit(solution)/shard_map/ppermute | solution.py:469
  69.6 12.6 %copy-start.31 = (f32[64,128]{1,0:T(8,128)}, f32[64,128]{1,0:T(8,128)S(1)}, u32[]{:S(2)}) copy-start(f32[64,128]{1,0:T(8,128)S(1)} %collective-permute-done.18.c_ref) | copy-start | bytes 98308
  69.6 4.9 %collective-permute-start.17 = (f32[64,128]{1,0:T(8,128)}, f32[64,128]{1,0:T(8,128)S(1)}, u32[]{:S(2)}, u32[]{:S(2)}) collective-permute-start(f32[64,128]{1,0:T(8,128)} %get-tuple-element.34.own_ref), channel_id=1, source_target_pairs={{0,4},{1,5},{2,6},{3,7},{4,8},{5,9},{6,10},{7,11},{8,12},{9,13},{1... | collective-permute-start | bytes 98312 | tf_op jit(solution)/shard_map/ppermute | solution.py:469
  74.6 7.7 %copy-start.32 = (f32[64,128]{1,0:T(8,128)}, f32[64,128]{1,0:T(8,128)S(1)}, u32[]{:S(2)}) copy-start(f32[64,128]{1,0:T(8,128)S(1)} %collective-permute-done.17.b_ref) | copy-start | bytes 98308
  74.6 7.7 %collective-permute-start.16 = (f32[64,128]{1,0:T(8,128)}, f32[64,128]{1,0:T(8,128)S(1)}, u32[]{:S(2)}, u32[]{:S(2)}) collective-permute-start(f32[64,128]{1,0:T(8,128)} %get-tuple-element.34.own_ref), channel_id=1, source_target_pairs={{0,8},{1,9},{2,10},{3,11},{4,12},{5,13},{6,14},{7,15},{8,0},{9,1},... | collective-permute-start | bytes 98312 | tf_op jit(solution)/shard_map/ppermute | solution.py:469
  75.3 1.0 copy-start.1
  76.2 1.0 copy-start.3
  80.4 1.0 copy-start.14
  81.5 0.8 copy-start.16
  82.3 0.6 copy-start.33
  84.3 21.2 %collective-permute-start.21 = (f32[64,128]{1,0:T(8,128)}, f32[64,128]{1,0:T(8,128)S(1)}, u32[]{:S(2)}, u32[]{:S(2)}) collective-permute-start(f32[64,128]{1,0:T(8,128)} %squares.1.own_ref), channel_id=1, source_target_pairs={{0,3},{1,0},{2,1},{3,2},{4,7},{5,4},{6,5},{7,6},{8,11},{9,8},{10,9... | collective-permute-start | bytes 98312 | tf_op jit(solution)/shard_map/ppermute | solution.py:473
  85.1 20.4 %collective-permute-start.20 = (f32[64,128]{1,0:T(8,128)}, f32[64,128]{1,0:T(8,128)S(1)}, u32[]{:S(2)}, u32[]{:S(2)}) collective-permute-start(f32[64,128]{1,0:T(8,128)} %squares.1.own_ref), channel_id=1, source_target_pairs={{0,1},{1,2},{2,3},{3,0},{4,5},{5,6},{6,7},{7,4},{8,9},{9,10},{10,1... | collective-permute-start | bytes 98312 | tf_op jit(solution)/shard_map/ppermute | solution.py:473
  85.8 19.7 %collective-permute-start.19 = (f32[64,128]{1,0:T(8,128)}, f32[64,128]{1,0:T(8,128)S(1)}, u32[]{:S(2)}, u32[]{:S(2)}) collective-permute-start(f32[64,128]{1,0:T(8,128)} %squares.1.own_ref), channel_id=1, source_target_pairs={{0,2},{1,3},{2,0},{3,1},{4,6},{5,7},{6,4},{7,5},{8,10},{9,11},{10,... | collective-permute-start | bytes 98312 | tf_op jit(solution)/shard_map/ppermute | solution.py:473
  88.5 1.0 copy-start.2
  89.4 1.0 copy-start.4
  90.7 0.6 copy-start.6
  91.3 21.9 %collective-permute-start.9 = (bf16[8,2,2,16,128]{4,3,2,1,0:T(8,128)(2,1)S(1)}, bf16[8,2,2,16,128]{4,3,2,1,0:T(8,128)(2,1)S(1)}, u32[]{:S(2)}, u32[]{:S(2)}) collective-permute-start(bf16[8,2,2,16,128]{4,3,2,1,0:T(8,128)(2,1)S(1)} %get-tuple-element.24), channel_id=1, source_target_pairs={{0,16},{16,0},{1,17},{17,1},{2,18},{18,2},{3,19},{19,3},{4,20},{20... | collective-permute-start | bytes 393224 | tf_op jit(solution)/shard_map/ppermute | solution.py:535
  95.6 1.2 %copy-start.15 = (f32[1024,256]{1,0:T(8,128)S(1)}, f32[1024,256]{1,0:T(8,128)}, u32[]{:S(2)}) copy-start(f32[1024,256]{1,0:T(8,128)} %copy-done.14) | copy-start | bytes 3145732
  96.9 1.0 copy-start.17
  104.7 0.8 copy-start.12
  105.5 0.6 copy-start.28
  105.5 0.6 copy-start.29
  105.5 0.6 copy-start.30
  107.7 1.0 copy-start.13
  113.2 0.6 copy-start.27

commit v2 on v1

--- a/solution.py
+++ b/solution.py
@@ -17,8 +17,8 @@
 TOKENS = 256
 PAGES = TOKENS // PAGE_TOKENS
 HALF = HEAD_SIZE // 2
-PACKED = 4 * TOKENS // 2
-CHUNK = 4 * TOKENS
+PACKED = 4 * HALF
+CHUNK = 4 * HEAD_SIZE
 TAIL = 16
 COLUMNS = 8192
 QUARTER = COLUMNS // 4
@@ -30,7 +30,14 @@
 LOG2_SCALE = math.log2(math.e) * HEAD_SIZE**-0.5
 VMEM = pltpu.VMEM
 SMEM = pltpu.SMEM
-PARAMS = pltpu.CompilerParams(vmem_limit_bytes=48 * 1024 * 1024)
+MIB = 1024 * 1024
+
+
+def params(mebibytes):
+    return pltpu.CompilerParams(vmem_limit_bytes=mebibytes * MIB)
+
+
+SMALL = pl.CostEstimate(flops=1024, bytes_accessed=1024, transcendentals=0)
 
 
 def spec(space=VMEM):
@@ -50,17 +57,12 @@
 
 
 def pack_kernel(owner_ref, context_ref, block_ref, out_ref):
-    half = TOKENS // 2
     for number in range(4):
         source = context_ref if number < 2 else block_ref
-        piece = source[0, number % 2]
-        out_ref[number * half : (number + 1) * half, :] = jnp.concatenate(
-            [piece[:half], piece[half:]], axis=1
-        )
+        out_ref[number * HALF : (number + 1) * HALF, :] = source[0, number % 2]
     owners = [owner_ref[p] for p in range(PAGES)]
-    page = lax.broadcasted_iota(jnp.int32, (TAIL, HEAD_SIZE), 1) // PAGE_TOKENS
-    page = page + lax.broadcasted_iota(jnp.int32, (TAIL, HEAD_SIZE), 0) * (HEAD_SIZE // PAGE_TOKENS)
-    codes = jnp.full((TAIL, HEAD_SIZE), -1, jnp.int32)
+    page = lax.broadcasted_iota(jnp.int32, (TAIL, TOKENS), 1) // PAGE_TOKENS
+    codes = jnp.full((TAIL, TOKENS), -1, jnp.int32)
     for p in range(PAGES):
         rank = jnp.int32(0)
         for q in range(p):
@@ -72,54 +74,43 @@
 def pack(page_owner, context_cache, new_block_cache):
     return pl.pallas_call(
         pack_kernel,
-        out_shape=shape((PACKED + TAIL, HEAD_SIZE), BF16),
+        out_shape=shape((PACKED + TAIL, TOKENS), BF16),
         in_specs=[spec(SMEM), spec(), spec()],
         out_specs=spec(),
+        compiler_params=params(4),
+        cost_estimate=SMALL,
         name="pack",
     )(page_owner, context_cache, new_block_cache)
 
 
-def join_kernel(mine_ref, other_ref, out_ref):
+def join_kernel(mine_ref, other_ref, after_ref, out_ref):
     odd = lax.axis_index("tp") % 2
-    half = TOKENS // 2
-
-    def write(first_ref, second_ref):
-        for number in range(4):
-            rows = slice(number * half, (number + 1) * half)
-            first, second = first_ref[rows, :], second_ref[rows, :]
-            out_ref[number * TOKENS : number * TOKENS + half, :] = jnp.concatenate(
-                [first[:, :HALF], second[:, :HALF]], axis=1
-            )
-            out_ref[number * TOKENS + half : (number + 1) * TOKENS, :] = jnp.concatenate(
-                [first[:, HALF:], second[:, HALF:]], axis=1
-            )
-
-    @pl.when(odd == 0)
-    def _():
-        write(mine_ref, other_ref)
-
-    @pl.when(odd == 1)
-    def _():
-        write(other_ref, mine_ref)
-
+    for number in range(4):
+        rows = slice(number * HALF, (number + 1) * HALF)
+        here = pl.multiple_of(number * HEAD_SIZE + odd * HALF, HALF)
+        there = pl.multiple_of(number * HEAD_SIZE + (1 - odd) * HALF, HALF)
+        out_ref[pl.ds(here, HALF), :] = mine_ref[rows, :]
+        out_ref[pl.ds(there, HALF), :] = other_ref[rows, :]
     out_ref[CHUNK:, :] = mine_ref[PACKED:, :]
 
 
-def join(mine, other):
+def join(mine, other, after):
     return pl.pallas_call(
         join_kernel,
-        out_shape=shape((CHUNK + TAIL, HEAD_SIZE), BF16),
-        in_specs=[spec(), spec()],
+        out_shape=shape((CHUNK + TAIL, TOKENS), BF16),
+        in_specs=[spec(), spec(), spec(pl.ANY)],
         out_specs=spec(),
+        compiler_params=params(4),
+        cost_estimate=SMALL,
         name="join",
-    )(mine, other)
+    )(mine, other, after)
 
 
 def attend_kernel(offsets, first, last, *refs):
     offset_ref, query_ref = refs[:2]
     count = len(offsets)
     chunks = refs[2 : 2 + count]
-    refs = refs[2 + count :]
+    refs = refs[3 + count :]
     if not first:
         top_in, sum_in = refs[:2]
         refs = refs[2:]
@@ -130,7 +121,7 @@
     blk = lax.axis_index("blk")
     offset = offset_ref[lax.axis_index("group")]
     lane = lax.broadcasted_iota(jnp.int32, (1, TOKENS), 1)
-    ones = jnp.ones((2 * TOKENS, HEAD_SIZE), BF16)
+    ones = jnp.ones((HEAD_SIZE, 2 * TOKENS), BF16)
     rows_causal = lax.broadcasted_iota(jnp.int32, (TOKENS, TOKENS), 0)
     keys_causal = lax.broadcasted_iota(jnp.int32, (TOKENS, TOKENS), 1)
     keys, values, bias = [], [], []
@@ -138,8 +129,11 @@
         source = (blk // 4 + flip) % 2 * 4 + (blk % 4 + turn + 4) % 4
         bias.append(jnp.where(source * TOKENS + lane < offset, 0.0, LOW_SCORE))
         bias.append(jnp.where(source * TOKENS + 0 * lane <= blk * TOKENS, 0.0, LOW_SCORE))
-        keys += [chunk[:TOKENS, :], chunk[2 * TOKENS : 3 * TOKENS, :]]
-        values += [chunk[TOKENS : 2 * TOKENS, :], chunk[3 * TOKENS : 4 * TOKENS, :]]
+        parts = [chunk[n * HEAD_SIZE : (n + 1) * HEAD_SIZE, :] for n in range(4)]
+        keys += [parts[0], parts[2]]
+        values.append(
+            jnp.concatenate([jnp.concatenate([parts[1], parts[3]], axis=1), ones], axis=0)
+        )
     for head in range(HEADS):
         query = query_ref[0, :, head * HEAD_SIZE : (head + 1) * HEAD_SIZE]
         rows = slice(head * TOKENS, (head + 1) * TOKENS)
@@ -152,7 +146,7 @@
         for number in range(count):
             scores = []
             for part in (2 * number, 2 * number + 1):
-                score = dot_t(query, keys[part]) * LOG2_SCALE + bias[part]
+                score = dot(query, keys[part]) * LOG2_SCALE + bias[part]
                 if offsets[number] == (0, 0) and part % 2 == 1:
                     score = jnp.where(keys_causal <= rows_causal, score, LOW_SCORE)
                 scores.append(score)
@@ -161,10 +155,7 @@
             weight = jnp.exp2(score - top_now)
             high = weight.astype(BF16)
             low = (weight - high.astype(F32)).astype(BF16)
-            value = jnp.concatenate(
-                [jnp.concatenate(values[2 * number : 2 * number + 2], axis=0), ones], axis=1
-            )
-            fresh = dot(high, value) + dot(low, value)
+            fresh = dot_t(high, values[number]) + dot_t(low, values[number])
             if first and number == 0:
                 total = fresh
             else:
@@ -179,30 +170,30 @@
             sum_out[rows, :] = total
 
 
-def attend(block_offset, queries, chunks, offsets, state, last):
+def attend(block_offset, queries, chunks, offsets, state, last, after):
     first = state is None
-    operands = [block_offset, queries, *chunks] + ([] if first else list(state))
+    operands = [block_offset, queries, *chunks, after] + ([] if first else list(state))
     rows = HEADS * TOKENS
     if last:
         out = shape((1, TOKENS, HEADS * HEAD_SIZE), BF16)
     else:
         out = (shape((rows, HEAD_SIZE), F32), shape((rows, 2 * HEAD_SIZE), F32))
-    pairs = rows * len(chunks) * 2 * TOKENS
     return pl.pallas_call(
         functools.partial(attend_kernel, offsets, first, last),
         out_shape=out,
-        in_specs=[spec(SMEM)] + [spec()] * (len(operands) - 1),
+        in_specs=[spec(SMEM)]
+        + [spec()] * (1 + len(chunks))
+        + [spec(pl.ANY)]
+        + [spec()] * (0 if first else 2),
         out_specs=spec() if last else (spec(), spec()),
-        compiler_params=PARAMS,
-        cost_estimate=pl.CostEstimate(
-            flops=pairs * HEAD_SIZE * 10, bytes_accessed=2 << 20, transcendentals=pairs
-        ),
+        compiler_params=params(24),
+        cost_estimate=SMALL,
         name="attend",
     )(*operands)
 
 
 def pages_kernel(offsets, *refs):
-    chunks, (mine_ref, other_ref) = refs[:-2], refs[-2:]
+    chunks, (mine_ref, other_ref) = refs[:-3], refs[-2:]
     blk = lax.axis_index("blk")
     instance = blk * 2 + lax.axis_index("group")
     other = blk * 2 + 1 - lax.axis_index("group")
@@ -213,12 +204,11 @@
     wanted = jnp.where(row % PAGE_TOKENS == token % PAGE_TOKENS, wanted, -2).astype(F32)
     for (flip, turn), chunk in zip(offsets, chunks):
         source = (blk // 4 + flip) % 2 * 4 + (blk % 4 + turn + 4) % 4
-        codes = chunk[CHUNK : CHUNK + TAIL, :].astype(F32)
-        codes = jnp.concatenate([codes[0:1], codes[1:2]], axis=1)
-        chooser = (wanted == codes).astype(BF16)
+        codes = chunk[CHUNK : CHUNK + TAIL, :].astype(F32)[0:1]
+        chooser = jnp.where(wanted == codes, 1.0, 0.0).astype(BF16)
         for part in range(2):
-            cache = chunk[(2 + part) * TOKENS : (3 + part) * TOKENS, :]
-            found = dot(chooser, cache).astype(BF16)
+            cache = chunk[(2 + part) * HEAD_SIZE : (3 + part) * HEAD_SIZE, :]
+            found = dot_t(chooser, cache).astype(BF16)
             for rank in range(2):
                 mine_ref[source, rank, part] = found[rank * PAGE_TOKENS : (rank + 1) * PAGE_TOKENS]
                 other_ref[source, rank, part] = found[
@@ -226,32 +216,35 @@
                 ]
 
 
-def select_pages(chunks, offsets):
+def select_pages(chunks, offsets, after):
     out = shape((8, 2, 2, PAGE_TOKENS, HEAD_SIZE), BF16)
     return pl.pallas_call(
         functools.partial(pages_kernel, offsets),
         out_shape=(out, out),
-        in_specs=[spec()] * len(chunks),
+        in_specs=[spec()] * len(chunks) + [spec(pl.ANY)],
         out_specs=(spec(), spec()),
-        compiler_params=PARAMS,
+        compiler_params=params(8),
+        cost_estimate=SMALL,
         name="pages",
-    )(*chunks)
-
-
-def pool_kernel(mine_ref, came_ref, out_ref):
+    )(*chunks, after)
+
+
+def pool_kernel(mine_ref, came_ref, after_ref, out_ref):
     group = lax.axis_index("group")
     out_ref[:, group] = mine_ref[...]
     out_ref[:, 1 - group] = came_ref[...]
 
 
-def pool(mine, came):
+def pool(mine, came, after):
     return pl.pallas_call(
         pool_kernel,
         out_shape=shape((8, 2, 2, 2, PAGE_TOKENS, HEAD_SIZE), BF16),
-        in_specs=[spec(), spec()],
+        in_specs=[spec(), spec(), spec(pl.ANY)],
         out_specs=spec(),
+        compiler_params=params(4),
+        cost_estimate=SMALL,
         name="pool",
-    )(mine, came)
+    )(mine, came, after)
 
 
 def attend_rows(length_ref, query_ref, step_ref, cache_ref, attended_ref, score_ref, mixed_ref):
@@ -339,15 +332,6 @@
         turn = jnp.where(slot == 0, 2, jnp.where(slot == 1, 1, jnp.where(slot == 2, 3, 0)))
         return (0, (y[0] + turn) % 4 * TILES + j % TILES)
 
-    def whole(a):
-        dims = a.shape
-        return pl.BlockSpec(dims, lambda j, y: (0,) * len(dims))
-
-    def out_block(slot):
-        return pl.BlockSpec(
-            (rows, width), lambda j, y: (0, jnp.clip(j - slot * TILES, 0, TILES - 1))
-        )
-
     return pl.pallas_call(
         decode_kernel,
         out_shape=tuple(shape((rows, QUARTER), BF16 if t else F32) for t in TURNS),
@@ -355,13 +339,6 @@
             num_scalar_prefetch=2,
             grid=(4 * TILES,),
             in_specs=[
-                whole(step_query),
-                whole(step_cache),
-                whole(row_cache),
-                pl.BlockSpec((out_weight.shape[0], width), lambda j, y, l: weight_block(j, y)),
-            ]
-            if False
-            else [
                 pl.BlockSpec(step_query.shape, lambda j, y, l: (0,) * 4),
                 pl.BlockSpec(step_cache.shape, lambda j, y, l: (0,) * 5),
                 pl.BlockSpec(row_cache.shape, lambda j, y, l: (0,) * 5),
@@ -380,15 +357,13 @@
                 pltpu.VMEM((HEADS * rows, HEAD_SIZE), F32),
             ],
         ),
-        compiler_params=PARAMS,
-        cost_estimate=pl.CostEstimate(
-            flops=2 * rows * 512 * COLUMNS, bytes_accessed=12 << 20, transcendentals=1 << 16
-        ),
+        compiler_params=params(56),
+        cost_estimate=SMALL,
         name="decode",
     )(place, row_lengths, step_query, step_cache, row_cache, out_weight)
 
 
-def quarter_kernel(own_ref, a_ref, b_ref, c_ref, *outs):
+def quarter_kernel(own_ref, a_ref, b_ref, c_ref, after_ref, *outs):
     z = lax.axis_index("tp") % 4
     for out, turn in zip(outs, TURNS):
         columns = pl.ds(pl.multiple_of((z + turn) % 4 * SHARE, SHARE), SHARE)
@@ -400,65 +375,65 @@
         )
 
 
-def sum_quarters(own, came):
+def sum_quarters(own, came, after):
     return pl.pallas_call(
         quarter_kernel,
         out_shape=tuple(shape((STEPS * ROWS, SHARE), F32) for _ in TURNS),
-        in_specs=[spec()] * 4,
+        in_specs=[spec()] * 4 + [spec(pl.ANY)],
         out_specs=(spec(),) * 4,
+        compiler_params=params(4),
+        cost_estimate=SMALL,
         name="quarters",
-    )(own, *came)
-
-
-def hidden_kernel(residual_ref, own_ref, a_ref, b_ref, c_ref, hidden_ref, square_ref):
+    )(own, *came, after)
+
+
+def diagonal():
+    rows = lax.broadcasted_iota(jnp.int32, (STEPS * ROWS, HEAD_SIZE), 0)
+    return rows == lax.broadcasted_iota(jnp.int32, (STEPS * ROWS, HEAD_SIZE), 1)
+
+
+def hidden_kernel(residual_ref, own_ref, a_ref, b_ref, c_ref, after_ref, hidden_ref, square_ref):
     residual = residual_ref[0].reshape(STEPS * ROWS, SHARE).astype(F32)
     hidden = residual + (own_ref[...] + a_ref[...] + b_ref[...] + c_ref[...])
     hidden_ref[...] = hidden
-    square_ref[...] = jnp.broadcast_to(
-        jnp.sum(hidden * hidden, axis=1, keepdims=True), square_ref.shape
-    )
-
-
-def sum_shares(residual, own, came):
+    square = jnp.sum(hidden * hidden, axis=1, keepdims=True)
+    square = jnp.sum(jnp.where(diagonal(), square, 0.0), axis=0, keepdims=True)
+    square_ref[...] = jnp.broadcast_to(square[None], square_ref.shape)
+
+
+def sum_shares(residual, own, came, after):
     return pl.pallas_call(
         hidden_kernel,
-        out_shape=(shape((STEPS * ROWS, SHARE), F32), shape((STEPS * ROWS, HEAD_SIZE), F32)),
-        in_specs=[spec()] * 5,
+        out_shape=(
+            shape((STEPS * ROWS, SHARE), F32),
+            shape((16, 8, HEAD_SIZE), F32),
+        ),
+        in_specs=[spec()] * 5 + [spec(pl.ANY)],
         out_specs=(spec(), spec()),
+        compiler_params=params(4),
+        cost_estimate=SMALL,
         name="hidden",
-    )(residual, own, *came)
-
-
-def squares_kernel(own_ref, a_ref, b_ref, c_ref, out_ref):
-    out_ref[...] = own_ref[...] + a_ref[...] + b_ref[...] + c_ref[...]
-
-
-def sum_squares(own, came):
-    return pl.pallas_call(
-        squares_kernel,
-        out_shape=shape((STEPS * ROWS, HEAD_SIZE), F32),
-        in_specs=[spec()] * 4,
-        out_specs=spec(),
-        name="squares",
-    )(own, *came)
-
-
-def finish_kernel(hidden_ref, gain_ref, own_ref, a_ref, b_ref, c_ref, out_ref):
-    square = own_ref[...] + a_ref[...] + b_ref[...] + c_ref[...]
+    )(residual, own, *came, after)
+
+
+def finish_kernel(hidden_ref, gain_ref, square_ref, after_ref, out_ref):
+    square = jnp.sum(square_ref[...], axis=0)[0:1]
+    square = jnp.sum(jnp.where(diagonal(), square, 0.0), axis=1, keepdims=True)
     scale = lax.rsqrt(square * (1.0 / COLUMNS) + EPSILON)
-    scale = jnp.concatenate([scale] * (SHARE // HEAD_SIZE), axis=1)
-    out = hidden_ref[...] * scale * gain_ref[...].astype(F32)
+    out = hidden_ref[...] * scale * gain_ref[...].reshape(1, SHARE).astype(F32)
     out_ref[0] = out.astype(BF16).reshape(STEPS, ROWS, SHARE)
 
 
-def finish(hidden, gain, own, came):
+def finish(hidden, gain, squares, after):
     return pl.pallas_call(
         finish_kernel,
         out_shape=shape((1, STEPS, ROWS, SHARE), BF16),
-        in_specs=[spec()] * 6,
+        in_specs=[spec()] * 3 + [spec(pl.ANY)],
         out_specs=spec(),
+        compiler_params=params(4),
+        cost_estimate=SMALL,
         name="finish",
-    )(hidden, gain, own, *came)
+    )(hidden, gain, squares, after)
 
 
 def move_x(a, turn):
@@ -487,7 +462,11 @@
     residual,
     norm_gain,
 ):
-    packed = pack(page_owner.reshape(PAGES), context_cache, new_block_cache)
+    packed = pack(
+        page_owner.reshape(PAGES),
+        jnp.swapaxes(context_cache, 2, 3),
+        jnp.swapaxes(new_block_cache, 2, 3),
+    )
     near = lax.ppermute(packed, "tp", [(i, i ^ 1) for i in range(16)])
     far = lax.ppermute(packed, "blk", [(i, i ^ 4) for i in range(8)])
     far_near = lax.ppermute(
@@ -501,20 +480,20 @@
     )
     came = [move_y(a, turn) for a, turn in zip(parts[:3], TURNS)]
 
-    chunk = join(packed, near)
-    chunk_far = join(far, far_near)
+    chunk = join(packed, near, parts[3])
     up = move_x(chunk, 1)
     down = move_x(chunk, 3)
+    chunk_far = join(far, far_near, chunk)
     far_up = move_x(chunk_far, 1)
     far_down = move_x(chunk_far, 3)
     up_two = move_x(up, 1)
     far_down_two = move_x(far_down, 3)
 
-    state = attend(block_offset, prompt_query, [chunk, chunk_far], [(0, 0), (1, 0)], None, False)
-
-    shares = sum_quarters(parts[3], came)
+    state = attend(
+        block_offset, prompt_query, [chunk, chunk_far], [(0, 0), (1, 0)], None, False, chunk_far
+    )
+    shares = sum_quarters(parts[3], came, state[0])
     came = [move_z(a, turn) for a, turn in zip(shares[:3], TURNS)]
-
     state = attend(
         block_offset,
         prompt_query,
@@ -522,22 +501,19 @@
         [(0, -1), (0, 1), (1, -1), (1, 1)],
         state,
         False,
-    )
-
-    hidden, square = sum_shares(residual, shares[3], came)
-    came = [move_y(square, turn) for turn in TURNS[:3]]
-    square = sum_squares(square, came)
-    came = [move_z(square, turn) for turn in TURNS[:3]]
-
+        shares[3],
+    )
+    hidden, square = sum_shares(residual, shares[3], came, state[0])
+    squares = lax.all_to_all(square, "tp", split_axis=0, concat_axis=0, tiled=True)
     chunks = [chunk, chunk_far, up, down, far_up, far_down, up_two, far_down_two]
     offsets = [(0, 0), (1, 0), (0, -1), (0, 1), (1, -1), (1, 1), (0, 2), (1, 2)]
-    mine, other = select_pages(chunks, offsets)
+    mine, other = select_pages(chunks, offsets, hidden)
     other = lax.ppermute(other, "group", [(0, 1), (1, 0)])
     prefill_out = attend(
-        block_offset, prompt_query, [up_two, far_down_two], [(0, 2), (1, 2)], state, True
-    )
-    page_pool = pool(mine, other).reshape(1, 32, 2, PAGE_TOKENS, HEAD_SIZE)
-    decode_out = finish(hidden, norm_gain.reshape(1, SHARE), square, came)
+        block_offset, prompt_query, [up_two, far_down_two], [(0, 2), (1, 2)], state, True, mine
+    )
+    page_pool = pool(mine, other, prefill_out).reshape(1, 32, 2, PAGE_TOKENS, HEAD_SIZE)
+    decode_out = finish(hidden, norm_gain, squares, page_pool)
     return (prefill_out, page_pool, decode_out)
 
 

time: 116 us -> 74 us (0.64)
  the two profiles are of different devices: /device:TPU:1 before, /device:TPU:6 now
where the time goes in v2:
time: 74 us; the launch traced here: 73.4 us
  starting transfers between devices  30.9 us (42%)
  Pallas kernels  29.3 us (40%)
  local copies, waits for them, and re-layouts  6.36 us (9%)
  waiting for transfers between devices  6.12 us (8%)
  between operations  0.79 us (1%)
    pallas_call x3, Pallas kernels, attend(): pl.pallas_call(functools.partial(attend_kernel, offsets, first, last), ou...  14.4 us
    pallas_call x1, Pallas kernels, decode(): pl.pallas_call(decode_kernel, out_shape=tuple((shape((rows, QUARTER), BF1...  11.3 us
    ppermute x6, starting transfers between devices, move_x(): lax.ppermute(a, 'blk', [(i, i // 4 * 4 + (i + turn) % 4) for i in range(8)])  7.8 us
    unnamed x22, local copies, waits for them, and re-layouts  6.36 us
    ppermute x1, starting transfers between devices, body(): far = lax.ppermute(packed, 'blk', [(i, i ^ 4) for i in range(8)])  6.29 us
    ppermute x3, starting transfers between devices, move_z(): lax.ppermute(a, 'tp', [(i, i // 4 * 4 + (i + turn) % 4) for i in range(16)])  5.47 us
    ppermute x3, starting transfers between devices, move_y(): return lax.ppermute(a, 'tp', [(i, (i + 4 * turn) % 16) for i in range(16)])  5.35 us
    all_to_all x1, starting transfers between devices, body(): lax.all_to_all(square, 'tp', split_axis=0, concat_axis=0, tiled=True)  3.86 us
  transfers between devices with their start and end apart: 17, of which 4 were waited for; matrix products, arithmetic and copies ran while one was open for 0% of the time, Pallas kernels for 37%

profile of v2, /device:TPU:6, one launch (start us, length us, event | category | flops | bytes accessed | tf_op | source)
XLA Modules:
  0.0 73.4 jit_solution(18238272294372000260)
XLA Ops:
  0.6 0.0 copy-start
  0.6 0.0 copy-start.6
  0.7 0.9 %copy-done.6 = bf16[1,2,256,64]{2,3,1,0:T(8,128)(2,1)S(1)} copy-done((bf16[1,2,256,64]{2,3,1,0:T(8,128)(2,1)S(1)}, bf16[1,2,256,64]{2,3,1,0:T(8,128)(2,1)}, u32[]{:S(2)}) %copy-start.6) | copy-done | bytes 65560
  1.5 0.0 copy-start.7
  1.5 0.8 %copy-done.7 = bf16[1,2,256,64]{2,3,1,0:T(8,128)(2,1)S(1)} copy-done((bf16[1,2,256,64]{2,3,1,0:T(8,128)(2,1)S(1)}, bf16[1,2,256,64]{2,3,1,0:T(8,128)(2,1)}, u32[]{:S(2)}) %copy-start.7) | copy-done | bytes 65560
  2.4 0.0 copy-start.10
  2.4 0.7 copy-done.10
  3.0 0.0 copy-start.8
  3.0 0.7 pack.1.mine_ref
  3.7 2.0 %collective-permute-start = (bf16[272,256]{1,0:T(8,128)(2,1)S(1)}, bf16[272,256]{1,0:T(8,128)(2,1)S(1)}, u32[]{:S(2)}, u32[]{:S(2)}) collective-permute-start(bf16[272,256]{1,0:T(8,128)(2,1)S(1)} %pack.1.mine_ref), channel_id=1, source_target_pairs={{0,1},{1,0},{2,3},{3,2},{4,5},{5,4},{6,7},{7,6},{8,9},{9,8},{10,11... | collective-permute-start | bytes 417800 | tf_op jit(solution)/shard_map/ppermute | solution.py:470
  5.7 6.3 %collective-permute-start.3 = (bf16[272,256]{1,0:T(8,128)(2,1)S(1)}, bf16[272,256]{1,0:T(8,128)(2,1)S(1)}, u32[]{:S(2)}, u32[]{:S(2)}) collective-permute-start(bf16[272,256]{1,0:T(8,128)(2,1)S(1)} %pack.1.mine_ref), channel_id=1, source_target_pairs={{0,128},{32,160},{64,192},{96,224},{128,0},{160,32},{192,64},{224,... | collective-permute-start | bytes 417800 | tf_op jit(solution)/shard_map/ppermute | solution.py:471
  12.0 0.0 collective-permute-start.4
  12.0 0.0 copy-start.5
  12.0 11.3 %decode.1 = (bf16[64,2048]{1,0:T(8,128)(2,1)}, bf16[64,2048]{1,0:T(8,128)(2,1)}, bf16[64,2048]{1,0:T(8,128)(2,1)}, f32[64,2048]{1,0:T(8,128)}) custom-call(s32[1]{0:T(128)} %bitcast.3.y_ref, s32[16]{0:T(128)} %bitcast.11, bf16[1,4,16,512]{3,2,1,0:T(8,128)(2,1)} %query_ref.1, bf16[1,4,2,16,128]{4,3,2,1,0:T(8,128)(2,1)} %step_ref.1, ...), custom_call_target="tpu_custom_call" | custom-call | flops 1024 | bytes 1024 | tf_op jit(solution)/shard_map/decode/pallas_call | solution.py:335
  23.3 0.0 copy-start.9
  23.3 1.6 %collective-permute-start.10 = (bf16[64,2048]{1,0:T(8,128)(2,1)}, bf16[64,2048]{1,0:T(8,128)(2,1)S(1)}, u32[]{:S(2)}, u32[]{:S(2)}) collective-permute-start(bf16[64,2048]{1,0:T(8,128)(2,1)} %get-tuple-element.21), channel_id=1, source_target_pairs={{0,4},{1,5},{2,6},{3,7},{4,8},{5,9},{6,10},{7,11},{8,12},{9,13},{1... | collective-permute-start | bytes 786440 | tf_op jit(solution)/shard_map/ppermute | solution.py:444
  24.9 1.7 %collective-permute-start.11 = (bf16[64,2048]{1,0:T(8,128)(2,1)}, bf16[64,2048]{1,0:T(8,128)(2,1)S(1)}, u32[]{:S(2)}, u32[]{:S(2)}) collective-permute-start(bf16[64,2048]{1,0:T(8,128)(2,1)} %get-tuple-element.22), channel_id=1, source_target_pairs={{0,12},{1,13},{2,14},{3,15},{4,0},{5,1},{6,2},{7,3},{8,4},{9,5},{1... | collective-permute-start | bytes 786440 | tf_op jit(solution)/shard_map/ppermute | solution.py:444
  26.6 0.0 collective-permute-done.other_ref
  26.6 0.0 copy-start.1
  26.6 1.0 %copy-done.1 = f32[64,2048]{1,0:T(8,128)S(1)} copy-done((f32[64,2048]{1,0:T(8,128)S(1)}, f32[64,2048]{1,0:T(8,128)}, u32[]{:S(2)}) %copy-start.1) | copy-done | bytes 524312
  27.7 0.0 collective-permute-done.3.mine_ref
  27.7 0.0 collective-permute-done.4.other_ref
  27.7 0.9 %collective-permute-start.5 = (bf16[528,256]{1,0:T(8,128)(2,1)S(1)}, bf16[528,256]{1,0:T(8,128)(2,1)S(1)}, u32[]{:S(2)}, u32[]{:S(2)}) collective-permute-start(bf16[528,256]{1,0:T(8,128)(2,1)S(1)} %join.3.refs_3_.refs_4_.refs_1_), channel_id=1, source_target_pairs={{0,96},{32,0},{64,32},{96,64},{128,224},{160,128},{192,160},{224,1... | collective-permute-start | bytes 811016 | tf_op jit(solution)/shard_map/ppermute | solution.py:440
  28.6 2.4 %collective-permute-start.1 = (bf16[528,256]{1,0:T(8,128)(2,1)S(1)}, bf16[528,256]{1,0:T(8,128)(2,1)S(1)}, u32[]{:S(2)}, u32[]{:S(2)}) collective-permute-start(bf16[528,256]{1,0:T(8,128)(2,1)S(1)} %join.2.after_ref.refs_2_.refs_0_), channel_id=1, source_target_pairs={{0,32},{32,64},{64,96},{96,0},{128,160},{160,192},{192,224},{224,1... | collective-permute-start | bytes 811016 | tf_op jit(solution)/shard_map/ppermute | solution.py:440
  31.1 0.0 collective-permute-start.8
  31.1 1.2 %collective-permute-done.10.b_ref = bf16[64,2048]{1,0:T(8,128)(2,1)S(1)} collective-permute-done((bf16[64,2048]{1,0:T(8,128)(2,1)}, bf16[64,2048]{1,0:T(8,128)(2,1)S(1)}, u32[]{:S(2)}, u32[]{:S(2)}) %collective-permute-start.10) | collective-permute-done | bytes 262176 | tf_op jit(solution)/shard_map/ppermute | solution.py:444
  32.3 0.8 %collective-permute-start.7 = (bf16[528,256]{1,0:T(8,128)(2,1)S(1)}, bf16[528,256]{1,0:T(8,128)(2,1)S(1)}, u32[]{:S(2)}, u32[]{:S(2)}) collective-permute-start(bf16[528,256]{1,0:T(8,128)(2,1)S(1)} %join.2.after_ref.refs_2_.refs_0_), channel_id=1, source_target_pairs={{0,96},{32,0},{64,32},{96,64},{128,224},{160,128},{192,160},{224,1... | collective-permute-start | bytes 811016 | tf_op jit(solution)/shard_map/ppermute | solution.py:440
  33.2 0.0 collective-permute-done.11.c_ref
  33.2 2.1 %collective-permute-start.9 = (bf16[64,2048]{1,0:T(8,128)(2,1)}, bf16[64,2048]{1,0:T(8,128)(2,1)S(1)}, u32[]{:S(2)}, u32[]{:S(2)}) collective-permute-start(bf16[64,2048]{1,0:T(8,128)(2,1)} %get-tuple-element.20), channel_id=1, source_target_pairs={{0,8},{1,9},{2,10},{3,11},{4,12},{5,13},{6,14},{7,15},{8,0},{9,1},... | collective-permute-start | bytes 786440 | tf_op jit(solution)/shard_map/ppermute | solution.py:444
  35.3 2.7 %collective-permute-done.5.refs_5_ = bf16[528,256]{1,0:T(8,128)(2,1)S(1)} collective-permute-done((bf16[528,256]{1,0:T(8,128)(2,1)S(1)}, bf16[528,256]{1,0:T(8,128)(2,1)S(1)}, u32[]{:S(2)}, u32[]{:S(2)}) %collective-permute-start.5) | collective-permute-done | bytes 270368 | tf_op jit(solution)/shard_map/ppermute | solution.py:440
  37.9 0.0 collective-permute-start.6
  37.9 0.1 collective-permute-done.1.refs_2_
  38.1 3.6 %collective-permute-start.2 = (bf16[528,256]{1,0:T(8,128)(2,1)S(1)}, bf16[528,256]{1,0:T(8,128)(2,1)S(1)}, u32[]{:S(2)}, u32[]{:S(2)}) collective-permute-start(bf16[528,256]{1,0:T(8,128)(2,1)S(1)} %collective-permute-done.1.refs_2_), channel_id=1, source_target_pairs={{0,32},{32,64},{64,96},{96,0},{128,160},{160,192},{192,224},{224,1... | collective-permute-start | bytes 811016 | tf_op jit(solution)/shard_map/ppermute | solution.py:440
  41.7 0.0 copy-done
  41.7 0.0 copy-done.8
  41.7 3.2 %attend.3 = (f32[1024,128]{1,0:T(8,128)S(1)}, f32[1024,256]{1,0:T(8,128)S(1)}) custom-call(s32[2]{0:T(128)S(1)} %copy-done.8, bf16[1,256,512]{2,1,0:T(8,128)(2,1)S(1)} %copy-done, bf16[528,256]{1,0:T(8,128)(2,1)S(1)} %join.2.after_ref.refs_2_.refs_0_, bf16[528,256]{1,0:T(8,128)(2,1)S(1)} %join.3.refs_3_.refs_4_.refs_1_, ...), custom_call_target="tpu_custom_call" | custom-call | flops 1024 | bytes 1024 | tf_op jit(solution)/shard_map/attend/pallas_call | solution.py:181
  44.9 0.0 collective-permute-done.9.a_ref
  44.9 0.0 copy-start.2
  44.9 1.0 %copy-done.2 = f32[64,2048]{1,0:T(8,128)S(1)} copy-done((f32[64,2048]{1,0:T(8,128)S(1)}, f32[64,2048]{1,0:T(8,128)}, u32[]{:S(2)}) %copy-start.2) | copy-done | bytes 524312
  46.0 0.1 quarters.1
  46.1 1.6 %collective-permute-start.12 = (f32[64,512]{1,0:T(8,128)S(1)}, f32[64,512]{1,0:T(8,128)S(1)}, u32[]{:S(2)}, u32[]{:S(2)}) collective-permute-start(f32[64,512]{1,0:T(8,128)S(1)} %get-tuple-element.25), channel_id=1, source_target_pairs={{0,2},{1,3},{2,0},{3,1},{4,6},{5,7},{6,4},{7,5},{8,10},{9,11},{10,... | collective-permute-start | bytes 393224 | tf_op jit(solution)/shard_map/ppermute | solution.py:448
  47.7 0.0 collective-permute-done.8.refs_4_
  47.7 1.9 %collective-permute-start.13 = (f32[64,512]{1,0:T(8,128)S(1)}, f32[64,512]{1,0:T(8,128)S(1)}, u32[]{:S(2)}, u32[]{:S(2)}) collective-permute-start(f32[64,512]{1,0:T(8,128)S(1)} %get-tuple-element.26), channel_id=1, source_target_pairs={{0,1},{1,2},{2,3},{3,0},{4,5},{5,6},{6,7},{7,4},{8,9},{9,10},{10,1... | collective-permute-start | bytes 393224 | tf_op jit(solution)/shard_map/ppermute | solution.py:448
  49.6 0.0 collective-permute-done.7.refs_3_
  49.7 1.9 %collective-permute-start.14 = (f32[64,512]{1,0:T(8,128)S(1)}, f32[64,512]{1,0:T(8,128)S(1)}, u32[]{:S(2)}, u32[]{:S(2)}) collective-permute-start(f32[64,512]{1,0:T(8,128)S(1)} %get-tuple-element.27), channel_id=1, source_target_pairs={{0,3},{1,0},{2,1},{3,2},{4,7},{5,4},{6,5},{7,6},{8,11},{9,8},{10,9... | collective-permute-start | bytes 393224 | tf_op jit(solution)/shard_map/ppermute | solution.py:448
  51.6 6.7 %attend.4 = (f32[1024,128]{1,0:T(8,128)S(1)}, f32[1024,256]{1,0:T(8,128)S(1)}) custom-call(s32[2]{0:T(128)S(1)} %copy-done.8, bf16[1,256,512]{2,1,0:T(8,128)(2,1)S(1)} %copy-done, bf16[528,256]{1,0:T(8,128)(2,1)S(1)} %collective-permute-done.1.refs_2_, bf16[528,256]{1,0:T(8,128)(2,1)S(1)} %collective-permute-done.7.refs_3_, ...), custom_call_target="tpu_custom_call" | custom-call | flops 1024 | bytes 1024 | tf_op jit(solution)/shard_map/attend/pallas_call | solution.py:181
  58.3 0.0 collective-permute-done.12.a_ref
  58.3 0.0 collective-permute-done.13.b_ref
  58.3 0.0 collective-permute-done.14.c_ref
  58.3 0.0 copy-done.5
  58.4 0.8 %hidden.1 = (f32[64,512]{1,0:T(8,128)S(1)}, f32[16,8,128]{2,1,0:T(8,128)}) custom-call(bf16[1,4,16,512]{3,2,1,0:T(8,128)(2,1)S(1)} %copy-done.5, f32[64,512]{1,0:T(8,128)S(1)} %get-tuple-element.24.refs_6_.own_ref, f32[64,512]{1,0:T(8,128)S(1)} %collective-permute-done.12.a_ref, f32[64,512]{1,0:T(8,128)S(1)} %collective-permute-done.13.b_ref, ...), custom_call_target="tpu_custom_call" | custom-call | flops 1024 | bytes 1024 | tf_op jit(solution)/shard_map/hidden/pallas_call | solution.py:405
  59.1 0.0 collective-permute-done.6.refs_7_.refs_3_
  59.1 0.0 collective-permute-done.2.refs_6_.refs_2_
  59.1 0.5 pages.1
  59.6 0.1 collective-permute-start.15
  59.7 3.9 %all-to-all-start = ((f32[16,8,128]{2,1,0:T(8,128)}), f32[16,8,128]{2,1,0:T(8,128)S(1)}, u32[]{:S(2)}, u32[]{:S(2)}) async-start(f32[16,8,128]{2,1,0:T(8,128)} %get-tuple-element.34), calls=%async_computation | async-start | bytes 131072 | tf_op jit(solution)/shard_map/all_to_all | solution.py:507
  63.6 4.4 %attend.5.after_ref = bf16[1,256,512]{2,1,0:T(8,128)(2,1)} custom-call(s32[2]{0:T(128)S(1)} %copy-done.8, bf16[1,256,512]{2,1,0:T(8,128)(2,1)S(1)} %copy-done, bf16[528,256]{1,0:T(8,128)(2,1)S(1)} %collective-permute-done.2.refs_6_.refs_2_, bf16[528,256]{1,0:T(8,128)(2,1)S(1)} %collective-permute-done.6.refs_7_.refs_3_, ...), custom_call_target="tpu_custom_call" | custom-call | flops 1024 | bytes 1024 | tf_op jit(solution)/shard_map/attend/pallas_call | solution.py:181
  68.0 0.0 collective-permute-done.15.came_ref
  68.0 0.9 %copy-done.3 = bf16[1,256,512]{2,1,0:T(8,128)(2,1)S(1)} copy-done((bf16[1,256,512]{2,1,0:T(8,128)(2,1)S(1)}, bf16[1,256,512]{2,1,0:T(8,128)(2,1)}, u32[]{:S(2)}) %copy-start.3) | copy-done | bytes 262168
  68.9 0.7 pool.1
  69.7 2.0 %all-to-all-done.square_ref = f32[16,8,128]{2,1,0:T(8,128)S(1)} async-done(((f32[16,8,128]{2,1,0:T(8,128)}), f32[16,8,128]{2,1,0:T(8,128)S(1)}, u32[]{:S(2)}, u32[]{:S(2)}) %all-to-all-start) | async-done | bytes 65568 | tf_op jit(solution)/shard_map/all_to_all | solution.py:507
  71.7 0.0 copy-done.9
  71.7 0.9 %copy-done.4 = bf16[8,2,2,2,16,128]{5,4,3,2,1,0:T(8,128)(2,1)S(1)} copy-done((bf16[8,2,2,2,16,128]{5,4,3,2,1,0:T(8,128)(2,1)S(1)}, bf16[8,2,2,2,16,128]{5,4,3,2,1,0:T(8,128)(2,1)}, u32[]{:S(2)}) %copy-start.4) | copy-done | bytes 262168
  72.7 0.7 %finish.1 = bf16[1,4,16,512]{3,2,1,0:T(8,128)(2,1)} custom-call(f32[64,512]{1,0:T(8,128)S(1)} %get-tuple-element.30.refs_8_.hidden_ref, bf16[512]{0:T(512)(128)(2,1)S(1)} %copy-done.9, f32[16,8,128]{2,1,0:T(8,128)S(1)} %all-to-all-done.square_ref, bf16[1,32,2,16,128]{4,3,2,1,0:T(8,128)(2,1)S(1)} %bitcast.7), custom_call_target="tpu_custom_call" | custom-call | flops 1024 | bytes 1024 | tf_op jit(solution)/shard_map/finish/pallas_call | solution.py:428
  (4 shorter events, 0.1 us)
Async XLA Ops:
  0.6 41.1 %copy-start = (bf16[1,256,512]{2,1,0:T(8,128)(2,1)S(1)}, bf16[1,256,512]{2,1,0:T(8,128)(2,1)}, u32[]{:S(2)}) copy-start(bf16[1,256,512]{2,1,0:T(8,128)(2,1)} %refs_1_.5) | copy-start | bytes 786436
  0.6 0.9 %copy-start.6 = (bf16[1,2,256,64]{2,3,1,0:T(8,128)(2,1)S(1)}, bf16[1,2,256,64]{2,3,1,0:T(8,128)(2,1)}, u32[]{:S(2)}) copy-start(bf16[1,2,256,64]{2,3,1,0:T(8,128)(2,1)} %param.13) | copy-start | bytes 196612
  1.5 0.8 %copy-start.7 = (bf16[1,2,256,64]{2,3,1,0:T(8,128)(2,1)S(1)}, bf16[1,2,256,64]{2,3,1,0:T(8,128)(2,1)}, u32[]{:S(2)}) copy-start(bf16[1,2,256,64]{2,3,1,0:T(8,128)(2,1)} %param.14) | copy-start | bytes 196612
  2.4 0.7 copy-start.10
  3.0 38.7 %copy-start.8 = (s32[2]{0:T(128)S(1)}, s32[2]{0:T(128)}, u32[]{:S(2)}) copy-start(s32[2]{0:T(128)} %refs_0_.5) | copy-start | bytes 28
  3.7 22.9 %collective-permute-start = (bf16[272,256]{1,0:T(8,128)(2,1)S(1)}, bf16[272,256]{1,0:T(8,128)(2,1)S(1)}, u32[]{:S(2)}, u32[]{:S(2)}) collective-permute-start(bf16[272,256]{1,0:T(8,128)(2,1)S(1)} %pack.1.mine_ref), channel_id=1, source_target_pairs={{0,1},{1,0},{2,3},{3,2},{4,5},{5,4},{6,7},{7,6},{8,9},{9,8},{10,11... | collective-permute-start | bytes 417800 | tf_op jit(solution)/shard_map/ppermute | solution.py:470
  5.7 22.0 %collective-permute-start.3 = (bf16[272,256]{1,0:T(8,128)(2,1)S(1)}, bf16[272,256]{1,0:T(8,128)(2,1)S(1)}, u32[]{:S(2)}, u32[]{:S(2)}) collective-permute-start(bf16[272,256]{1,0:T(8,128)(2,1)S(1)} %pack.1.mine_ref), channel_id=1, source_target_pairs={{0,128},{32,160},{64,192},{96,224},{128,0},{160,32},{192,64},{224,... | collective-permute-start | bytes 417800 | tf_op jit(solution)/shard_map/ppermute | solution.py:471
  12.0 15.7 %collective-permute-start.4 = (bf16[272,256]{1,0:T(8,128)(2,1)S(1)}, bf16[272,256]{1,0:T(8,128)(2,1)S(1)}, u32[]{:S(2)}, u32[]{:S(2)}) collective-permute-start(bf16[272,256]{1,0:T(8,128)(2,1)S(1)} %pack.1.mine_ref), channel_id=1, source_target_pairs={{0,129},{1,128},{2,131},{3,130},{4,133},{5,132},{6,135},{7,134},{8... | collective-permute-start | bytes 417800 | tf_op jit(solution)/shard_map/ppermute | solution.py:472
  12.0 46.3 %copy-start.5 = (bf16[1,4,16,512]{3,2,1,0:T(8,128)(2,1)S(1)}, bf16[1,4,16,512]{3,2,1,0:T(8,128)(2,1)}, u32[]{:S(2)}) copy-start(bf16[1,4,16,512]{3,2,1,0:T(8,128)(2,1)} %residual_ref.1) | copy-start | bytes 196612
  23.3 48.4 %copy-start.9 = (bf16[512]{0:T(512)(128)(2,1)S(1)}, bf16[512]{0:T(512)(128)(2,1)}, u32[]{:S(2)}) copy-start(bf16[512]{0:T(512)(128)(2,1)} %gain_ref.1) | copy-start | bytes 3076
  23.3 9.0 %collective-permute-start.10 = (bf16[64,2048]{1,0:T(8,128)(2,1)}, bf16[64,2048]{1,0:T(8,128)(2,1)S(1)}, u32[]{:S(2)}, u32[]{:S(2)}) collective-permute-start(bf16[64,2048]{1,0:T(8,128)(2,1)} %get-tuple-element.21), channel_id=1, source_target_pairs={{0,4},{1,5},{2,6},{3,7},{4,8},{5,9},{6,10},{7,11},{8,12},{9,13},{1... | collective-permute-start | bytes 786440 | tf_op jit(solution)/shard_map/ppermute | solution.py:444
  24.9 8.2 %collective-permute-start.11 = (bf16[64,2048]{1,0:T(8,128)(2,1)}, bf16[64,2048]{1,0:T(8,128)(2,1)S(1)}, u32[]{:S(2)}, u32[]{:S(2)}) collective-permute-start(bf16[64,2048]{1,0:T(8,128)(2,1)} %get-tuple-element.22), channel_id=1, source_target_pairs={{0,12},{1,13},{2,14},{3,15},{4,0},{5,1},{6,2},{7,3},{8,4},{9,5},{1... | collective-permute-start | bytes 786440 | tf_op jit(solution)/shard_map/ppermute | solution.py:444
  26.6 1.0 %copy-start.1 = (f32[64,2048]{1,0:T(8,128)S(1)}, f32[64,2048]{1,0:T(8,128)}, u32[]{:S(2)}) copy-start(f32[64,2048]{1,0:T(8,128)} %get-tuple-element.19.after_ref.own_ref) | copy-start | bytes 1572868
  27.7 10.2 %collective-permute-start.5 = (bf16[528,256]{1,0:T(8,128)(2,1)S(1)}, bf16[528,256]{1,0:T(8,128)(2,1)S(1)}, u32[]{:S(2)}, u32[]{:S(2)}) collective-permute-start(bf16[528,256]{1,0:T(8,128)(2,1)S(1)} %join.3.refs_3_.refs_4_.refs_1_), channel_id=1, source_target_pairs={{0,96},{32,0},{64,32},{96,64},{128,224},{160,128},{192,160},{224,1... | collective-permute-start | bytes 811016 | tf_op jit(solution)/shard_map/ppermute | solution.py:440
  28.6 9.4 %collective-permute-start.1 = (bf16[528,256]{1,0:T(8,128)(2,1)S(1)}, bf16[528,256]{1,0:T(8,128)(2,1)S(1)}, u32[]{:S(2)}, u32[]{:S(2)}) collective-permute-start(bf16[528,256]{1,0:T(8,128)(2,1)S(1)} %join.2.after_ref.refs_2_.refs_0_), channel_id=1, source_target_pairs={{0,32},{32,64},{64,96},{96,0},{128,160},{160,192},{192,224},{224,1... | collective-permute-start | bytes 811016 | tf_op jit(solution)/shard_map/ppermute | solution.py:440
  31.1 16.7 %collective-permute-start.8 = (bf16[528,256]{1,0:T(8,128)(2,1)S(1)}, bf16[528,256]{1,0:T(8,128)(2,1)S(1)}, u32[]{:S(2)}, u32[]{:S(2)}) collective-permute-start(bf16[528,256]{1,0:T(8,128)(2,1)S(1)} %join.3.refs_3_.refs_4_.refs_1_), channel_id=1, source_target_pairs={{0,32},{32,64},{64,96},{96,0},{128,160},{160,192},{192,224},{224,1... | collective-permute-start | bytes 811016 | tf_op jit(solution)/shard_map/ppermute | solution.py:440
  32.3 17.3 %collective-permute-start.7 = (bf16[528,256]{1,0:T(8,128)(2,1)S(1)}, bf16[528,256]{1,0:T(8,128)(2,1)S(1)}, u32[]{:S(2)}, u32[]{:S(2)}) collective-permute-start(bf16[528,256]{1,0:T(8,128)(2,1)S(1)} %join.2.after_ref.refs_2_.refs_0_), channel_id=1, source_target_pairs={{0,96},{32,0},{64,32},{96,64},{128,224},{160,128},{192,160},{224,1... | collective-permute-start | bytes 811016 | tf_op jit(solution)/shard_map/ppermute | solution.py:440
  33.2 11.7 %collective-permute-start.9 = (bf16[64,2048]{1,0:T(8,128)(2,1)}, bf16[64,2048]{1,0:T(8,128)(2,1)S(1)}, u32[]{:S(2)}, u32[]{:S(2)}) collective-permute-start(bf16[64,2048]{1,0:T(8,128)(2,1)} %get-tuple-element.20), channel_id=1, source_target_pairs={{0,8},{1,9},{2,10},{3,11},{4,12},{5,13},{6,14},{7,15},{8,0},{9,1},... | collective-permute-start | bytes 786440 | tf_op jit(solution)/shard_map/ppermute | solution.py:444
  37.9 21.2 %collective-permute-start.6 = (bf16[528,256]{1,0:T(8,128)(2,1)S(1)}, bf16[528,256]{1,0:T(8,128)(2,1)S(1)}, u32[]{:S(2)}, u32[]{:S(2)}) collective-permute-start(bf16[528,256]{1,0:T(8,128)(2,1)S(1)} %collective-permute-done.5.refs_5_), channel_id=1, source_target_pairs={{0,96},{32,0},{64,32},{96,64},{128,224},{160,128},{192,160},{224,1... | collective-permute-start | bytes 811016 | tf_op jit(solution)/shard_map/ppermute | solution.py:440
  38.1 21.1 %collective-permute-start.2 = (bf16[528,256]{1,0:T(8,128)(2,1)S(1)}, bf16[528,256]{1,0:T(8,128)(2,1)S(1)}, u32[]{:S(2)}, u32[]{:S(2)}) collective-permute-start(bf16[528,256]{1,0:T(8,128)(2,1)S(1)} %collective-permute-done.1.refs_2_), channel_id=1, source_target_pairs={{0,32},{32,64},{64,96},{96,0},{128,160},{160,192},{192,224},{224,1... | collective-permute-start | bytes 811016 | tf_op jit(solution)/shard_map/ppermute | solution.py:440
  44.9 1.0 %copy-start.2 = (f32[64,2048]{1,0:T(8,128)S(1)}, f32[64,2048]{1,0:T(8,128)}, u32[]{:S(2)}) copy-start(f32[64,2048]{1,0:T(8,128)} %get-tuple-element.19.after_ref.own_ref) | copy-start | bytes 1572868
  46.1 12.2 %collective-permute-start.12 = (f32[64,512]{1,0:T(8,128)S(1)}, f32[64,512]{1,0:T(8,128)S(1)}, u32[]{:S(2)}, u32[]{:S(2)}) collective-permute-start(f32[64,512]{1,0:T(8,128)S(1)} %get-tuple-element.25), channel_id=1, source_target_pairs={{0,2},{1,3},{2,0},{3,1},{4,6},{5,7},{6,4},{7,5},{8,10},{9,11},{10,... | collective-permute-start | bytes 393224 | tf_op jit(solution)/shard_map/ppermute | solution.py:448
  47.7 10.6 %collective-permute-start.13 = (f32[64,512]{1,0:T(8,128)S(1)}, f32[64,512]{1,0:T(8,128)S(1)}, u32[]{:S(2)}, u32[]{:S(2)}) collective-permute-start(f32[64,512]{1,0:T(8,128)S(1)} %get-tuple-element.26), channel_id=1, source_target_pairs={{0,1},{1,2},{2,3},{3,0},{4,5},{5,6},{6,7},{7,4},{8,9},{9,10},{10,1... | collective-permute-start | bytes 393224 | tf_op jit(solution)/shard_map/ppermute | solution.py:448
  49.7 8.7 %collective-permute-start.14 = (f32[64,512]{1,0:T(8,128)S(1)}, f32[64,512]{1,0:T(8,128)S(1)}, u32[]{:S(2)}, u32[]{:S(2)}) collective-permute-start(f32[64,512]{1,0:T(8,128)S(1)} %get-tuple-element.27), channel_id=1, source_target_pairs={{0,3},{1,0},{2,1},{3,2},{4,7},{5,4},{6,5},{7,6},{8,11},{9,8},{10,9... | collective-permute-start | bytes 393224 | tf_op jit(solution)/shard_map/ppermute | solution.py:448
  59.6 8.4 %collective-permute-start.15 = (bf16[8,2,2,16,128]{4,3,2,1,0:T(8,128)(2,1)S(1)}, bf16[8,2,2,16,128]{4,3,2,1,0:T(8,128)(2,1)S(1)}, u32[]{:S(2)}, u32[]{:S(2)}) collective-permute-start(bf16[8,2,2,16,128]{4,3,2,1,0:T(8,128)(2,1)S(1)} %get-tuple-element.33), channel_id=1, source_target_pairs={{0,16},{16,0},{1,17},{17,1},{2,18},{18,2},{3,19},{19,3},{4,20},{20... | collective-permute-start | bytes 393224 | tf_op jit(solution)/shard_map/ppermute | solution.py:511
  59.7 12.0 %all-to-all-start = ((f32[16,8,128]{2,1,0:T(8,128)}), f32[16,8,128]{2,1,0:T(8,128)S(1)}, u32[]{:S(2)}, u32[]{:S(2)}) async-start(f32[16,8,128]{2,1,0:T(8,128)} %get-tuple-element.34), calls=%async_computation | async-start | bytes 131072 | tf_op jit(solution)/shard_map/all_to_all | solution.py:507
  68.0 1.0 %copy-start.3 = (bf16[1,256,512]{2,1,0:T(8,128)(2,1)S(1)}, bf16[1,256,512]{2,1,0:T(8,128)(2,1)}, u32[]{:S(2)}) copy-start(bf16[1,256,512]{2,1,0:T(8,128)(2,1)} %attend.5.after_ref) | copy-start | bytes 786436
  71.7 1.0 %copy-start.4 = (bf16[8,2,2,2,16,128]{5,4,3,2,1,0:T(8,128)(2,1)S(1)}, bf16[8,2,2,2,16,128]{5,4,3,2,1,0:T(8,128)(2,1)}, u32[]{:S(2)}) copy-start(bf16[8,2,2,2,16,128]{5,4,3,2,1,0:T(8,128)(2,1)} %pool.1) | copy-start | bytes 786436

commit v3 on v2

v3 whole, which is shorter than its diff:
```python
import functools
import math

import jax
import jax.numpy as jnp
from jax import lax
from jax.experimental import pallas as pl
from jax.experimental.pallas import tpu as pltpu
from jax.sharding import PartitionSpec as P

HEAD_SIZE = 128
PAGE_TOKENS = 16
STEPS = 4
ROWS = 16
LEN = 256
HEADS = 4
TOKENS = 256
PAGES = TOKENS // PAGE_TOKENS
HALF = HEAD_SIZE // 2
PACKED = 4 * HALF
CHUNK = 4 * HEAD_SIZE
TAIL = 16
PIECE = CHUNK + TAIL
COLUMNS = 8192
QUARTER = COLUMNS // 4
SHARE = COLUMNS // 16
LOW_SCORE = -1e30
EPSILON = 1e-05
F32 = jnp.float32
BF16 = jnp.bfloat16
LOG2_SCALE = math.log2(math.e) * HEAD_SIZE**-0.5
VMEM = pltpu.VMEM
SMEM = pltpu.SMEM
MIB = 1024 * 1024
WHOLE = 60.5


def params(mebibytes):
    return pltpu.CompilerParams(vmem_limit_bytes=int(mebibytes * MIB))


def spec(space=VMEM):
    return pl.BlockSpec(memory_space=space)


def shape(dims, dtype):
    return jax.ShapeDtypeStruct(dims, dtype)


def dot_t(a, b):
    return lax.dot_general(a, b, (((1,), (1,)), ((), ())), preferred_element_type=F32)


def dot(a, b):
    return lax.dot_general(a, b, (((1,), (0,)), ((), ())), preferred_element_type=F32)


TOKEN = shape((8, HEAD_SIZE), F32)


def run(kernel, title, mebibytes, token, outs, operands, scratch=(), emit=True, cost=0):
    tokens = [] if token is None else [token]
    count = len(operands) + len(tokens)

    def with_token(*refs):
        results, rest = refs[count : count + len(outs)], refs[count + len(outs) :]
        if emit:
            gone, *rest = rest
            gone[...] = refs[len(operands)][...] if tokens else jnp.zeros(gone.shape, gone.dtype)
        kernel(*refs[: len(operands)], *results, *rest)

    return pl.pallas_call(
        with_token,
        out_shape=(*outs, TOKEN) if emit else tuple(outs),
        in_specs=[spec(space) for _, space in operands] + [spec()] * len(tokens),
        out_specs=(spec(),) * (len(outs) + emit),
        scratch_shapes=list(scratch),
        compiler_params=params(mebibytes),
        cost_estimate=pl.CostEstimate(
            flops=1024 + 1150000000 * cost, bytes_accessed=1024, transcendentals=0
        ),
        name=title,
    )(*[a for a, _ in operands], *tokens)


def pack_kernel(owner_hbm, context_hbm, block_hbm, out_ref, owner_ref, sems):
    copies = [pltpu.make_async_copy(owner_hbm, owner_ref, sems.at[4])]
    for number in range(4):
        source = context_hbm if number < 2 else block_hbm
        copies.append(
            pltpu.make_async_copy(
                source.at[0, number % 2],
                out_ref.at[pl.ds(number * HALF, HALF), :],
                sems.at[number],
            )
        )
    for copy in copies:
        copy.start()
    copies[0].wait()
    owners = [owner_ref[0, p] for p in range(PAGES)]
    page = lax.broadcasted_iota(jnp.int32, (TAIL, TOKENS), 1) // PAGE_TOKENS
    codes = jnp.full((TAIL, TOKENS), -1, jnp.int32)
    for p in range(PAGES):
        rank = jnp.int32(0)
        for q in range(p):
            rank = rank + (owners[q] == owners[p]).astype(jnp.int32)
        codes = jnp.where(page == p, owners[p] * 2 + rank, codes)
    out_ref[PACKED:, :] = codes.astype(F32).astype(BF16)
    for copy in copies[1:]:
        copy.wait()


def pack(page_owner, context_cache, new_block_cache):
    return run(
        pack_kernel,
        "pack",
        WHOLE,
        None,
        [shape((PACKED + TAIL, TOKENS), BF16)],
        [(a, pl.ANY) for a in (page_owner, context_cache, new_block_cache)],
        [pltpu.SMEM((1, PAGES), jnp.int32), pltpu.SemaphoreType.DMA((5,))],
        emit=False,
    )[0]


def join_kernel(mine_ref, near_ref, far_ref, far_near_ref, out_ref):
    odd = lax.axis_index("tp") % 2
    for base, first_ref, second_ref in ((0, mine_ref, near_ref), (PIECE, far_ref, far_near_ref)):
        for number in range(4):
            rows = slice(number * HALF, (number + 1) * HALF)
            here = pl.multiple_of(base + number * HEAD_SIZE + odd * HALF, 16)
            there = pl.multiple_of(base + number * HEAD_SIZE + (1 - odd) * HALF, 16)
            out_ref[pl.ds(here, HALF), :] = first_ref[rows, :]
            out_ref[pl.ds(there, HALF), :] = second_ref[rows, :]
        out_ref[base + CHUNK : base + PIECE, :] = first_ref[PACKED:, :]


def join(mine, near, far, far_near, token):
    outs = [shape((2 * PIECE, TOKENS), BF16)]
    operands = [(a, VMEM) for a in (mine, near, far, far_near)]
    return run(join_kernel, "join", 4, token, outs, operands)


def relay_kernel(up_ref, down_ref, up_out, down_out):
    up_out[...] = up_ref[:PIECE, :]
    down_out[...] = down_ref[PIECE:, :]


def relay(up, down, token):
    outs = [shape((PIECE, TOKENS), BF16)] * 2
    operands = [(up, VMEM), (down, VMEM)]
    return run(relay_kernel, "relay", 4, token, outs, operands, cost=2)


def source_of(flip, turn):
    blk = lax.axis_index("blk")
    return (blk // 4 + flip) % 2 * 4 + (blk % 4 + turn + 4) % 4


def attend_kernel(places, first, last, early, *refs):
    offset_ref, query_ref = refs[:2]
    arrays = 1 + max(place[0] for place in places)
    chunks = refs[2 : 2 + arrays]
    refs = refs[2 + arrays :]
    if not first:
        top_in, sum_in = refs[:2]
        refs = refs[2:]
    refs = refs[early:]
    blk = lax.axis_index("blk")
    offset = offset_ref[lax.axis_index("group")]
    key_number = lax.broadcasted_iota(jnp.int32, (TOKENS, TOKENS), 0)
    query_number = lax.broadcasted_iota(jnp.int32, (TOKENS, TOKENS), 1)
    queries = [
        query_ref[0, :, h * HEAD_SIZE : (h + 1) * HEAD_SIZE].T for h in range(HEADS)
    ]
    ones = jnp.ones((TAIL, TOKENS), BF16)
    groups = []
    for number, base, flip, turn in places:
        source = source_of(flip, turn)
        parts = [
            chunks[number][base + n * HEAD_SIZE : base + (n + 1) * HEAD_SIZE, :] for n in range(4)
        ]
        open_context = jnp.where(source * TOKENS + key_number < offset, 0.0, LOW_SCORE)
        open_block = jnp.where(source <= blk, 0.0, LOW_SCORE)
        groups.append(
            [
                (parts[0].T, jnp.concatenate([parts[1], ones], axis=0), open_context, False),
                (
                    parts[2].T,
                    jnp.concatenate([parts[3], ones], axis=0),
                    open_block,
                    (flip, turn) == (0, 0),
                ),
            ]
        )

    def scores_of(group, head):
        scores = []
        for key, _, bias, diagonal in group:
            score = dot(key, queries[head]) * LOG2_SCALE + bias
            if diagonal:
                score = jnp.where(key_number <= query_number, score, LOW_SCORE)
            scores.append(score)
        return scores

    steps = [(group, head) for group in groups for head in range(HEADS)]
    tops = [jnp.full((1, TOKENS), LOW_SCORE, F32) if first else top_in[h, 0:1] for h in range(HEADS)]
    sums = [None if first else sum_in[h] for h in range(HEADS)]
    ahead = scores_of(*steps[0])
    for number, (group, head) in enumerate(steps):
        scores = ahead
        if number + 1 < len(steps):
            ahead = scores_of(*steps[number + 1])
        top = jnp.maximum(
            tops[head], jnp.max(jnp.maximum(scores[0], scores[1]), axis=0, keepdims=True)
        )
        fresh = None
        for score, (_, value, _, _) in zip(scores, group):
            weight = jnp.exp2(score - top)
            high = weight.astype(BF16)
            low = (weight - high.astype(F32)).astype(BF16)
            part = dot(value, high) + dot(value, low)
            fresh = part if fresh is None else fresh + part
        if sums[head] is not None:
            fresh = sums[head] * jnp.exp2(tops[head] - top) + fresh
        sums[head] = fresh
        tops[head] = top
    for head in range(HEADS):
        if last:
            (out_ref,) = refs
            mixed = sums[head][:HEAD_SIZE] / sums[head][HEAD_SIZE : HEAD_SIZE + 1]
            out_ref[0, :, head * HEAD_SIZE : (head + 1) * HEAD_SIZE] = mixed.T.astype(BF16)
        else:
            top_out, sum_out = refs
            top_out[head] = jnp.broadcast_to(tops[head], (8, TOKENS))
            sum_out[head] = sums[head]


def attend(block_offset, queries, chunks, places, state, last, token, early=()):
    first = state is None
    if last:
        outs = [shape((1, TOKENS, HEADS * HEAD_SIZE), BF16)]
    else:
        outs = [
            shape((HEADS, 8, TOKENS), F32),
            shape((HEADS, HEAD_SIZE + TAIL, TOKENS), F32),
        ]
    operands = [(block_offset, SMEM)]
    operands += [(a, VMEM) for a in (queries, *chunks, *(() if first else state), *early)]
    return run(
        functools.partial(attend_kernel, places, first, last, len(early)),
        "attend",
        24,
        token,
        outs,
        operands,
        cost=3,
    )


def pages_kernel(places, *refs):
    chunks, (mine_ref, other_ref) = refs[:-2], refs[-2:]
    instance = lax.axis_index("blk") * 2 + lax.axis_index("group")
    other = lax.axis_index("blk") * 2 + 1 - lax.axis_index("group")
    slots = 4 * PAGE_TOKENS
    row = lax.broadcasted_iota(jnp.int32, (slots, TOKENS), 0)
    lane = lax.broadcasted_iota(jnp.int32, (slots, TOKENS), 1)
    wanted = jnp.where(row < 2 * PAGE_TOKENS, instance * 2, other * 2) + row // PAGE_TOKENS % 2
    wanted = jnp.where(row % PAGE_TOKENS == lane % PAGE_TOKENS, wanted, -2).astype(F32)
    for number, base, flip, turn in places:
        source = source_of(flip, turn)
        chunk = chunks[number]
        codes = chunk[base + CHUNK : base + PIECE, :].astype(F32)[0:1]
        chooser = jnp.where(wanted == codes, 1.0, 0.0).astype(BF16)
        for part in range(2):
            start = base + (2 + part) * HEAD_SIZE
            found = dot_t(chooser, chunk[start : start + HEAD_SIZE, :]).astype(BF16)
            for rank in range(2):
                mine_ref[source, rank, part] = found[rank * PAGE_TOKENS : (rank + 1) * PAGE_TOKENS]
                other_ref[source, rank, part] = found[
                    (2 + rank) * PAGE_TOKENS : (3 + rank) * PAGE_TOKENS
                ]


def select_pages(chunks, places, token):
    out = shape((8, 2, 2, PAGE_TOKENS, HEAD_SIZE), BF16)
    return run(
        functools.partial(pages_kernel, places),
        "pages",
        8,
        token,
        [out, out],
        [(a, VMEM) for a in chunks],
    )


def pool_kernel(mine_ref, came_ref, out_ref):
    group = lax.axis_index("group")
    out_ref[:, group] = mine_ref[...]
    out_ref[:, 1 - group] = came_ref[...]


def pool(mine, came, token):
    out = shape((8, 2, 2, 2, PAGE_TOKENS, HEAD_SIZE), BF16)
    return run(pool_kernel, "pool", 4, token, [out], [(mine, VMEM), (came, VMEM)])


def attend_rows(
    length_ref, query_ref, step_ref, cache_ref, attended_ref, score_ref, mixed_ref, waits
):
    count = HEADS * STEPS * ROWS
    query = jnp.concatenate(
        [
            query_ref[0, :, :, h * HEAD_SIZE : (h + 1) * HEAD_SIZE].reshape(STEPS * ROWS, HEAD_SIZE)
            for h in range(HEADS)
        ],
        axis=0,
    )
    scaling = HEAD_SIZE**-0.5

    def row_of(width):
        return lax.broadcasted_iota(jnp.int32, (count, width), 0) % ROWS

    row_wide, row_head = row_of(LEN), row_of(HEAD_SIZE)
    lengths = jnp.zeros((count, LEN), jnp.int32)
    for r in range(ROWS):
        if r % (ROWS // 2) == 0:
            waits[r // (ROWS // 2)].wait()
        score = dot_t(query, cache_ref[0, 0, r])
        if r == 0:
            score_ref[...] = score
        else:
            score_ref[...] = jnp.where(row_wide == r, score, score_ref[...])
        lengths = jnp.where(row_wide == r, length_ref[0, r], lengths)
    live = lax.broadcasted_iota(jnp.int32, (count, LEN), 1) < lengths
    score_old = jnp.where(live, score_ref[...] * scaling, LOW_SCORE)
    new_keys = step_ref[0, :, 0].reshape(STEPS * ROWS, HEAD_SIZE)
    new_values = step_ref[0, :, 1].reshape(STEPS * ROWS, HEAD_SIZE)
    lane = lax.broadcasted_iota(jnp.int32, (count, STEPS * ROWS), 1)
    place = lax.broadcasted_iota(jnp.int32, (count, STEPS * ROWS), 0)
    open_new = (lane % ROWS == place % ROWS) & (lane // ROWS <= place // ROWS % STEPS)
    score_new = jnp.where(open_new, dot_t(query, new_keys) * scaling, LOW_SCORE)
    top = jnp.maximum(
        jnp.max(score_old, axis=1, keepdims=True), jnp.max(score_new, axis=1, keepdims=True)
    )
    weight_old = jnp.where(live, jnp.exp(score_old - top), 0.0)
    weight_new = jnp.where(open_new, jnp.exp(score_new - top), 0.0)
    totals = jnp.sum(weight_old, axis=1, keepdims=True) + jnp.sum(weight_new, axis=1, keepdims=True)
    rounded = weight_old.astype(BF16)
    for r in range(ROWS):
        if r % (ROWS // 2) == 0:
            waits[2 + r // (ROWS // 2)].wait()
        mixed = dot(rounded, cache_ref[0, 1, r])
        if r == 0:
            mixed_ref[...] = mixed
        else:
            mixed_ref[...] = jnp.where(row_head == r, mixed, mixed_ref[...])
    mixed = mixed_ref[...] + dot(weight_new.astype(BF16), new_values)
    attended = (mixed / totals).astype(BF16)
    for h in range(HEADS):
        attended_ref[:, h * HEAD_SIZE : (h + 1) * HEAD_SIZE] = attended[
            h * STEPS * ROWS : (h + 1) * STEPS * ROWS
        ]


TURNS = (2, 1, 3, 0)
SPLIT = 2
WIDTH = QUARTER // SPLIT


def decode_kernel(length_hbm, query_hbm, step_hbm, cache_hbm, weight_hbm, *refs):
    outs = refs[:4]
    length_ref, query_ref, step_ref, cache_ref, weight_ref = refs[4:9]
    attended_ref, score_ref, mixed_ref, row_sems, cache_sems, weight_sems = refs[9:]
    firsts = [
        pltpu.make_async_copy(query_hbm, query_ref, row_sems.at[0]),
        pltpu.make_async_copy(step_hbm, step_ref, row_sems.at[1]),
        pltpu.make_async_copy(length_hbm, length_ref, row_sems.at[2]),
    ]
    waits = []
    for number in range(4):
        rows = pl.ds(number % 2 * (ROWS // 2), ROWS // 2)
        waits.append(
            pltpu.make_async_copy(
                cache_hbm.at[0, number // 2, rows],
                cache_ref.at[0, number // 2, rows],
                cache_sems.at[number],
            )
        )
    y = lax.axis_index("tp") // 4
    copies = []
    for number in range(4 * SPLIT):
        column = (y + TURNS[number // SPLIT]) % 4 * QUARTER + number % SPLIT * WIDTH
        copies.append(
            pltpu.make_async_copy(
                weight_hbm.at[:, pl.ds(pl.multiple_of(column, WIDTH), WIDTH)],
                weight_ref.at[number],
                weight_sems.at[number],
            )
        )
    for copy in firsts + waits + copies:
        copy.start()
    for copy in firsts:
        copy.wait()
    attend_rows(
        length_ref, query_ref, step_ref, cache_ref, attended_ref, score_ref, mixed_ref, waits
    )
    attended = attended_ref[...]
    for number, copy in enumerate(copies):
        copy.wait()
        part = dot(attended, weight_ref[number])
        out = outs[number // SPLIT]
        columns = slice(number % SPLIT * WIDTH, (number % SPLIT + 1) * WIDTH)
        out[:, columns] = part.astype(out.dtype)


def decode(row_lengths, step_query, step_cache, row_cache, out_weight):
    rows = STEPS * ROWS
    operands = (row_lengths, step_query, step_cache, row_cache, out_weight)
    return run(
        decode_kernel,
        "decode",
        WHOLE - 1.95,
        None,
        [shape((rows, QUARTER), BF16 if turn else F32) for turn in TURNS],
        [(a, pl.ANY) for a in operands],
        [
            pltpu.SMEM((1, ROWS), jnp.int32),
            pltpu.VMEM(step_query.shape, BF16),
            pltpu.VMEM(step_cache.shape, BF16),
            pltpu.VMEM(row_cache.shape, BF16),
            pltpu.VMEM((4 * SPLIT, out_weight.shape[0], WIDTH), BF16),
            pltpu.VMEM((rows, HEADS * HEAD_SIZE), BF16),
            pltpu.VMEM((HEADS * rows, LEN), F32),
            pltpu.VMEM((HEADS * rows, HEAD_SIZE), F32),
            pltpu.SemaphoreType.DMA((3,)),
            pltpu.SemaphoreType.DMA((4,)),
            pltpu.SemaphoreType.DMA((4 * SPLIT,)),
        ],
        cost=9,
    )


def quarter_kernel(own_ref, a_ref, b_ref, c_ref, *outs):
    z = lax.axis_index("tp") % 4
    for out, turn in zip(outs, TURNS):
        columns = pl.ds(pl.multiple_of((z + turn) % 4 * SHARE, SHARE), SHARE)
        out[...] = (
            own_ref[:, columns]
            + a_ref[:, columns].astype(F32)
            + b_ref[:, columns].astype(F32)
            + c_ref[:, columns].astype(F32)
        )


def sum_quarters(own, came, token):
    outs = [shape((STEPS * ROWS, SHARE), F32) for _ in TURNS]
    operands = [(a, VMEM) for a in (own, *came)]
    return run(quarter_kernel, "quarters", 4, token, outs, operands, cost=4)


def diagonal():
    rows = lax.broadcasted_iota(jnp.int32, (STEPS * ROWS, HEAD_SIZE), 0)
    return rows == lax.broadcasted_iota(jnp.int32, (STEPS * ROWS, HEAD_SIZE), 1)


def hidden_kernel(residual_ref, own_ref, a_ref, b_ref, c_ref, hidden_ref, square_ref):
    residual = residual_ref[0].reshape(STEPS * ROWS, SHARE).astype(F32)
    hidden = residual + (own_ref[...] + a_ref[...] + b_ref[...] + c_ref[...])
    hidden_ref[...] = hidden
    square = jnp.sum(hidden * hidden, axis=1, keepdims=True)
    square = jnp.sum(jnp.where(diagonal(), square, 0.0), axis=0, keepdims=True)
    square_ref[...] = jnp.broadcast_to(square[None], square_ref.shape)


def sum_shares(residual, own, came, token):
    outs = [shape((STEPS * ROWS, SHARE), F32), shape((16, 8, HEAD_SIZE), F32)]
    operands = [(a, VMEM) for a in (residual, own, *came)]
    return run(hidden_kernel, "hidden", 4, token, outs, operands)


def finish_kernel(hidden_ref, gain_ref, square_ref, out_ref):
    square = jnp.sum(square_ref[...], axis=0)[0:1]
    square = jnp.sum(jnp.where(diagonal(), square, 0.0), axis=1, keepdims=True)
    scale = lax.rsqrt(square * (1.0 / COLUMNS) + EPSILON)
    out = hidden_ref[...] * scale * gain_ref[...].reshape(1, SHARE).astype(F32)
    out_ref[0] = out.astype(BF16).reshape(STEPS, ROWS, SHARE)


def finish(hidden, gain, squares, token):
    outs = [shape((1, STEPS, ROWS, SHARE), BF16)]
    operands = [(a, VMEM) for a in (hidden, gain, squares)]
    return run(finish_kernel, "finish", 4, token, outs, operands)


def move_x(a, turn):
    return lax.ppermute(a, "blk", [(i, i // 4 * 4 + (i + turn) % 4) for i in range(8)])


def move_y(a, turn):
    return lax.ppermute(a, "tp", [(i, (i + 4 * turn) % 16) for i in range(16)])


def move_z(a, turn):
    return lax.ppermute(a, "tp", [(i, i // 4 * 4 + (i + turn) % 4) for i in range(16)])


def body(
    prompt_query,
    context_cache,
    new_block_cache,
    block_offset,
    page_owner,
    step_query,
    step_cache,
    row_cache,
    row_lengths,
    out_weight,
    residual,
    norm_gain,
):
    packed = pack(
        page_owner.reshape(1, PAGES),
        jnp.swapaxes(context_cache, 2, 3),
        jnp.swapaxes(new_block_cache, 2, 3),
    )
    near = lax.ppermute(packed, "tp", [(i, i ^ 1) for i in range(16)])
    far = lax.ppermute(packed, "blk", [(i, i ^ 4) for i in range(8)])
    far_near = lax.ppermute(
        packed,
        ("blk", "tp"),
        [(b * 16 + t, (b ^ 4) * 16 + (t ^ 1)) for b in range(8) for t in range(16)],
    )
    *parts, own, token = decode(row_lengths, step_query, step_cache, row_cache, out_weight)
    came = [move_y(a, turn) for a, turn in zip(parts, TURNS)]
    here, token = join(packed, near, far, far_near, token)
    up = move_x(here, 1)
    down = move_x(here, 3)
    *state, token = attend(
        block_offset,
        prompt_query,
        [here],
        [(0, 0, 0, 0), (0, PIECE, 1, 0)],
        None,
        False,
        token,
        [own],
    )
    *shares, own, token = sum_quarters(own, came, token)
    came = [move_z(a, turn) for a, turn in zip(shares, TURNS)]
    up_two, down_two, token = relay(up, down, token)
    up_two = move_x(up_two, 1)
    down_two = move_x(down_two, 3)
    places = [(0, 0, 0, -1), (0, PIECE, 1, -1), (1, 0, 0, 1), (1, PIECE, 1, 1)]
    *state, token = attend(block_offset, prompt_query, [up, down], places, state, False, token)
    hidden, square, token = sum_shares(residual, own, came, token)
    squares = lax.all_to_all(square, "tp", split_axis=0, concat_axis=0, tiled=True)
    places = [(0, 0, 0, 0), (0, PIECE, 1, 0), (1, 0, 0, -1), (1, PIECE, 1, -1)]
    places += [(2, 0, 0, 1), (2, PIECE, 1, 1), (3, 0, 0, 2), (4, 0, 1, 2)]
    mine, other, token = select_pages([here, up, down, up_two, down_two], places, token)
    other = lax.ppermute(other, "group", [(0, 1), (1, 0)])
    prefill_out, token = attend(
        block_offset,
        prompt_query,
        [up_two, down_two],
        [(0, 0, 0, 2), (1, 0, 1, 2)],
        state,
        True,
        token,
    )
    page_pool, token = pool(mine, other, token)
    decode_out, token = finish(hidden, norm_gain, squares, token)
    return (prefill_out, page_pool.reshape(1, 32, 2, PAGE_TOKENS, HEAD_SIZE), decode_out)


def solution(mesh):
    placed = (
        P("group", "blk", "tp"),
        P("group", None, "blk", "tp"),
        P("group", None, "blk", "tp"),
        P(),
        P("group", "blk", None),
        P(("blk", "group"), None, None, "tp"),
        P(("blk", "group"), None, None, None, "tp"),
        P(("blk", "group"), None, None, None, "tp"),
        P(("blk", "group"), None),
        P("tp", None),
        P(("blk", "group"), None, None, "tp"),
        P("tp"),
    )
    return jax.shard_map(
        body,
        mesh=mesh,
        in_specs=placed,
        out_specs=(
            P("group", "blk", "tp"),
            P(("blk", "group"), None, None, None, "tp"),
            P(("blk", "group"), None, None, "tp"),
        ),
        check_vma=False,
    )
```

time: 74 us -> 64.1 us (0.87)
  Pallas kernels: 29.3 us -> 22.8 us
  local copies, waits for them, and re-layouts: 6.36 us -> 2.82 us
  starting transfers between devices: 30.9 us -> 31.8 us
  waiting for transfers between devices: 6.12 us -> 5.3 us
    pallas_call x12, Pallas kernels: 29.3 us -> 22.8 us  [run(): pl.pallas_call(with_token, out_shape=(*outs, TOKEN) if emit else tuple(ou...]
    ppermute x6 -> x4, starting transfers between devices: 7.8 us -> 4.21 us  [move_x(): lax.ppermute(a, 'blk', [(i, i // 4 * 4 + (i + turn) % 4) for i in range(8)])]
    unnamed x22 -> x20, local copies, waits for them, and re-layouts: 6.36 us -> 2.82 us
    all_to_all x1, starting transfers between devices: 3.86 us -> 7.27 us  [body(): lax.all_to_all(square, 'tp', split_axis=0, concat_axis=0, tiled=True)]
    ppermute x6 -> x4, waiting for transfers between devices: 2.82 us -> 0.57 us  [move_x(): lax.ppermute(a, 'blk', [(i, i // 4 * 4 + (i + turn) % 4) for i in range(8)])]
    ppermute x3, starting transfers between devices: 5.35 us -> 6.52 us  [move_y(): return lax.ppermute(a, 'tp', [(i, (i + 4 * turn) % 16) for i in range(16)])]
    ppermute x3, waiting for transfers between devices: 1.25 us -> 2.37 us  [move_y(): return lax.ppermute(a, 'tp', [(i, (i + 4 * turn) % 16) for i in range(16)])]
  transfers between devices with their start and end apart: 17 -> 15, of which waited for: 4 -> 4; matrix products, arithmetic and copies ran while one was open for 0% -> 0% of each run, Pallas kernels for 37% -> 32%
where the time goes in v3:
time: 64.1 us; the launch traced here: 63.6 us
  starting transfers between devices  31.8 us (50%)
  Pallas kernels  22.8 us (36%)
  waiting for transfers between devices  5.3 us (8%)
  local copies, waits for them, and re-layouts  2.82 us (4%)
  between operations  0.84 us (1%)
    pallas_call x12, Pallas kernels, run(): pl.pallas_call(with_token, out_shape=(*outs, TOKEN) if emit else tuple(ou...  22.8 us
    all_to_all x1, starting transfers between devices, body(): lax.all_to_all(square, 'tp', split_axis=0, concat_axis=0, tiled=True)  7.27 us
    ppermute x3, starting transfers between devices, move_y(): return lax.ppermute(a, 'tp', [(i, (i + 4 * turn) % 16) for i in range(16)])  6.52 us
    ppermute x1, starting transfers between devices, body(): far = lax.ppermute(packed, 'blk', [(i, i ^ 4) for i in range(8)])  6.29 us
    ppermute x3, starting transfers between devices, move_z(): lax.ppermute(a, 'tp', [(i, i // 4 * 4 + (i + turn) % 4) for i in range(16)])  5.46 us
    ppermute x4, starting transfers between devices, move_x(): lax.ppermute(a, 'blk', [(i, i // 4 * 4 + (i + turn) % 4) for i in range(8)])  4.21 us
    unnamed x20, local copies, waits for them, and re-layouts  2.82 us
    ppermute x3, waiting for transfers between devices, move_y(): return lax.ppermute(a, 'tp', [(i, (i + 4 * turn) % 16) for i in range(16)])  2.37 us
  transfers between devices with their start and end apart: 15, of which 4 were waited for; matrix products, arithmetic and copies ran while one was open for 0% of the time, Pallas kernels for 32%

profile of v3, /device:TPU:6, one launch (start us, length us, event | category | flops | bytes accessed | tf_op | source)
XLA Modules:
  0.0 63.6 jit_solution(10190932000323696827)
XLA Ops:
  0.6 1.6 %pack.1.refs_0_ = bf16[272,256]{1,0:T(8,128)(2,1)} custom-call(s32[1,16]{1,0:T(1,128)} %bitcast.6, bf16[1,2,64,256]{3,2,1,0:T(8,128)(2,1)} %bitcast.4, bf16[1,2,64,256]{3,2,1,0:T(8,128)(2,1)} %bitcast.5), custom_call_target="tpu_custom_call" | custom-call | flops 1024 | bytes 1024 | tf_op jit(solution)/shard_map/pack/pallas_call | solution.py:72
  2.2 0.0 copy-start
  2.2 0.0 copy-start.4
  2.2 0.0 copy-start.5
  2.2 2.0 %collective-permute-start = (bf16[272,256]{1,0:T(8,128)(2,1)}, bf16[272,256]{1,0:T(8,128)(2,1)S(1)}, u32[]{:S(2)}, u32[]{:S(2)}) collective-permute-start(bf16[272,256]{1,0:T(8,128)(2,1)} %pack.1.refs_0_), channel_id=1, source_target_pairs={{0,1},{1,0},{2,3},{3,2},{4,5},{5,4},{6,7},{7,6},{8,9},{9,8},{10,11... | collective-permute-start | bytes 417800 | tf_op jit(solution)/shard_map/ppermute | solution.py:527
  4.2 6.3 %collective-permute-start.1 = (bf16[272,256]{1,0:T(8,128)(2,1)}, bf16[272,256]{1,0:T(8,128)(2,1)S(1)}, u32[]{:S(2)}, u32[]{:S(2)}) collective-permute-start(bf16[272,256]{1,0:T(8,128)(2,1)} %pack.1.refs_0_), channel_id=1, source_target_pairs={{0,128},{32,160},{64,192},{96,224},{128,0},{160,32},{192,64},{224,... | collective-permute-start | bytes 417800 | tf_op jit(solution)/shard_map/ppermute | solution.py:528
  10.5 0.0 collective-permute-start.2
  10.5 8.3 %decode.1 = (bf16[64,2048]{1,0:T(8,128)(2,1)}, bf16[64,2048]{1,0:T(8,128)(2,1)}, bf16[64,2048]{1,0:T(8,128)(2,1)}, f32[64,2048]{1,0:T(8,128)}, f32[8,128]{1,0:T(8,128)}) custom-call(s32[1,16]{1,0:T(1,128)} %refs_0_.5, bf16[1,4,16,512]{3,2,1,0:T(8,128)(2,1)} %refs_1_.5, bf16[1,4,2,16,128]{4,3,2,1,0:T(8,128)(2,1)} %refs_2_.1, ...), custom_call_target="tpu_custom_call" | custom-call | flops 10350001152 | bytes 1024 | tf_op jit(solution)/shard_map/decode/pallas_call | solution.py:72
  18.9 3.3 %collective-permute-start.5 = (bf16[64,2048]{1,0:T(8,128)(2,1)}, bf16[64,2048]{1,0:T(8,128)(2,1)S(1)}, u32[]{:S(2)}, u32[]{:S(2)}) collective-permute-start(bf16[64,2048]{1,0:T(8,128)(2,1)} %get-tuple-element.38), channel_id=1, source_target_pairs={{0,8},{1,9},{2,10},{3,11},{4,12},{5,13},{6,14},{7,15},{8,0},{9,1},... | collective-permute-start | bytes 786440 | tf_op jit(solution)/shard_map/ppermute | solution.py:501
  22.2 0.7 %collective-permute-start.6 = (bf16[64,2048]{1,0:T(8,128)(2,1)}, bf16[64,2048]{1,0:T(8,128)(2,1)S(1)}, u32[]{:S(2)}, u32[]{:S(2)}) collective-permute-start(bf16[64,2048]{1,0:T(8,128)(2,1)} %get-tuple-element.39), channel_id=1, source_target_pairs={{0,4},{1,5},{2,6},{3,7},{4,8},{5,9},{6,10},{7,11},{8,12},{9,13},{1... | collective-permute-start | bytes 786440 | tf_op jit(solution)/shard_map/ppermute | solution.py:501
  22.9 0.0 collective-permute-done.refs_1_
  22.9 2.6 %collective-permute-start.7 = (bf16[64,2048]{1,0:T(8,128)(2,1)}, bf16[64,2048]{1,0:T(8,128)(2,1)S(1)}, u32[]{:S(2)}, u32[]{:S(2)}) collective-permute-start(bf16[64,2048]{1,0:T(8,128)(2,1)} %get-tuple-element.40), channel_id=1, source_target_pairs={{0,12},{1,13},{2,14},{3,15},{4,0},{5,1},{6,2},{7,3},{8,4},{9,5},{1... | collective-permute-start | bytes 786440 | tf_op jit(solution)/shard_map/ppermute | solution.py:501
  25.4 0.0 collective-permute-done.1.refs_2_
  25.4 0.0 collective-permute-done.2.refs_3_
  25.4 0.0 copy-done
  25.4 0.0 copy-start.2
  25.4 0.7 %copy-done.2 = f32[8,128]{1,0:T(8,128)S(1)} copy-done((f32[8,128]{1,0:T(8,128)S(1)}, f32[8,128]{1,0:T(8,128)}, u32[]{:S(2)}) %copy-start.2) | copy-done | bytes 4120
  26.1 0.0 copy-start.9
  26.1 0.1 join.1
  26.2 0.6 collective-permute-start.3
  26.7 1.5 %collective-permute-start.4 = (bf16[1056,256]{1,0:T(8,128)(2,1)S(1)}, bf16[1056,256]{1,0:T(8,128)(2,1)S(1)}, u32[]{:S(2)}, u32[]{:S(2)}) collective-permute-start(bf16[1056,256]{1,0:T(8,128)(2,1)S(1)} %get-tuple-element.36.refs_2_.refs_0_), channel_id=1, source_target_pairs={{0,96},{32,0},{64,32},{96,64},{128,224},{160,128},{192,160},{224,1... | collective-permute-start | bytes 1622024 | tf_op jit(solution)/shard_map/ppermute | solution.py:497
  28.3 0.0 copy-done.4
  28.3 0.0 copy-done.5
  28.3 0.0 copy-start.8
  28.3 1.0 %copy-done.8 = f32[64,2048]{1,0:T(8,128)S(1)} copy-done((f32[64,2048]{1,0:T(8,128)S(1)}, f32[64,2048]{1,0:T(8,128)}, u32[]{:S(2)}) %copy-start.8) | copy-done | bytes 524312
  29.3 2.4 %attend.3 = (f32[4,8,256]{2,1,0:T(8,128)S(1)}, f32[4,144,256]{2,1,0:T(8,128)S(1)}, f32[8,128]{1,0:T(8,128)S(1)}) custom-call(s32[2]{0:T(128)S(1)} %copy-done.5, bf16[1,256,512]{2,1,0:T(8,128)(2,1)S(1)} %copy-done.4, bf16[1056,256]{1,0:T(8,128)(2,1)S(1)} %get-tuple-element.36.refs_2_.refs_0_, f32[64,2048]{1,0:T(8,128)S(1)} %copy-done.8, ...), custom_call_target="tpu_custom_call" | custom-call | flops 3450000896 | bytes 1024 | tf_op jit(solution)/shard_map/attend/pallas_call | solution.py:72
  31.8 0.0 collective-permute-done.5.refs_1_
  31.8 2.0 %collective-permute-done.6.refs_2_ = bf16[64,2048]{1,0:T(8,128)(2,1)S(1)} collective-permute-done((bf16[64,2048]{1,0:T(8,128)(2,1)}, bf16[64,2048]{1,0:T(8,128)(2,1)S(1)}, u32[]{:S(2)}, u32[]{:S(2)}) %collective-permute-start.6) | collective-permute-done | bytes 262176 | tf_op jit(solution)/shard_map/ppermute | solution.py:501
  33.8 0.3 collective-permute-done.7.refs_3_
  34.1 0.0 copy-done.9
  34.1 0.1 quarters.1
  34.3 1.6 %collective-permute-start.10 = (f32[64,512]{1,0:T(8,128)S(1)}, f32[64,512]{1,0:T(8,128)S(1)}, u32[]{:S(2)}, u32[]{:S(2)}) collective-permute-start(f32[64,512]{1,0:T(8,128)S(1)} %get-tuple-element.52), channel_id=1, source_target_pairs={{0,2},{1,3},{2,0},{3,1},{4,6},{5,7},{6,4},{7,5},{8,10},{9,11},{10,... | collective-permute-start | bytes 393224 | tf_op jit(solution)/shard_map/ppermute | solution.py:505
  35.9 1.6 %collective-permute-start.11 = (f32[64,512]{1,0:T(8,128)S(1)}, f32[64,512]{1,0:T(8,128)S(1)}, u32[]{:S(2)}, u32[]{:S(2)}) collective-permute-start(f32[64,512]{1,0:T(8,128)S(1)} %get-tuple-element.53), channel_id=1, source_target_pairs={{0,1},{1,2},{2,3},{3,0},{4,5},{5,6},{6,7},{7,4},{8,9},{9,10},{10,1... | collective-permute-start | bytes 393224 | tf_op jit(solution)/shard_map/ppermute | solution.py:505
  37.5 2.2 %collective-permute-start.12 = (f32[64,512]{1,0:T(8,128)S(1)}, f32[64,512]{1,0:T(8,128)S(1)}, u32[]{:S(2)}, u32[]{:S(2)}) collective-permute-start(f32[64,512]{1,0:T(8,128)S(1)} %get-tuple-element.54), channel_id=1, source_target_pairs={{0,3},{1,0},{2,1},{3,2},{4,7},{5,4},{6,5},{7,6},{8,11},{9,8},{10,9... | collective-permute-start | bytes 393224 | tf_op jit(solution)/shard_map/ppermute | solution.py:505
  39.7 0.0 collective-permute-done.3.refs_0_.refs_2_.refs_1_
  39.7 0.6 collective-permute-done.4.refs_1_.refs_3_.refs_2_
  40.3 0.0 copy-start.1
  40.3 0.4 collective-permute-start.8
  40.7 1.7 %collective-permute-start.9 = (bf16[528,256]{1,0:T(8,128)(2,1)S(1)}, bf16[528,256]{1,0:T(8,128)(2,1)S(1)}, u32[]{:S(2)}, u32[]{:S(2)}) collective-permute-start(bf16[528,256]{1,0:T(8,128)(2,1)S(1)} %get-tuple-element.45), channel_id=1, source_target_pairs={{0,96},{32,0},{64,32},{96,64},{128,224},{160,128},{192,160},{224,1... | collective-permute-start | bytes 811016 | tf_op jit(solution)/shard_map/ppermute | solution.py:497
  42.4 4.1 %attend.4 = (f32[4,8,256]{2,1,0:T(8,128)S(1)}, f32[4,144,256]{2,1,0:T(8,128)S(1)}, f32[8,128]{1,0:T(8,128)S(1)}) custom-call(s32[2]{0:T(128)S(1)} %copy-done.5, bf16[1,256,512]{2,1,0:T(8,128)(2,1)S(1)} %copy-done.4, bf16[1056,256]{1,0:T(8,128)(2,1)S(1)} %collective-permute-done.3.refs_0_.refs_2_.refs_1_, ...), custom_call_target="tpu_custom_call" | custom-call | flops 3450000896 | bytes 1024 | tf_op jit(solution)/shard_map/attend/pallas_call | solution.py:72
  46.6 0.0 copy-start.6
  46.6 0.0 copy-start.3
  46.6 0.0 collective-permute-done.10.refs_2_
  46.6 0.0 collective-permute-done.11.refs_3_
  46.6 0.0 collective-permute-done.12.refs_4_
  46.6 0.0 copy-done.1
  46.6 0.8 %hidden.1 = (f32[64,512]{1,0:T(8,128)S(1)}, f32[16,8,128]{2,1,0:T(8,128)}, f32[8,128]{1,0:T(8,128)S(1)}) custom-call(bf16[1,4,16,512]{3,2,1,0:T(8,128)(2,1)S(1)} %copy-done.1, f32[64,512]{1,0:T(8,128)S(1)} %get-tuple-element.51.refs_1_, f32[64,512]{1,0:T(8,128)S(1)} %collective-permute-done.10.refs_2_, f32[64,512]{1,0:T(8,128)S(1)} %collective-permute-done.11.refs_3_, ...), custom_call_target="tpu_custom_call" | custom-call | flops 1024 | bytes 1024 | tf_op jit(solution)/shard_map/hidden/pallas_call | solution.py:72
  47.4 0.0 copy-done.6
  47.4 7.3 %all-to-all-start = ((f32[16,8,128]{2,1,0:T(8,128)}), f32[16,8,128]{2,1,0:T(8,128)S(1)}, u32[]{:S(2)}, u32[]{:S(2)}) async-start(f32[16,8,128]{2,1,0:T(8,128)} %get-tuple-element.64), calls=%async_computation | async-start | bytes 131072 | tf_op jit(solution)/shard_map/all_to_all | solution.py:557
  54.7 0.0 collective-permute-done.8.refs_3_.refs_2_
  54.7 0.0 collective-permute-done.9.refs_4_.refs_3_
  54.7 0.5 pages.1
  55.2 0.1 collective-permute-start.13
  55.3 0.0 copy-start.7
  55.3 1.1 %copy-done.7 = f32[4,144,256]{2,1,0:T(8,128)S(1)} copy-done((f32[4,144,256]{2,1,0:T(8,128)S(1)}, f32[4,144,256]{2,1,0:T(8,128)}, u32[]{:S(2)}) %copy-start.7) | copy-done | bytes 589848
  56.3 3.4 %attend.5 = (bf16[1,256,512]{2,1,0:T(8,128)(2,1)}, f32[8,128]{1,0:T(8,128)S(1)}) custom-call(s32[2]{0:T(128)S(1)} %copy-done.5, bf16[1,256,512]{2,1,0:T(8,128)(2,1)S(1)} %copy-done.4, bf16[528,256]{1,0:T(8,128)(2,1)S(1)} %collective-permute-done.8.refs_3_.refs_2_, bf16[528,256]{1,0:T(8,128)(2,1)S(1)} %collective-permute-done.9.refs_4_.refs_3_, ...), custom_call_target="tpu_custom_call" | custom-call | flops 3450000896 | bytes 1024 | tf_op jit(solution)/shard_map/attend/pallas_call | solution.py:72
  59.7 0.0 collective-permute-done.13.refs_1_
  59.7 0.7 %pool.1 = (bf16[8,2,2,2,16,128]{5,4,3,2,1,0:T(8,128)(2,1)}, f32[8,128]{1,0:T(8,128)S(1)}) custom-call(bf16[8,2,2,16,128]{4,3,2,1,0:T(8,128)(2,1)S(1)} %get-tuple-element.59.refs_0_, bf16[8,2,2,16,128]{4,3,2,1,0:T(8,128)(2,1)S(1)} %collective-permute-done.13.refs_1_, f32[8,128]{1,0:T(8,128)S(1)} %get-tuple-element.61.refs_2_), custom_call_target="tpu_custom_call" | custom-call | flops 1024 | bytes 1024 | tf_op jit(solution)/shard_map/pool/pallas_call | solution.py:72
  60.5 2.3 %all-to-all-done.refs_2_ = f32[16,8,128]{2,1,0:T(8,128)S(1)} async-done(((f32[16,8,128]{2,1,0:T(8,128)}), f32[16,8,128]{2,1,0:T(8,128)S(1)}, u32[]{:S(2)}, u32[]{:S(2)}) %all-to-all-start) | async-done | bytes 65568 | tf_op jit(solution)/shard_map/all_to_all | solution.py:557
  62.8 0.0 copy-done.3
  62.8 0.7 %finish.1 = (bf16[1,4,16,512]{3,2,1,0:T(8,128)(2,1)}, f32[8,128]{1,0:T(8,128)}) custom-call(f32[64,512]{1,0:T(8,128)S(1)} %get-tuple-element.63.refs_0_, bf16[512]{0:T(512)(128)(2,1)S(1)} %copy-done.3, f32[16,8,128]{2,1,0:T(8,128)S(1)} %all-to-all-done.refs_2_, f32[8,128]{1,0:T(8,128)S(1)} %get-tuple-element.65.refs_3_), custom_call_target="tpu_custom_call" | custom-call | flops 1024 | bytes 1024 | tf_op jit(solution)/shard_map/finish/pallas_call | solution.py:72
  (1 shorter events, 0.0 us)
Async XLA Ops:
  2.2 23.2 %copy-start = (bf16[272,256]{1,0:T(8,128)(2,1)S(1)}, bf16[272,256]{1,0:T(8,128)(2,1)}, u32[]{:S(2)}) copy-start(bf16[272,256]{1,0:T(8,128)(2,1)} %pack.1.refs_0_) | copy-start | bytes 417796
  2.2 26.1 %copy-start.4 = (bf16[1,256,512]{2,1,0:T(8,128)(2,1)S(1)}, bf16[1,256,512]{2,1,0:T(8,128)(2,1)}, u32[]{:S(2)}) copy-start(bf16[1,256,512]{2,1,0:T(8,128)(2,1)} %refs_1_.8) | copy-start | bytes 786436
  2.2 26.1 %copy-start.5 = (s32[2]{0:T(128)S(1)}, s32[2]{0:T(128)}, u32[]{:S(2)}) copy-start(s32[2]{0:T(128)} %refs_0_.9) | copy-start | bytes 28
  2.2 20.6 %collective-permute-start = (bf16[272,256]{1,0:T(8,128)(2,1)}, bf16[272,256]{1,0:T(8,128)(2,1)S(1)}, u32[]{:S(2)}, u32[]{:S(2)}) collective-permute-start(bf16[272,256]{1,0:T(8,128)(2,1)} %pack.1.refs_0_), channel_id=1, source_target_pairs={{0,1},{1,0},{2,3},{3,2},{4,5},{5,4},{6,7},{7,6},{8,9},{9,8},{10,11... | collective-permute-start | bytes 417800 | tf_op jit(solution)/shard_map/ppermute | solution.py:527
  4.2 21.2 %collective-permute-start.1 = (bf16[272,256]{1,0:T(8,128)(2,1)}, bf16[272,256]{1,0:T(8,128)(2,1)S(1)}, u32[]{:S(2)}, u32[]{:S(2)}) collective-permute-start(bf16[272,256]{1,0:T(8,128)(2,1)} %pack.1.refs_0_), channel_id=1, source_target_pairs={{0,128},{32,160},{64,192},{96,224},{128,0},{160,32},{192,64},{224,... | collective-permute-start | bytes 417800 | tf_op jit(solution)/shard_map/ppermute | solution.py:528
  10.5 14.9 %collective-permute-start.2 = (bf16[272,256]{1,0:T(8,128)(2,1)}, bf16[272,256]{1,0:T(8,128)(2,1)S(1)}, u32[]{:S(2)}, u32[]{:S(2)}) collective-permute-start(bf16[272,256]{1,0:T(8,128)(2,1)} %pack.1.refs_0_), channel_id=1, source_target_pairs={{0,129},{1,128},{2,131},{3,130},{4,133},{5,132},{6,135},{7,134},{8... | collective-permute-start | bytes 417800 | tf_op jit(solution)/shard_map/ppermute | solution.py:529
  18.9 12.9 %collective-permute-start.5 = (bf16[64,2048]{1,0:T(8,128)(2,1)}, bf16[64,2048]{1,0:T(8,128)(2,1)S(1)}, u32[]{:S(2)}, u32[]{:S(2)}) collective-permute-start(bf16[64,2048]{1,0:T(8,128)(2,1)} %get-tuple-element.38), channel_id=1, source_target_pairs={{0,8},{1,9},{2,10},{3,11},{4,12},{5,13},{6,14},{7,15},{8,0},{9,1},... | collective-permute-start | bytes 786440 | tf_op jit(solution)/shard_map/ppermute | solution.py:501
  22.2 11.6 %collective-permute-start.6 = (bf16[64,2048]{1,0:T(8,128)(2,1)}, bf16[64,2048]{1,0:T(8,128)(2,1)S(1)}, u32[]{:S(2)}, u32[]{:S(2)}) collective-permute-start(bf16[64,2048]{1,0:T(8,128)(2,1)} %get-tuple-element.39), channel_id=1, source_target_pairs={{0,4},{1,5},{2,6},{3,7},{4,8},{5,9},{6,10},{7,11},{8,12},{9,13},{1... | collective-permute-start | bytes 786440 | tf_op jit(solution)/shard_map/ppermute | solution.py:501
  22.9 11.3 %collective-permute-start.7 = (bf16[64,2048]{1,0:T(8,128)(2,1)}, bf16[64,2048]{1,0:T(8,128)(2,1)S(1)}, u32[]{:S(2)}, u32[]{:S(2)}) collective-permute-start(bf16[64,2048]{1,0:T(8,128)(2,1)} %get-tuple-element.40), channel_id=1, source_target_pairs={{0,12},{1,13},{2,14},{3,15},{4,0},{5,1},{6,2},{7,3},{8,4},{9,5},{1... | collective-permute-start | bytes 786440 | tf_op jit(solution)/shard_map/ppermute | solution.py:501
  25.4 0.7 %copy-start.2 = (f32[8,128]{1,0:T(8,128)S(1)}, f32[8,128]{1,0:T(8,128)}, u32[]{:S(2)}) copy-start(f32[8,128]{1,0:T(8,128)} %get-tuple-element.35.refs_4_) | copy-start | bytes 12292
  26.1 8.0 %copy-start.9 = (f32[64,2048]{1,0:T(8,128)S(1)}, f32[64,2048]{1,0:T(8,128)}, u32[]{:S(2)}) copy-start(f32[64,2048]{1,0:T(8,128)} %get-tuple-element.37.refs_3_.refs_0_) | copy-start | bytes 1572868
  26.2 13.5 %collective-permute-start.3 = (bf16[1056,256]{1,0:T(8,128)(2,1)S(1)}, bf16[1056,256]{1,0:T(8,128)(2,1)S(1)}, u32[]{:S(2)}, u32[]{:S(2)}) collective-permute-start(bf16[1056,256]{1,0:T(8,128)(2,1)S(1)} %get-tuple-element.36.refs_2_.refs_0_), channel_id=1, source_target_pairs={{0,32},{32,64},{64,96},{96,0},{128,160},{160,192},{192,224},{224,1... | collective-permute-start | bytes 1622024 | tf_op jit(solution)/shard_map/ppermute | solution.py:497
  26.7 13.5 %collective-permute-start.4 = (bf16[1056,256]{1,0:T(8,128)(2,1)S(1)}, bf16[1056,256]{1,0:T(8,128)(2,1)S(1)}, u32[]{:S(2)}, u32[]{:S(2)}) collective-permute-start(bf16[1056,256]{1,0:T(8,128)(2,1)S(1)} %get-tuple-element.36.refs_2_.refs_0_), channel_id=1, source_target_pairs={{0,96},{32,0},{64,32},{96,64},{128,224},{160,128},{192,160},{224,1... | collective-permute-start | bytes 1622024 | tf_op jit(solution)/shard_map/ppermute | solution.py:497
  28.3 1.0 %copy-start.8 = (f32[64,2048]{1,0:T(8,128)S(1)}, f32[64,2048]{1,0:T(8,128)}, u32[]{:S(2)}) copy-start(f32[64,2048]{1,0:T(8,128)} %get-tuple-element.37.refs_3_.refs_0_) | copy-start | bytes 1572868
  34.3 12.3 %collective-permute-start.10 = (f32[64,512]{1,0:T(8,128)S(1)}, f32[64,512]{1,0:T(8,128)S(1)}, u32[]{:S(2)}, u32[]{:S(2)}) collective-permute-start(f32[64,512]{1,0:T(8,128)S(1)} %get-tuple-element.52), channel_id=1, source_target_pairs={{0,2},{1,3},{2,0},{3,1},{4,6},{5,7},{6,4},{7,5},{8,10},{9,11},{10,... | collective-permute-start | bytes 393224 | tf_op jit(solution)/shard_map/ppermute | solution.py:505
  35.9 10.7 %collective-permute-start.11 = (f32[64,512]{1,0:T(8,128)S(1)}, f32[64,512]{1,0:T(8,128)S(1)}, u32[]{:S(2)}, u32[]{:S(2)}) collective-permute-start(f32[64,512]{1,0:T(8,128)S(1)} %get-tuple-element.53), channel_id=1, source_target_pairs={{0,1},{1,2},{2,3},{3,0},{4,5},{5,6},{6,7},{7,4},{8,9},{9,10},{10,1... | collective-permute-start | bytes 393224 | tf_op jit(solution)/shard_map/ppermute | solution.py:505
  37.5 9.1 %collective-permute-start.12 = (f32[64,512]{1,0:T(8,128)S(1)}, f32[64,512]{1,0:T(8,128)S(1)}, u32[]{:S(2)}, u32[]{:S(2)}) collective-permute-start(f32[64,512]{1,0:T(8,128)S(1)} %get-tuple-element.54), channel_id=1, source_target_pairs={{0,3},{1,0},{2,1},{3,2},{4,7},{5,4},{6,5},{7,6},{8,11},{9,8},{10,9... | collective-permute-start | bytes 393224 | tf_op jit(solution)/shard_map/ppermute | solution.py:505
  40.3 6.3 %copy-start.1 = (bf16[1,4,16,512]{3,2,1,0:T(8,128)(2,1)S(1)}, bf16[1,4,16,512]{3,2,1,0:T(8,128)(2,1)}, u32[]{:S(2)}) copy-start(bf16[1,4,16,512]{3,2,1,0:T(8,128)(2,1)} %refs_0_.8) | copy-start | bytes 196612
  40.3 14.3 %collective-permute-start.8 = (bf16[528,256]{1,0:T(8,128)(2,1)S(1)}, bf16[528,256]{1,0:T(8,128)(2,1)S(1)}, u32[]{:S(2)}, u32[]{:S(2)}) collective-permute-start(bf16[528,256]{1,0:T(8,128)(2,1)S(1)} %get-tuple-element.44), channel_id=1, source_target_pairs={{0,32},{32,64},{64,96},{96,0},{128,160},{160,192},{192,224},{224,1... | collective-permute-start | bytes 811016 | tf_op jit(solution)/shard_map/ppermute | solution.py:497
  40.7 14.0 %collective-permute-start.9 = (bf16[528,256]{1,0:T(8,128)(2,1)S(1)}, bf16[528,256]{1,0:T(8,128)(2,1)S(1)}, u32[]{:S(2)}, u32[]{:S(2)}) collective-permute-start(bf16[528,256]{1,0:T(8,128)(2,1)S(1)} %get-tuple-element.45), channel_id=1, source_target_pairs={{0,96},{32,0},{64,32},{96,64},{128,224},{160,128},{192,160},{224,1... | collective-permute-start | bytes 811016 | tf_op jit(solution)/shard_map/ppermute | solution.py:497
  46.6 0.8 %copy-start.6 = (f32[4,144,256]{2,1,0:T(8,128)}, f32[4,144,256]{2,1,0:T(8,128)S(1)}, u32[]{:S(2)}) copy-start(f32[4,144,256]{2,1,0:T(8,128)S(1)} %get-tuple-element.50.refs_5_) | copy-start | bytes 1769476
  46.6 16.2 %copy-start.3 = (bf16[512]{0:T(512)(128)(2,1)S(1)}, bf16[512]{0:T(512)(128)(2,1)}, u32[]{:S(2)}) copy-start(bf16[512]{0:T(512)(128)(2,1)} %refs_1_.9) | copy-start | bytes 3076
  47.4 15.4 %all-to-all-start = ((f32[16,8,128]{2,1,0:T(8,128)}), f32[16,8,128]{2,1,0:T(8,128)S(1)}, u32[]{:S(2)}, u32[]{:S(2)}) async-start(f32[16,8,128]{2,1,0:T(8,128)} %get-tuple-element.64), calls=%async_computation | async-start | bytes 131072 | tf_op jit(solution)/shard_map/all_to_all | solution.py:557
  55.2 4.6 %collective-permute-start.13 = (bf16[8,2,2,16,128]{4,3,2,1,0:T(8,128)(2,1)S(1)}, bf16[8,2,2,16,128]{4,3,2,1,0:T(8,128)(2,1)S(1)}, u32[]{:S(2)}, u32[]{:S(2)}) collective-permute-start(bf16[8,2,2,16,128]{4,3,2,1,0:T(8,128)(2,1)S(1)} %get-tuple-element.60), channel_id=1, source_target_pairs={{0,16},{16,0},{1,17},{17,1},{2,18},{18,2},{3,19},{19,3},{4,20},{20... | collective-permute-start | bytes 393224 | tf_op jit(solution)/shard_map/ppermute | solution.py:561
  55.3 1.1 %copy-start.7 = (f32[4,144,256]{2,1,0:T(8,128)S(1)}, f32[4,144,256]{2,1,0:T(8,128)}, u32[]{:S(2)}) copy-start(f32[4,144,256]{2,1,0:T(8,128)} %copy-done.6) | copy-start | bytes 1769476

commit v4 on v3

--- a/solution.py
+++ b/solution.py
@@ -32,7 +32,7 @@
 VMEM = pltpu.VMEM
 SMEM = pltpu.SMEM
 MIB = 1024 * 1024
-WHOLE = 60.5
+WHOLE = 60
 
 
 def params(mebibytes):
@@ -162,89 +162,115 @@
     arrays = 1 + max(place[0] for place in places)
     chunks = refs[2 : 2 + arrays]
     refs = refs[2 + arrays :]
+    start = None
     if not first:
-        top_in, sum_in = refs[:2]
+        start = refs[:2]
         refs = refs[2:]
     refs = refs[early:]
+    if last:
+        out_ref, *refs = refs
+    top_ref, sum_ref = refs
     blk = lax.axis_index("blk")
     offset = offset_ref[lax.axis_index("group")]
     key_number = lax.broadcasted_iota(jnp.int32, (TOKENS, TOKENS), 0)
     query_number = lax.broadcasted_iota(jnp.int32, (TOKENS, TOKENS), 1)
-    queries = [
-        query_ref[0, :, h * HEAD_SIZE : (h + 1) * HEAD_SIZE].T for h in range(HEADS)
-    ]
+    queries = [query_ref[0, :, h * HEAD_SIZE : (h + 1) * HEAD_SIZE].T for h in range(HEADS)]
     ones = jnp.ones((TAIL, TOKENS), BF16)
-    groups = []
+
+    def context_tile(number, base, flip, turn):
+        start = source_of(flip, turn) * TOKENS
+        bias = jnp.where(start + key_number < offset, 0.0, LOW_SCORE)
+        return (number, base, lambda score: score + bias)
+
+    def diagonal_tile(number, base):
+        low = jnp.where(key_number <= query_number, 0.0, LOW_SCORE)
+        return (number, base + 2 * HEAD_SIZE, lambda score: score + low)
+
+    def masked_tile(number, base, flip, turn):
+        low = jnp.where(source_of(flip, turn) < blk, 0.0, LOW_SCORE)
+        return (number, base + 2 * HEAD_SIZE, lambda score: score + low)
+
+    def block_tile(number, base):
+        return (number, base + 2 * HEAD_SIZE, lambda score: score)
+
+    def fold(groups, fresh_start):
+        steps = []
+        for tiles in groups:
+            keys, values = [], []
+            for number, base, _ in tiles:
+                keys.append(chunks[number][base : base + HEAD_SIZE, :].T)
+                value = chunks[number][base + HEAD_SIZE : base + 2 * HEAD_SIZE, :]
+                values.append(jnp.concatenate([value, ones], axis=0))
+            steps += [(head, keys, values, [close for _, _, close in tiles]) for head in range(HEADS)]
+
+        def scores_of(head, keys, values, closes):
+            return [
+                close(dot(key, queries[head]) * LOG2_SCALE) for key, close in zip(keys, closes)
+            ]
+
+        tops, sums = [None] * HEADS, [None] * HEADS
+        ahead = scores_of(*steps[0])
+        for index, (head, keys, values, closes) in enumerate(steps):
+            scores = ahead
+            if index + 1 < len(steps):
+                ahead = scores_of(*steps[index + 1])
+            if index < HEADS and not fresh_start:
+                source = (top_ref, sum_ref) if start is None else start
+                tops[head], sums[head] = source[0][head, 0:1], source[1][head]
+            top = jnp.max(functools.reduce(jnp.maximum, scores), axis=0, keepdims=True)
+            before = tops[head]
+            if before is not None:
+                top = jnp.maximum(before, top)
+            total = None
+            for score, value in zip(scores, values):
+                weight = jnp.exp2(score - top)
+                high = weight.astype(BF16)
+                low = (weight - high.astype(F32)).astype(BF16)
+                part = dot(value, high) + dot(value, low)
+                total = part if total is None else total + part
+            if before is not None:
+                total = sums[head] * jnp.exp2(before - top) + total
+            tops[head], sums[head] = top, total
+        for head in range(HEADS):
+            sum_ref[head] = sums[head]
+            top_ref[head] = jnp.broadcast_to(tops[head], (8, TOKENS))
+
+    here, there, flipped = [], [], []
     for number, base, flip, turn in places:
-        source = source_of(flip, turn)
-        parts = [
-            chunks[number][base + n * HEAD_SIZE : base + (n + 1) * HEAD_SIZE, :] for n in range(4)
-        ]
-        open_context = jnp.where(source * TOKENS + key_number < offset, 0.0, LOW_SCORE)
-        open_block = jnp.where(source <= blk, 0.0, LOW_SCORE)
-        groups.append(
-            [
-                (parts[0].T, jnp.concatenate([parts[1], ones], axis=0), open_context, False),
-                (
-                    parts[2].T,
-                    jnp.concatenate([parts[3], ones], axis=0),
-                    open_block,
-                    (flip, turn) == (0, 0),
-                ),
-            ]
-        )
-
-    def scores_of(group, head):
-        scores = []
-        for key, _, bias, diagonal in group:
-            score = dot(key, queries[head]) * LOG2_SCALE + bias
-            if diagonal:
-                score = jnp.where(key_number <= query_number, score, LOW_SCORE)
-            scores.append(score)
-        return scores
-
-    steps = [(group, head) for group in groups for head in range(HEADS)]
-    tops = [jnp.full((1, TOKENS), LOW_SCORE, F32) if first else top_in[h, 0:1] for h in range(HEADS)]
-    sums = [None if first else sum_in[h] for h in range(HEADS)]
-    ahead = scores_of(*steps[0])
-    for number, (group, head) in enumerate(steps):
-        scores = ahead
-        if number + 1 < len(steps):
-            ahead = scores_of(*steps[number + 1])
-        top = jnp.maximum(
-            tops[head], jnp.max(jnp.maximum(scores[0], scores[1]), axis=0, keepdims=True)
-        )
-        fresh = None
-        for score, (_, value, _, _) in zip(scores, group):
-            weight = jnp.exp2(score - top)
-            high = weight.astype(BF16)
-            low = (weight - high.astype(F32)).astype(BF16)
-            part = dot(value, high) + dot(value, low)
-            fresh = part if fresh is None else fresh + part
-        if sums[head] is not None:
-            fresh = sums[head] * jnp.exp2(tops[head] - top) + fresh
-        sums[head] = fresh
-        tops[head] = top
-    for head in range(HEADS):
-        if last:
-            (out_ref,) = refs
-            mixed = sums[head][:HEAD_SIZE] / sums[head][HEAD_SIZE : HEAD_SIZE + 1]
-            out_ref[0, :, head * HEAD_SIZE : (head + 1) * HEAD_SIZE] = mixed.T.astype(BF16)
+        context = context_tile(number, base, flip, turn)
+        if flip:
+            there.append(context)
+            flipped.append(block_tile(number, base))
+        elif turn == 0:
+            here.append([context, diagonal_tile(number, base)])
         else:
-            top_out, sum_out = refs
-            top_out[head] = jnp.broadcast_to(tops[head], (8, TOKENS))
-            sum_out[head] = sums[head]
+            here.append([context, masked_tile(number, base, flip, turn)])
+    if len(there) == 1:
+        here[-1] += there
+    else:
+        here.append(there)
+    fold(here, first)
+    start = None
+
+    @pl.when(blk >= 4)
+    def _():
+        fold([flipped], False)
+
+    if last:
+        for head in range(HEADS):
+            total = sum_ref[head]
+            mixed = total[:HEAD_SIZE] / total[HEAD_SIZE : HEAD_SIZE + 1]
+            out_ref[0, :, head * HEAD_SIZE : (head + 1) * HEAD_SIZE] = mixed.astype(BF16).T
 
 
 def attend(block_offset, queries, chunks, places, state, last, token, early=()):
     first = state is None
+    top, total = (HEADS, 8, TOKENS), (HEADS, HEAD_SIZE + TAIL, TOKENS)
     if last:
         outs = [shape((1, TOKENS, HEADS * HEAD_SIZE), BF16)]
+        scratch = [pltpu.VMEM(top, F32), pltpu.VMEM(total, F32)]
     else:
-        outs = [
-            shape((HEADS, 8, TOKENS), F32),
-            shape((HEADS, HEAD_SIZE + TAIL, TOKENS), F32),
-        ]
+        outs, scratch = [shape(top, F32), shape(total, F32)], []
     operands = [(block_offset, SMEM)]
     operands += [(a, VMEM) for a in (queries, *chunks, *(() if first else state), *early)]
     return run(
@@ -254,6 +280,7 @@
         token,
         outs,
         operands,
+        scratch,
         cost=3,
     )
 
@@ -420,7 +447,7 @@
     return run(
         decode_kernel,
         "decode",
-        WHOLE - 1.95,
+        58,
         None,
         [shape((rows, QUARTER), BF16 if turn else F32) for turn in TURNS],
         [(a, pl.ANY) for a in operands],
@@ -526,12 +553,9 @@
     )
     near = lax.ppermute(packed, "tp", [(i, i ^ 1) for i in range(16)])
     far = lax.ppermute(packed, "blk", [(i, i ^ 4) for i in range(8)])
-    far_near = lax.ppermute(
-        packed,
-        ("blk", "tp"),
-        [(b * 16 + t, (b ^ 4) * 16 + (t ^ 1)) for b in range(8) for t in range(16)],
-    )
     *parts, own, token = decode(row_lengths, step_query, step_cache, row_cache, out_weight)
+    far, parts[0] = lax.optimization_barrier((far, parts[0]))
+    far_near = lax.ppermute(far, "tp", [(i, i ^ 1) for i in range(16)])
     came = [move_y(a, turn) for a, turn in zip(parts, TURNS)]
     here, token = join(packed, near, far, far_near, token)
     up = move_x(here, 1)

time: 64.1 us -> 61.6 us (0.961)
  starting transfers between devices: 31.8 us -> 29.3 us
  waiting for transfers between devices: 5.3 us -> 7.01 us
  Pallas kernels: 22.8 us -> 21.3 us
    all_to_all x1, starting transfers between devices: 7.27 us -> 5.05 us  [body(): lax.all_to_all(square, 'tp', split_axis=0, concat_axis=0, tiled=True)]
    ppermute x3, waiting for transfers between devices: 2.37 us -> 4.23 us  [move_y(): return lax.ppermute(a, 'tp', [(i, (i + 4 * turn) % 16) for i in range(16)])]
    pallas_call x12, Pallas kernels: 22.8 us -> 21.3 us  [run(): pl.pallas_call(with_token, out_shape=(*outs, TOKEN) if emit else tuple(ou...]
    ppermute x3, starting transfers between devices: 6.52 us -> 5.21 us  [move_y(): return lax.ppermute(a, 'tp', [(i, (i + 4 * turn) % 16) for i in range(16)])]
    ppermute x1, starting transfers between devices: 0.01 us -> 1.1 us  [body(): far_near = lax.ppermute(far, 'tp', [(i, i ^ 1) for i in range(16)])]
    ppermute x1, starting transfers between devices: 2 us -> 1.02 us  [body(): near = lax.ppermute(packed, 'tp', [(i, i ^ 1) for i in range(16)])]
    ppermute x1, starting transfers between devices: 6.29 us -> 7.28 us  [body(): far = lax.ppermute(packed, 'blk', [(i, i ^ 4) for i in range(8)])]
  transfers between devices with their start and end apart: 15 -> 15, of which waited for: 4 -> 2; matrix products, arithmetic and copies ran while one was open for 0% -> 0% of each run, Pallas kernels for 32% -> 31%
where the time goes in v4:
time: 61.6 us; the launch traced here: 61.3 us
  starting transfers between devices  29.3 us (48%)
  Pallas kernels  21.3 us (35%)
  waiting for transfers between devices  7.01 us (11%)
  local copies, waits for them, and re-layouts  2.82 us (5%)
  between operations  0.85 us (1%)
    pallas_call x12, Pallas kernels, run(): pl.pallas_call(with_token, out_shape=(*outs, TOKEN) if emit else tuple(ou...  21.3 us
    ppermute x1, starting transfers between devices, body(): far = lax.ppermute(packed, 'blk', [(i, i ^ 4) for i in range(8)])  7.28 us
    ppermute x3, starting transfers between devices, move_z(): lax.ppermute(a, 'tp', [(i, i // 4 * 4 + (i + turn) % 4) for i in range(16)])  5.38 us
    ppermute x3, starting transfers between devices, move_y(): return lax.ppermute(a, 'tp', [(i, (i + 4 * turn) % 16) for i in range(16)])  5.21 us
    all_to_all x1, starting transfers between devices, body(): lax.all_to_all(square, 'tp', split_axis=0, concat_axis=0, tiled=True)  5.05 us
    ppermute x3, waiting for transfers between devices, move_y(): return lax.ppermute(a, 'tp', [(i, (i + 4 * turn) % 16) for i in range(16)])  4.23 us
    ppermute x4, starting transfers between devices, move_x(): lax.ppermute(a, 'blk', [(i, i // 4 * 4 + (i + turn) % 4) for i in range(8)])  4.21 us
    unnamed x20, local copies, waits for them, and re-layouts  2.82 us
  transfers between devices with their start and end apart: 15, of which 2 were waited for; matrix products, arithmetic and copies ran while one was open for 0% of the time, Pallas kernels for 31%

profile of v4, /device:TPU:6, one launch (start us, length us, event | category | flops | bytes accessed | tf_op | source)
XLA Modules:
  0.0 61.3 jit_solution(13514114235034225613)
XLA Ops:
  0.6 1.6 %pack.1.refs_0_ = bf16[272,256]{1,0:T(8,128)(2,1)} custom-call(s32[1,16]{1,0:T(1,128)} %bitcast.6, bf16[1,2,64,256]{3,2,1,0:T(8,128)(2,1)} %bitcast.4, bf16[1,2,64,256]{3,2,1,0:T(8,128)(2,1)} %bitcast.5), custom_call_target="tpu_custom_call" | custom-call | flops 1024 | bytes 1024 | tf_op jit(solution)/shard_map/pack/pallas_call | solution.py:72
  2.2 0.0 copy-start
  2.2 0.0 copy-start.4
  2.2 0.0 copy-start.5
  2.2 7.3 %collective-permute-start.1 = (bf16[272,256]{1,0:T(8,128)(2,1)}, bf16[272,256]{1,0:T(8,128)(2,1)S(1)}, u32[]{:S(2)}, u32[]{:S(2)}) collective-permute-start(bf16[272,256]{1,0:T(8,128)(2,1)} %pack.1.refs_0_), channel_id=1, source_target_pairs={{0,128},{32,160},{64,192},{96,224},{128,0},{160,32},{192,64},{224,... | collective-permute-start | bytes 417800 | tf_op jit(solution)/shard_map/ppermute | solution.py:555
  9.5 1.0 %collective-permute-start = (bf16[272,256]{1,0:T(8,128)(2,1)}, bf16[272,256]{1,0:T(8,128)(2,1)S(1)}, u32[]{:S(2)}, u32[]{:S(2)}) collective-permute-start(bf16[272,256]{1,0:T(8,128)(2,1)} %pack.1.refs_0_), channel_id=1, source_target_pairs={{0,1},{1,0},{2,3},{3,2},{4,5},{5,4},{6,7},{7,6},{8,9},{9,8},{10,11... | collective-permute-start | bytes 417800 | tf_op jit(solution)/shard_map/ppermute | solution.py:554
  10.5 8.3 %decode.1 = (bf16[64,2048]{1,0:T(8,128)(2,1)}, bf16[64,2048]{1,0:T(8,128)(2,1)}, bf16[64,2048]{1,0:T(8,128)(2,1)}, f32[64,2048]{1,0:T(8,128)}, f32[8,128]{1,0:T(8,128)}) custom-call(s32[1,16]{1,0:T(1,128)} %refs_0_.5, bf16[1,4,16,512]{3,2,1,0:T(8,128)(2,1)} %refs_1_.5, bf16[1,4,2,16,128]{4,3,2,1,0:T(8,128)(2,1)} %refs_2_.1, ...), custom_call_target="tpu_custom_call" | custom-call | flops 10350001152 | bytes 1024 | tf_op jit(solution)/shard_map/decode/pallas_call | solution.py:72
  18.9 0.0 collective-permute-done.1.refs_2_
  18.9 1.1 %collective-permute-start.2 = (bf16[272,256]{1,0:T(8,128)(2,1)S(1)}, bf16[272,256]{1,0:T(8,128)(2,1)S(1)}, u32[]{:S(2)}, u32[]{:S(2)}) collective-permute-start(bf16[272,256]{1,0:T(8,128)(2,1)S(1)} %collective-permute-done.1.refs_2_), channel_id=1, source_target_pairs={{0,1},{1,0},{2,3},{3,2},{4,5},{5,4},{6,7},{7,6},{8,9},{9,8},{10,11... | collective-permute-start | bytes 417800 | tf_op jit(solution)/shard_map/ppermute | solution.py:558
  20.0 1.6 %collective-permute-start.6 = (bf16[64,2048]{1,0:T(8,128)(2,1)}, bf16[64,2048]{1,0:T(8,128)(2,1)S(1)}, u32[]{:S(2)}, u32[]{:S(2)}) collective-permute-start(bf16[64,2048]{1,0:T(8,128)(2,1)} %get-tuple-element.43), channel_id=1, source_target_pairs={{0,4},{1,5},{2,6},{3,7},{4,8},{5,9},{6,10},{7,11},{8,12},{9,13},{1... | collective-permute-start | bytes 786440 | tf_op jit(solution)/shard_map/ppermute | solution.py:528
  21.6 1.7 %collective-permute-start.7 = (bf16[64,2048]{1,0:T(8,128)(2,1)}, bf16[64,2048]{1,0:T(8,128)(2,1)S(1)}, u32[]{:S(2)}, u32[]{:S(2)}) collective-permute-start(bf16[64,2048]{1,0:T(8,128)(2,1)} %get-tuple-element.44), channel_id=1, source_target_pairs={{0,12},{1,13},{2,14},{3,15},{4,0},{5,1},{6,2},{7,3},{8,4},{9,5},{1... | collective-permute-start | bytes 786440 | tf_op jit(solution)/shard_map/ppermute | solution.py:528
  23.2 2.0 %collective-permute-start.5 = (bf16[64,2048]{1,0:T(8,128)(2,1)}, bf16[64,2048]{1,0:T(8,128)(2,1)S(1)}, u32[]{:S(2)}, u32[]{:S(2)}) collective-permute-start(bf16[64,2048]{1,0:T(8,128)(2,1)} %get-tuple-element.42), channel_id=1, source_target_pairs={{0,8},{1,9},{2,10},{3,11},{4,12},{5,13},{6,14},{7,15},{8,0},{9,1},... | collective-permute-start | bytes 786440 | tf_op jit(solution)/shard_map/ppermute | solution.py:528
  25.2 0.0 collective-permute-done.refs_1_
  25.2 0.0 collective-permute-done.2.refs_3_
  25.2 0.0 copy-done
  25.2 0.0 copy-start.2
  25.2 0.7 %copy-done.2 = f32[8,128]{1,0:T(8,128)S(1)} copy-done((f32[8,128]{1,0:T(8,128)S(1)}, f32[8,128]{1,0:T(8,128)}, u32[]{:S(2)}) %copy-start.2) | copy-done | bytes 4120
  25.9 0.0 copy-start.9
  26.0 0.6 collective-permute-start.3
  26.5 1.5 %collective-permute-start.4 = (bf16[1056,256]{1,0:T(8,128)(2,1)S(1)}, bf16[1056,256]{1,0:T(8,128)(2,1)S(1)}, u32[]{:S(2)}, u32[]{:S(2)}) collective-permute-start(bf16[1056,256]{1,0:T(8,128)(2,1)S(1)} %get-tuple-element.40.refs_2_.refs_0_), channel_id=1, source_target_pairs={{0,96},{32,0},{64,32},{96,64},{128,224},{160,128},{192,160},{224,1... | collective-permute-start | bytes 1622024 | tf_op jit(solution)/shard_map/ppermute | solution.py:524
  28.1 0.0 copy-done.4
  28.1 0.0 copy-done.5
  28.1 0.0 copy-start.8
  28.1 1.0 %copy-done.8 = f32[64,2048]{1,0:T(8,128)S(1)} copy-done((f32[64,2048]{1,0:T(8,128)S(1)}, f32[64,2048]{1,0:T(8,128)}, u32[]{:S(2)}) %copy-start.8) | copy-done | bytes 524312
  29.1 2.1 %attend.3 = (f32[4,8,256]{2,1,0:T(8,128)S(1)}, f32[4,144,256]{2,1,0:T(8,128)S(1)}, f32[8,128]{1,0:T(8,128)S(1)}) custom-call(s32[2]{0:T(128)S(1)} %copy-done.5, bf16[1,256,512]{2,1,0:T(8,128)(2,1)S(1)} %copy-done.4, bf16[1056,256]{1,0:T(8,128)(2,1)S(1)} %get-tuple-element.40.refs_2_.refs_0_, f32[64,2048]{1,0:T(8,128)S(1)} %copy-done.8, ...), custom_call_target="tpu_custom_call" | custom-call | flops 3450000896 | bytes 1024 | tf_op jit(solution)/shard_map/attend/pallas_call | solution.py:72
  31.2 0.0 collective-permute-done.6.refs_2_
  31.2 0.0 collective-permute-done.7.refs_3_
  31.3 4.2 %collective-permute-done.5.refs_1_ = bf16[64,2048]{1,0:T(8,128)(2,1)S(1)} collective-permute-done((bf16[64,2048]{1,0:T(8,128)(2,1)}, bf16[64,2048]{1,0:T(8,128)(2,1)S(1)}, u32[]{:S(2)}, u32[]{:S(2)}) %collective-permute-start.5) | collective-permute-done | bytes 262176 | tf_op jit(solution)/shard_map/ppermute | solution.py:528
  35.5 0.0 copy-done.9
  35.5 0.1 quarters.1
  35.6 1.6 %collective-permute-start.10 = (f32[64,512]{1,0:T(8,128)S(1)}, f32[64,512]{1,0:T(8,128)S(1)}, u32[]{:S(2)}, u32[]{:S(2)}) collective-permute-start(f32[64,512]{1,0:T(8,128)S(1)} %get-tuple-element.56), channel_id=1, source_target_pairs={{0,2},{1,3},{2,0},{3,1},{4,6},{5,7},{6,4},{7,5},{8,10},{9,11},{10,... | collective-permute-start | bytes 393224 | tf_op jit(solution)/shard_map/ppermute | solution.py:532
  37.2 1.0 %collective-permute-start.11 = (f32[64,512]{1,0:T(8,128)S(1)}, f32[64,512]{1,0:T(8,128)S(1)}, u32[]{:S(2)}, u32[]{:S(2)}) collective-permute-start(f32[64,512]{1,0:T(8,128)S(1)} %get-tuple-element.57), channel_id=1, source_target_pairs={{0,1},{1,2},{2,3},{3,0},{4,5},{5,6},{6,7},{7,4},{8,9},{9,10},{10,1... | collective-permute-start | bytes 393224 | tf_op jit(solution)/shard_map/ppermute | solution.py:532
  38.2 2.8 %collective-permute-start.12 = (f32[64,512]{1,0:T(8,128)S(1)}, f32[64,512]{1,0:T(8,128)S(1)}, u32[]{:S(2)}, u32[]{:S(2)}) collective-permute-start(f32[64,512]{1,0:T(8,128)S(1)} %get-tuple-element.58), channel_id=1, source_target_pairs={{0,3},{1,0},{2,1},{3,2},{4,7},{5,4},{6,5},{7,6},{8,11},{9,8},{10,9... | collective-permute-start | bytes 393224 | tf_op jit(solution)/shard_map/ppermute | solution.py:532
  41.0 0.0 collective-permute-done.3.refs_0_.refs_2_.refs_1_
  41.0 0.0 collective-permute-done.4.refs_1_.refs_3_.refs_2_
  41.0 0.0 copy-start.1
  41.0 0.6 collective-permute-start.8
  41.6 1.5 %collective-permute-start.9 = (bf16[528,256]{1,0:T(8,128)(2,1)S(1)}, bf16[528,256]{1,0:T(8,128)(2,1)S(1)}, u32[]{:S(2)}, u32[]{:S(2)}) collective-permute-start(bf16[528,256]{1,0:T(8,128)(2,1)S(1)} %get-tuple-element.49), channel_id=1, source_target_pairs={{0,96},{32,0},{64,32},{96,64},{128,224},{160,128},{192,160},{224,1... | collective-permute-start | bytes 811016 | tf_op jit(solution)/shard_map/ppermute | solution.py:524
  43.1 3.4 %attend.4 = (f32[4,8,256]{2,1,0:T(8,128)S(1)}, f32[4,144,256]{2,1,0:T(8,128)S(1)}, f32[8,128]{1,0:T(8,128)S(1)}) custom-call(s32[2]{0:T(128)S(1)} %copy-done.5, bf16[1,256,512]{2,1,0:T(8,128)(2,1)S(1)} %copy-done.4, bf16[1056,256]{1,0:T(8,128)(2,1)S(1)} %collective-permute-done.3.refs_0_.refs_2_.refs_1_, ...), custom_call_target="tpu_custom_call" | custom-call | flops 3450000896 | bytes 1024 | tf_op jit(solution)/shard_map/attend/pallas_call | solution.py:72
  46.5 0.0 copy-start.6
  46.5 0.0 copy-start.3
  46.5 0.0 collective-permute-done.10.refs_2_
  46.5 0.0 collective-permute-done.11.refs_3_
  46.6 0.0 collective-permute-done.12.refs_4_
  46.6 0.0 copy-done.1
  46.6 0.8 %hidden.1 = (f32[64,512]{1,0:T(8,128)S(1)}, f32[16,8,128]{2,1,0:T(8,128)}, f32[8,128]{1,0:T(8,128)S(1)}) custom-call(bf16[1,4,16,512]{3,2,1,0:T(8,128)(2,1)S(1)} %copy-done.1, f32[64,512]{1,0:T(8,128)S(1)} %get-tuple-element.55.refs_1_, f32[64,512]{1,0:T(8,128)S(1)} %collective-permute-done.10.refs_2_, f32[64,512]{1,0:T(8,128)S(1)} %collective-permute-done.11.refs_3_, ...), custom_call_target="tpu_custom_call" | custom-call | flops 1024 | bytes 1024 | tf_op jit(solution)/shard_map/hidden/pallas_call | solution.py:72
  47.3 0.0 copy-done.6
  47.3 5.0 %all-to-all-start = ((f32[16,8,128]{2,1,0:T(8,128)}), f32[16,8,128]{2,1,0:T(8,128)S(1)}, u32[]{:S(2)}, u32[]{:S(2)}) async-start(f32[16,8,128]{2,1,0:T(8,128)} %get-tuple-element.68), calls=%async_computation | async-start | bytes 131072 | tf_op jit(solution)/shard_map/all_to_all | solution.py:581
  52.4 0.0 collective-permute-done.8.refs_3_.refs_2_
  52.4 0.0 collective-permute-done.9.refs_4_.refs_3_
  52.4 0.5 pages.1
  52.9 0.1 collective-permute-start.13
  53.0 0.0 copy-start.7
  53.0 1.1 %copy-done.7 = f32[4,144,256]{2,1,0:T(8,128)S(1)} copy-done((f32[4,144,256]{2,1,0:T(8,128)S(1)}, f32[4,144,256]{2,1,0:T(8,128)}, u32[]{:S(2)}) %copy-start.7) | copy-done | bytes 589848
  54.1 3.0 %attend.5 = (bf16[1,256,512]{2,1,0:T(8,128)(2,1)}, f32[8,128]{1,0:T(8,128)S(1)}) custom-call(s32[2]{0:T(128)S(1)} %copy-done.5, bf16[1,256,512]{2,1,0:T(8,128)(2,1)S(1)} %copy-done.4, bf16[528,256]{1,0:T(8,128)(2,1)S(1)} %collective-permute-done.8.refs_3_.refs_2_, bf16[528,256]{1,0:T(8,128)(2,1)S(1)} %collective-permute-done.9.refs_4_.refs_3_, ...), custom_call_target="tpu_custom_call" | custom-call | flops 3450000896 | bytes 1024 | tf_op jit(solution)/shard_map/attend/pallas_call | solution.py:72
  57.1 0.0 collective-permute-done.13.refs_1_
  57.1 0.7 %pool.1 = (bf16[8,2,2,2,16,128]{5,4,3,2,1,0:T(8,128)(2,1)}, f32[8,128]{1,0:T(8,128)S(1)}) custom-call(bf16[8,2,2,16,128]{4,3,2,1,0:T(8,128)(2,1)S(1)} %get-tuple-element.63.refs_0_, bf16[8,2,2,16,128]{4,3,2,1,0:T(8,128)(2,1)S(1)} %collective-permute-done.13.refs_1_, f32[8,128]{1,0:T(8,128)S(1)} %get-tuple-element.65.refs_2_), custom_call_target="tpu_custom_call" | custom-call | flops 1024 | bytes 1024 | tf_op jit(solution)/shard_map/pool/pallas_call | solution.py:72
  57.8 2.7 %all-to-all-done.refs_2_ = f32[16,8,128]{2,1,0:T(8,128)S(1)} async-done(((f32[16,8,128]{2,1,0:T(8,128)}), f32[16,8,128]{2,1,0:T(8,128)S(1)}, u32[]{:S(2)}, u32[]{:S(2)}) %all-to-all-start) | async-done | bytes 65568 | tf_op jit(solution)/shard_map/all_to_all | solution.py:581
  60.5 0.0 copy-done.3
  60.5 0.7 %finish.1 = (bf16[1,4,16,512]{3,2,1,0:T(8,128)(2,1)}, f32[8,128]{1,0:T(8,128)}) custom-call(f32[64,512]{1,0:T(8,128)S(1)} %get-tuple-element.67.refs_0_, bf16[512]{0:T(512)(128)(2,1)S(1)} %copy-done.3, f32[16,8,128]{2,1,0:T(8,128)S(1)} %all-to-all-done.refs_2_, f32[8,128]{1,0:T(8,128)S(1)} %get-tuple-element.69.refs_3_), custom_call_target="tpu_custom_call" | custom-call | flops 1024 | bytes 1024 | tf_op jit(solution)/shard_map/finish/pallas_call | solution.py:72
  (2 shorter events, 0.1 us)
Async XLA Ops:
  2.2 23.0 %copy-start = (bf16[272,256]{1,0:T(8,128)(2,1)S(1)}, bf16[272,256]{1,0:T(8,128)(2,1)}, u32[]{:S(2)}) copy-start(bf16[272,256]{1,0:T(8,128)(2,1)} %pack.1.refs_0_) | copy-start | bytes 417796
  2.2 25.9 %copy-start.4 = (bf16[1,256,512]{2,1,0:T(8,128)(2,1)S(1)}, bf16[1,256,512]{2,1,0:T(8,128)(2,1)}, u32[]{:S(2)}) copy-start(bf16[1,256,512]{2,1,0:T(8,128)(2,1)} %refs_1_.8) | copy-start | bytes 786436
  2.2 25.8 %copy-start.5 = (s32[2]{0:T(128)S(1)}, s32[2]{0:T(128)}, u32[]{:S(2)}) copy-start(s32[2]{0:T(128)} %refs_0_.9) | copy-start | bytes 28
  2.2 16.6 %collective-permute-start.1 = (bf16[272,256]{1,0:T(8,128)(2,1)}, bf16[272,256]{1,0:T(8,128)(2,1)S(1)}, u32[]{:S(2)}, u32[]{:S(2)}) collective-permute-start(bf16[272,256]{1,0:T(8,128)(2,1)} %pack.1.refs_0_), channel_id=1, source_target_pairs={{0,128},{32,160},{64,192},{96,224},{128,0},{160,32},{192,64},{224,... | collective-permute-start | bytes 417800 | tf_op jit(solution)/shard_map/ppermute | solution.py:555
  9.5 15.7 %collective-permute-start = (bf16[272,256]{1,0:T(8,128)(2,1)}, bf16[272,256]{1,0:T(8,128)(2,1)S(1)}, u32[]{:S(2)}, u32[]{:S(2)}) collective-permute-start(bf16[272,256]{1,0:T(8,128)(2,1)} %pack.1.refs_0_), channel_id=1, source_target_pairs={{0,1},{1,0},{2,3},{3,2},{4,5},{5,4},{6,7},{7,6},{8,9},{9,8},{10,11... | collective-permute-start | bytes 417800 | tf_op jit(solution)/shard_map/ppermute | solution.py:554
  18.9 6.3 %collective-permute-start.2 = (bf16[272,256]{1,0:T(8,128)(2,1)S(1)}, bf16[272,256]{1,0:T(8,128)(2,1)S(1)}, u32[]{:S(2)}, u32[]{:S(2)}) collective-permute-start(bf16[272,256]{1,0:T(8,128)(2,1)S(1)} %collective-permute-done.1.refs_2_), channel_id=1, source_target_pairs={{0,1},{1,0},{2,3},{3,2},{4,5},{5,4},{6,7},{7,6},{8,9},{9,8},{10,11... | collective-permute-start | bytes 417800 | tf_op jit(solution)/shard_map/ppermute | solution.py:558
  20.0 11.2 %collective-permute-start.6 = (bf16[64,2048]{1,0:T(8,128)(2,1)}, bf16[64,2048]{1,0:T(8,128)(2,1)S(1)}, u32[]{:S(2)}, u32[]{:S(2)}) collective-permute-start(bf16[64,2048]{1,0:T(8,128)(2,1)} %get-tuple-element.43), channel_id=1, source_target_pairs={{0,4},{1,5},{2,6},{3,7},{4,8},{5,9},{6,10},{7,11},{8,12},{9,13},{1... | collective-permute-start | bytes 786440 | tf_op jit(solution)/shard_map/ppermute | solution.py:528
  21.6 9.7 %collective-permute-start.7 = (bf16[64,2048]{1,0:T(8,128)(2,1)}, bf16[64,2048]{1,0:T(8,128)(2,1)S(1)}, u32[]{:S(2)}, u32[]{:S(2)}) collective-permute-start(bf16[64,2048]{1,0:T(8,128)(2,1)} %get-tuple-element.44), channel_id=1, source_target_pairs={{0,12},{1,13},{2,14},{3,15},{4,0},{5,1},{6,2},{7,3},{8,4},{9,5},{1... | collective-permute-start | bytes 786440 | tf_op jit(solution)/shard_map/ppermute | solution.py:528
  23.2 12.2 %collective-permute-start.5 = (bf16[64,2048]{1,0:T(8,128)(2,1)}, bf16[64,2048]{1,0:T(8,128)(2,1)S(1)}, u32[]{:S(2)}, u32[]{:S(2)}) collective-permute-start(bf16[64,2048]{1,0:T(8,128)(2,1)} %get-tuple-element.42), channel_id=1, source_target_pairs={{0,8},{1,9},{2,10},{3,11},{4,12},{5,13},{6,14},{7,15},{8,0},{9,1},... | collective-permute-start | bytes 786440 | tf_op jit(solution)/shard_map/ppermute | solution.py:528
  25.2 0.7 %copy-start.2 = (f32[8,128]{1,0:T(8,128)S(1)}, f32[8,128]{1,0:T(8,128)}, u32[]{:S(2)}) copy-start(f32[8,128]{1,0:T(8,128)} %get-tuple-element.39.refs_4_) | copy-start | bytes 12292
  25.9 9.6 %copy-start.9 = (f32[64,2048]{1,0:T(8,128)S(1)}, f32[64,2048]{1,0:T(8,128)}, u32[]{:S(2)}) copy-start(f32[64,2048]{1,0:T(8,128)} %get-tuple-element.41.refs_3_.refs_0_) | copy-start | bytes 1572868
  26.0 15.0 %collective-permute-start.3 = (bf16[1056,256]{1,0:T(8,128)(2,1)S(1)}, bf16[1056,256]{1,0:T(8,128)(2,1)S(1)}, u32[]{:S(2)}, u32[]{:S(2)}) collective-permute-start(bf16[1056,256]{1,0:T(8,128)(2,1)S(1)} %get-tuple-element.40.refs_2_.refs_0_), channel_id=1, source_target_pairs={{0,32},{32,64},{64,96},{96,0},{128,160},{160,192},{192,224},{224,1... | collective-permute-start | bytes 1622024 | tf_op jit(solution)/shard_map/ppermute | solution.py:524
  26.5 14.5 %collective-permute-start.4 = (bf16[1056,256]{1,0:T(8,128)(2,1)S(1)}, bf16[1056,256]{1,0:T(8,128)(2,1)S(1)}, u32[]{:S(2)}, u32[]{:S(2)}) collective-permute-start(bf16[1056,256]{1,0:T(8,128)(2,1)S(1)} %get-tuple-element.40.refs_2_.refs_0_), channel_id=1, source_target_pairs={{0,96},{32,0},{64,32},{96,64},{128,224},{160,128},{192,160},{224,1... | collective-permute-start | bytes 1622024 | tf_op jit(solution)/shard_map/ppermute | solution.py:524
  28.1 1.0 %copy-start.8 = (f32[64,2048]{1,0:T(8,128)S(1)}, f32[64,2048]{1,0:T(8,128)}, u32[]{:S(2)}) copy-start(f32[64,2048]{1,0:T(8,128)} %get-tuple-element.41.refs_3_.refs_0_) | copy-start | bytes 1572868
  35.6 10.9 %collective-permute-start.10 = (f32[64,512]{1,0:T(8,128)S(1)}, f32[64,512]{1,0:T(8,128)S(1)}, u32[]{:S(2)}, u32[]{:S(2)}) collective-permute-start(f32[64,512]{1,0:T(8,128)S(1)} %get-tuple-element.56), channel_id=1, source_target_pairs={{0,2},{1,3},{2,0},{3,1},{4,6},{5,7},{6,4},{7,5},{8,10},{9,11},{10,... | collective-permute-start | bytes 393224 | tf_op jit(solution)/shard_map/ppermute | solution.py:532
  37.2 9.4 %collective-permute-start.11 = (f32[64,512]{1,0:T(8,128)S(1)}, f32[64,512]{1,0:T(8,128)S(1)}, u32[]{:S(2)}, u32[]{:S(2)}) collective-permute-start(f32[64,512]{1,0:T(8,128)S(1)} %get-tuple-element.57), channel_id=1, source_target_pairs={{0,1},{1,2},{2,3},{3,0},{4,5},{5,6},{6,7},{7,4},{8,9},{9,10},{10,1... | collective-permute-start | bytes 393224 | tf_op jit(solution)/shard_map/ppermute | solution.py:532
  38.2 8.4 %collective-permute-start.12 = (f32[64,512]{1,0:T(8,128)S(1)}, f32[64,512]{1,0:T(8,128)S(1)}, u32[]{:S(2)}, u32[]{:S(2)}) collective-permute-start(f32[64,512]{1,0:T(8,128)S(1)} %get-tuple-element.58), channel_id=1, source_target_pairs={{0,3},{1,0},{2,1},{3,2},{4,7},{5,4},{6,5},{7,6},{8,11},{9,8},{10,9... | collective-permute-start | bytes 393224 | tf_op jit(solution)/shard_map/ppermute | solution.py:532
  41.0 5.5 %copy-start.1 = (bf16[1,4,16,512]{3,2,1,0:T(8,128)(2,1)S(1)}, bf16[1,4,16,512]{3,2,1,0:T(8,128)(2,1)}, u32[]{:S(2)}) copy-start(bf16[1,4,16,512]{3,2,1,0:T(8,128)(2,1)} %refs_0_.8) | copy-start | bytes 196612
  41.0 11.4 %collective-permute-start.8 = (bf16[528,256]{1,0:T(8,128)(2,1)S(1)}, bf16[528,256]{1,0:T(8,128)(2,1)S(1)}, u32[]{:S(2)}, u32[]{:S(2)}) collective-permute-start(bf16[528,256]{1,0:T(8,128)(2,1)S(1)} %get-tuple-element.48), channel_id=1, source_target_pairs={{0,32},{32,64},{64,96},{96,0},{128,160},{160,192},{192,224},{224,1... | collective-permute-start | bytes 811016 | tf_op jit(solution)/shard_map/ppermute | solution.py:524
  41.6 10.8 %collective-permute-start.9 = (bf16[528,256]{1,0:T(8,128)(2,1)S(1)}, bf16[528,256]{1,0:T(8,128)(2,1)S(1)}, u32[]{:S(2)}, u32[]{:S(2)}) collective-permute-start(bf16[528,256]{1,0:T(8,128)(2,1)S(1)} %get-tuple-element.49), channel_id=1, source_target_pairs={{0,96},{32,0},{64,32},{96,64},{128,224},{160,128},{192,160},{224,1... | collective-permute-start | bytes 811016 | tf_op jit(solution)/shard_map/ppermute | solution.py:524
  46.5 0.8 %copy-start.6 = (f32[4,144,256]{2,1,0:T(8,128)}, f32[4,144,256]{2,1,0:T(8,128)S(1)}, u32[]{:S(2)}) copy-start(f32[4,144,256]{2,1,0:T(8,128)S(1)} %get-tuple-element.54.refs_5_) | copy-start | bytes 1769476
  46.5 14.0 %copy-start.3 = (bf16[512]{0:T(512)(128)(2,1)S(1)}, bf16[512]{0:T(512)(128)(2,1)}, u32[]{:S(2)}) copy-start(bf16[512]{0:T(512)(128)(2,1)} %refs_1_.9) | copy-start | bytes 3076
  47.3 13.2 %all-to-all-start = ((f32[16,8,128]{2,1,0:T(8,128)}), f32[16,8,128]{2,1,0:T(8,128)S(1)}, u32[]{:S(2)}, u32[]{:S(2)}) async-start(f32[16,8,128]{2,1,0:T(8,128)} %get-tuple-element.68), calls=%async_computation | async-start | bytes 131072 | tf_op jit(solution)/shard_map/all_to_all | solution.py:581
  52.9 4.2 %collective-permute-start.13 = (bf16[8,2,2,16,128]{4,3,2,1,0:T(8,128)(2,1)S(1)}, bf16[8,2,2,16,128]{4,3,2,1,0:T(8,128)(2,1)S(1)}, u32[]{:S(2)}, u32[]{:S(2)}) collective-permute-start(bf16[8,2,2,16,128]{4,3,2,1,0:T(8,128)(2,1)S(1)} %get-tuple-element.64), channel_id=1, source_target_pairs={{0,16},{16,0},{1,17},{17,1},{2,18},{18,2},{3,19},{19,3},{4,20},{20... | collective-permute-start | bytes 393224 | tf_op jit(solution)/shard_map/ppermute | solution.py:585
  53.0 1.1 %copy-start.7 = (f32[4,144,256]{2,1,0:T(8,128)S(1)}, f32[4,144,256]{2,1,0:T(8,128)}, u32[]{:S(2)}) copy-start(f32[4,144,256]{2,1,0:T(8,128)} %copy-done.6) | copy-start | bytes 1769476

commit v5 on v4

--- a/solution.py
+++ b/solution.py
@@ -58,7 +58,7 @@
 TOKEN = shape((8, HEAD_SIZE), F32)
 
 
-def run(kernel, title, mebibytes, token, outs, operands, scratch=(), emit=True, cost=0):
+def run(kernel, title, mebibytes, token, outs, operands, scratch=(), emit=True, cost=0, space=VMEM):
     tokens = [] if token is None else [token]
     count = len(operands) + len(tokens)
 
@@ -73,7 +73,7 @@
         with_token,
         out_shape=(*outs, TOKEN) if emit else tuple(outs),
         in_specs=[spec(space) for _, space in operands] + [spec()] * len(tokens),
-        out_specs=(spec(),) * (len(outs) + emit),
+        out_specs=(spec(space),) * len(outs) + (spec(),) * emit,
         scratch_shapes=list(scratch),
         compiler_params=params(mebibytes),
         cost_estimate=pl.CostEstimate(
@@ -391,14 +391,15 @@
 
 
 TURNS = (2, 1, 3, 0)
+ORDER = (0, 2, 1, 3)
 SPLIT = 2
 WIDTH = QUARTER // SPLIT
 
 
 def decode_kernel(length_hbm, query_hbm, step_hbm, cache_hbm, weight_hbm, *refs):
     outs = refs[:4]
-    length_ref, query_ref, step_ref, cache_ref, weight_ref = refs[4:9]
-    attended_ref, score_ref, mixed_ref, row_sems, cache_sems, weight_sems = refs[9:]
+    length_ref, query_ref, step_ref, cache_ref, weight_ref, own_ref, part_ref = refs[4:11]
+    attended_ref, score_ref, mixed_ref, row_sems, cache_sems, weight_sems, out_sems = refs[11:]
     firsts = [
         pltpu.make_async_copy(query_hbm, query_ref, row_sems.at[0]),
         pltpu.make_async_copy(step_hbm, step_ref, row_sems.at[1]),
@@ -417,7 +418,7 @@
     y = lax.axis_index("tp") // 4
     copies = []
     for number in range(4 * SPLIT):
-        column = (y + TURNS[number // SPLIT]) % 4 * QUARTER + number % SPLIT * WIDTH
+        column = (y + ORDER[number // SPLIT]) % 4 * QUARTER + number % SPLIT * WIDTH
         copies.append(
             pltpu.make_async_copy(
                 weight_hbm.at[:, pl.ds(pl.multiple_of(column, WIDTH), WIDTH)],
@@ -433,12 +434,22 @@
         length_ref, query_ref, step_ref, cache_ref, attended_ref, score_ref, mixed_ref, waits
     )
     attended = attended_ref[...]
+    leaving = []
     for number, copy in enumerate(copies):
         copy.wait()
         part = dot(attended, weight_ref[number])
-        out = outs[number // SPLIT]
+        quarter = number // SPLIT
         columns = slice(number % SPLIT * WIDTH, (number % SPLIT + 1) * WIDTH)
-        out[:, columns] = part.astype(out.dtype)
+        if quarter == 0:
+            own_ref[:, columns] = part
+        else:
+            part_ref[quarter - 1, :, columns] = part.astype(BF16)
+        if number % SPLIT == SPLIT - 1:
+            source = own_ref if quarter == 0 else part_ref.at[quarter - 1]
+            leaving.append(pltpu.make_async_copy(source, outs[quarter], out_sems.at[quarter]))
+            leaving[-1].start()
+    for copy in leaving:
+        copy.wait()
 
 
 def decode(row_lengths, step_query, step_cache, row_cache, out_weight):
@@ -449,7 +460,7 @@
         "decode",
         58,
         None,
-        [shape((rows, QUARTER), BF16 if turn else F32) for turn in TURNS],
+        [shape((rows, QUARTER), BF16 if turn else F32) for turn in ORDER],
         [(a, pl.ANY) for a in operands],
         [
             pltpu.SMEM((1, ROWS), jnp.int32),
@@ -457,14 +468,19 @@
             pltpu.VMEM(step_cache.shape, BF16),
             pltpu.VMEM(row_cache.shape, BF16),
             pltpu.VMEM((4 * SPLIT, out_weight.shape[0], WIDTH), BF16),
+            pltpu.VMEM((rows, QUARTER), F32),
+            pltpu.VMEM((3, rows, QUARTER), BF16),
             pltpu.VMEM((rows, HEADS * HEAD_SIZE), BF16),
             pltpu.VMEM((HEADS * rows, LEN), F32),
             pltpu.VMEM((HEADS * rows, HEAD_SIZE), F32),
             pltpu.SemaphoreType.DMA((3,)),
             pltpu.SemaphoreType.DMA((4,)),
             pltpu.SemaphoreType.DMA((4 * SPLIT,)),
+            pltpu.SemaphoreType.DMA((4,)),
         ],
         cost=9,
+        emit=False,
+        space=pl.ANY,
     )
 
 
@@ -472,16 +488,17 @@
     z = lax.axis_index("tp") % 4
     for out, turn in zip(outs, TURNS):
         columns = pl.ds(pl.multiple_of((z + turn) % 4 * SHARE, SHARE), SHARE)
-        out[...] = (
+        total = (
             own_ref[:, columns]
             + a_ref[:, columns].astype(F32)
             + b_ref[:, columns].astype(F32)
             + c_ref[:, columns].astype(F32)
         )
+        out[...] = total.astype(out.dtype)
 
 
 def sum_quarters(own, came, token):
-    outs = [shape((STEPS * ROWS, SHARE), F32) for _ in TURNS]
+    outs = [shape((STEPS * ROWS, SHARE), BF16 if turn == 2 else F32) for turn in TURNS]
     operands = [(a, VMEM) for a in (own, *came)]
     return run(quarter_kernel, "quarters", 4, token, outs, operands, cost=4)
 
@@ -493,7 +510,9 @@
 
 def hidden_kernel(residual_ref, own_ref, a_ref, b_ref, c_ref, hidden_ref, square_ref):
     residual = residual_ref[0].reshape(STEPS * ROWS, SHARE).astype(F32)
-    hidden = residual + (own_ref[...] + a_ref[...] + b_ref[...] + c_ref[...])
+    hidden = residual + (
+        own_ref[...] + a_ref[...].astype(F32) + b_ref[...] + c_ref[...]
+    )
     hidden_ref[...] = hidden
     square = jnp.sum(hidden * hidden, axis=1, keepdims=True)
     square = jnp.sum(jnp.where(diagonal(), square, 0.0), axis=0, keepdims=True)
@@ -503,7 +522,7 @@
 def sum_shares(residual, own, came, token):
     outs = [shape((STEPS * ROWS, SHARE), F32), shape((16, 8, HEAD_SIZE), F32)]
     operands = [(a, VMEM) for a in (residual, own, *came)]
-    return run(hidden_kernel, "hidden", 4, token, outs, operands)
+    return run(hidden_kernel, "hidden", 4, token, outs, operands, cost=4)
 
 
 def finish_kernel(hidden_ref, gain_ref, square_ref, out_ref):
@@ -553,11 +572,11 @@
     )
     near = lax.ppermute(packed, "tp", [(i, i ^ 1) for i in range(16)])
     far = lax.ppermute(packed, "blk", [(i, i ^ 4) for i in range(8)])
-    *parts, own, token = decode(row_lengths, step_query, step_cache, row_cache, out_weight)
+    own, *parts = decode(row_lengths, step_query, step_cache, row_cache, out_weight)
     far, parts[0] = lax.optimization_barrier((far, parts[0]))
     far_near = lax.ppermute(far, "tp", [(i, i ^ 1) for i in range(16)])
     came = [move_y(a, turn) for a, turn in zip(parts, TURNS)]
-    here, token = join(packed, near, far, far_near, token)
+    here, token = join(packed, near, far, far_near, None)
     up = move_x(here, 1)
     down = move_x(here, 3)
     *state, token = attend(
@@ -572,11 +591,11 @@
     )
     *shares, own, token = sum_quarters(own, came, token)
     came = [move_z(a, turn) for a, turn in zip(shares, TURNS)]
+    places = [(0, 0, 0, -1), (0, PIECE, 1, -1)]
+    *state, token = attend(block_offset, prompt_query, [up], places, state, False, token)
     up_two, down_two, token = relay(up, down, token)
     up_two = move_x(up_two, 1)
     down_two = move_x(down_two, 3)
-    places = [(0, 0, 0, -1), (0, PIECE, 1, -1), (1, 0, 0, 1), (1, PIECE, 1, 1)]
-    *state, token = attend(block_offset, prompt_query, [up, down], places, state, False, token)
     hidden, square, token = sum_shares(residual, own, came, token)
     squares = lax.all_to_all(square, "tp", split_axis=0, concat_axis=0, tiled=True)
     places = [(0, 0, 0, 0), (0, PIECE, 1, 0), (1, 0, 0, -1), (1, PIECE, 1, -1)]
@@ -586,8 +605,8 @@
     prefill_out, token = attend(
         block_offset,
         prompt_query,
-        [up_two, down_two],
-        [(0, 0, 0, 2), (1, 0, 1, 2)],
+        [down, up_two, down_two],
+        [(0, 0, 0, 1), (0, PIECE, 1, 1), (1, 0, 0, 2), (2, 0, 1, 2)],
         state,
         True,
         token,

time: 61.6 us -> 60.6 us (0.984)
  starting transfers between devices: 29.3 us -> 26.9 us
  waiting for transfers between devices: 7.01 us -> 8.76 us
  local copies, waits for them, and re-layouts: 2.82 us -> 2.13 us
    ppermute x3, waiting for transfers between devices: 0.01 us -> 2.29 us  [move_z(): lax.ppermute(a, 'tp', [(i, i // 4 * 4 + (i + turn) % 4) for i in range(16)])]
    ppermute x3, starting transfers between devices: 5.38 us -> 3.9 us  [move_z(): lax.ppermute(a, 'tp', [(i, i // 4 * 4 + (i + turn) % 4) for i in range(16)])]
    all_to_all x1, waiting for transfers between devices: 2.74 us -> 1.52 us  [body(): lax.all_to_all(square, 'tp', split_axis=0, concat_axis=0, tiled=True)]
    all_to_all x1, starting transfers between devices: 5.05 us -> 4.12 us  [body(): lax.all_to_all(square, 'tp', split_axis=0, concat_axis=0, tiled=True)]
    ppermute x3, waiting for transfers between devices: 4.23 us -> 4.92 us  [move_y(): return lax.ppermute(a, 'tp', [(i, (i + 4 * turn) % 16) for i in range(16)])]
    unnamed x20 -> x18, local copies, waits for them, and re-layouts: 2.82 us -> 2.13 us
  transfers between devices with their start and end apart: 15 -> 15, of which waited for: 2 -> 4; matrix products, arithmetic and copies ran while one was open for 0% -> 0% of each run, Pallas kernels for 31% -> 32%
where the time goes in v5:
time: 60.6 us; the launch traced here: 59.9 us
  starting transfers between devices  26.9 us (44%)
  Pallas kernels  21.2 us (35%)
  waiting for transfers between devices  8.76 us (14%)
  local copies, waits for them, and re-layouts  2.13 us (4%)
  between operations  0.82 us (1%)
    pallas_call x12, Pallas kernels, run(): pl.pallas_call(with_token, out_shape=(*outs, TOKEN) if emit else tuple(ou...  21.2 us
    ppermute x1, starting transfers between devices, body(): far = lax.ppermute(packed, 'blk', [(i, i ^ 4) for i in range(8)])  7.28 us
    ppermute x3, starting transfers between devices, move_y(): return lax.ppermute(a, 'tp', [(i, (i + 4 * turn) % 16) for i in range(16)])  5.22 us
    ppermute x3, waiting for transfers between devices, move_y(): return lax.ppermute(a, 'tp', [(i, (i + 4 * turn) % 16) for i in range(16)])  4.92 us
    ppermute x4, starting transfers between devices, move_x(): lax.ppermute(a, 'blk', [(i, i // 4 * 4 + (i + turn) % 4) for i in range(8)])  4.21 us
    all_to_all x1, starting transfers between devices, body(): lax.all_to_all(square, 'tp', split_axis=0, concat_axis=0, tiled=True)  4.12 us
    ppermute x3, starting transfers between devices, move_z(): lax.ppermute(a, 'tp', [(i, i // 4 * 4 + (i + turn) % 4) for i in range(16)])  3.9 us
    ppermute x3, waiting for transfers between devices, move_z(): lax.ppermute(a, 'tp', [(i, i // 4 * 4 + (i + turn) % 4) for i in range(16)])  2.29 us
  transfers between devices with their start and end apart: 15, of which 4 were waited for; matrix products, arithmetic and copies ran while one was open for 0% of the time, Pallas kernels for 32%

profile of v5, /device:TPU:6, one launch (start us, length us, event | category | flops | bytes accessed | tf_op | source)
XLA Modules:
  0.0 59.9 jit_solution(5220971184792435404)
XLA Ops:
  0.6 1.6 %pack.1.refs_0_ = bf16[272,256]{1,0:T(8,128)(2,1)} custom-call(s32[1,16]{1,0:T(1,128)} %bitcast.6, bf16[1,2,64,256]{3,2,1,0:T(8,128)(2,1)} %bitcast.4, bf16[1,2,64,256]{3,2,1,0:T(8,128)(2,1)} %bitcast.5), custom_call_target="tpu_custom_call" | custom-call | flops 1024 | bytes 1024 | tf_op jit(solution)/shard_map/pack/pallas_call | solution.py:72
  2.2 0.0 copy-start
  2.2 0.0 copy-start.2
  2.2 0.0 copy-start.4
  2.3 7.3 %collective-permute-start.1 = (bf16[272,256]{1,0:T(8,128)(2,1)}, bf16[272,256]{1,0:T(8,128)(2,1)S(1)}, u32[]{:S(2)}, u32[]{:S(2)}) collective-permute-start(bf16[272,256]{1,0:T(8,128)(2,1)} %pack.1.refs_0_), channel_id=1, source_target_pairs={{0,128},{32,160},{64,192},{96,224},{128,0},{160,32},{192,64},{224,... | collective-permute-start | bytes 417800 | tf_op jit(solution)/shard_map/ppermute | solution.py:574
  9.5 1.0 %collective-permute-start = (bf16[272,256]{1,0:T(8,128)(2,1)}, bf16[272,256]{1,0:T(8,128)(2,1)S(1)}, u32[]{:S(2)}, u32[]{:S(2)}) collective-permute-start(bf16[272,256]{1,0:T(8,128)(2,1)} %pack.1.refs_0_), channel_id=1, source_target_pairs={{0,1},{1,0},{2,3},{3,2},{4,5},{5,4},{6,7},{7,6},{8,9},{9,8},{10,11... | collective-permute-start | bytes 417800 | tf_op jit(solution)/shard_map/ppermute | solution.py:573
  10.5 8.3 %decode.1 = (f32[64,2048]{1,0:T(8,128)}, bf16[64,2048]{1,0:T(8,128)(2,1)}, bf16[64,2048]{1,0:T(8,128)(2,1)}, bf16[64,2048]{1,0:T(8,128)(2,1)}) custom-call(s32[1,16]{1,0:T(1,128)} %refs_0_.5, bf16[1,4,16,512]{3,2,1,0:T(8,128)(2,1)} %refs_1_.5, bf16[1,4,2,16,128]{4,3,2,1,0:T(8,128)(2,1)} %refs_2_.1, bf16[1,2,16,256,128]{4,3,2,1,0:T(8,128)(2,1)} %refs_3_.1, ...), custom_call_target="tpu_custom_call" | custom-call | flops 10350001152 | bytes 1024 | tf_op jit(solution)/shard_map/decode/pallas_call | solution.py:72
  18.8 0.0 copy-start.8
  18.8 0.0 collective-permute-done.1.refs_2_
  18.9 1.1 %collective-permute-start.2 = (bf16[272,256]{1,0:T(8,128)(2,1)S(1)}, bf16[272,256]{1,0:T(8,128)(2,1)S(1)}, u32[]{:S(2)}, u32[]{:S(2)}) collective-permute-start(bf16[272,256]{1,0:T(8,128)(2,1)S(1)} %collective-permute-done.1.refs_2_), channel_id=1, source_target_pairs={{0,1},{1,0},{2,3},{3,2},{4,5},{5,4},{6,7},{7,6},{8,9},{9,8},{10,11... | collective-permute-start | bytes 417800 | tf_op jit(solution)/shard_map/ppermute | solution.py:577
  19.9 1.6 %collective-permute-start.6 = (bf16[64,2048]{1,0:T(8,128)(2,1)}, bf16[64,2048]{1,0:T(8,128)(2,1)S(1)}, u32[]{:S(2)}, u32[]{:S(2)}) collective-permute-start(bf16[64,2048]{1,0:T(8,128)(2,1)} %get-tuple-element.44), channel_id=1, source_target_pairs={{0,4},{1,5},{2,6},{3,7},{4,8},{5,9},{6,10},{7,11},{8,12},{9,13},{1... | collective-permute-start | bytes 786440 | tf_op jit(solution)/shard_map/ppermute | solution.py:547
  21.5 1.7 %collective-permute-start.7 = (bf16[64,2048]{1,0:T(8,128)(2,1)}, bf16[64,2048]{1,0:T(8,128)(2,1)S(1)}, u32[]{:S(2)}, u32[]{:S(2)}) collective-permute-start(bf16[64,2048]{1,0:T(8,128)(2,1)} %get-tuple-element.45), channel_id=1, source_target_pairs={{0,12},{1,13},{2,14},{3,15},{4,0},{5,1},{6,2},{7,3},{8,4},{9,5},{1... | collective-permute-start | bytes 786440 | tf_op jit(solution)/shard_map/ppermute | solution.py:547
  23.2 2.0 %collective-permute-start.5 = (bf16[64,2048]{1,0:T(8,128)(2,1)}, bf16[64,2048]{1,0:T(8,128)(2,1)S(1)}, u32[]{:S(2)}, u32[]{:S(2)}) collective-permute-start(bf16[64,2048]{1,0:T(8,128)(2,1)} %get-tuple-element.43), channel_id=1, source_target_pairs={{0,8},{1,9},{2,10},{3,11},{4,12},{5,13},{6,14},{7,15},{8,0},{9,1},... | collective-permute-start | bytes 786440 | tf_op jit(solution)/shard_map/ppermute | solution.py:547
  25.2 0.0 collective-permute-done.refs_1_
  25.2 0.0 collective-permute-done.2.refs_3_
  25.2 0.0 copy-done
  25.2 0.6 collective-permute-start.4
  25.8 1.5 %collective-permute-start.3 = (bf16[1056,256]{1,0:T(8,128)(2,1)S(1)}, bf16[1056,256]{1,0:T(8,128)(2,1)S(1)}, u32[]{:S(2)}, u32[]{:S(2)}) collective-permute-start(bf16[1056,256]{1,0:T(8,128)(2,1)S(1)} %get-tuple-element.38.refs_2_.refs_0_), channel_id=1, source_target_pairs={{0,96},{32,0},{64,32},{96,64},{128,224},{160,128},{192,160},{224,1... | collective-permute-start | bytes 1622024 | tf_op jit(solution)/shard_map/ppermute | solution.py:543
  27.3 0.0 copy-done.2
  27.3 0.0 copy-done.4
  27.3 0.0 copy-start.7
  27.4 1.0 %copy-done.7 = f32[64,2048]{1,0:T(8,128)S(1)} copy-done((f32[64,2048]{1,0:T(8,128)S(1)}, f32[64,2048]{1,0:T(8,128)}, u32[]{:S(2)}) %copy-start.7) | copy-done | bytes 524312
  28.4 2.1 %attend.3 = (f32[4,8,256]{2,1,0:T(8,128)S(1)}, f32[4,144,256]{2,1,0:T(8,128)S(1)}, f32[8,128]{1,0:T(8,128)S(1)}) custom-call(s32[2]{0:T(128)S(1)} %copy-done.4, bf16[1,256,512]{2,1,0:T(8,128)(2,1)S(1)} %copy-done.2, bf16[1056,256]{1,0:T(8,128)(2,1)S(1)} %get-tuple-element.38.refs_2_.refs_0_, f32[64,2048]{1,0:T(8,128)S(1)} %copy-done.7, ...), custom_call_target="tpu_custom_call" | custom-call | flops 3450000896 | bytes 1024 | tf_op jit(solution)/shard_map/attend/pallas_call | solution.py:72
  30.5 0.0 collective-permute-done.6.refs_2_
  30.5 0.5 collective-permute-done.7.refs_3_
  31.0 4.5 %collective-permute-done.5.refs_1_ = bf16[64,2048]{1,0:T(8,128)(2,1)S(1)} collective-permute-done((bf16[64,2048]{1,0:T(8,128)(2,1)}, bf16[64,2048]{1,0:T(8,128)(2,1)S(1)}, u32[]{:S(2)}, u32[]{:S(2)}) %collective-permute-start.5) | collective-permute-done | bytes 262176 | tf_op jit(solution)/shard_map/ppermute | solution.py:547
  35.4 0.0 copy-done.8
  35.4 0.1 quarters.1
  35.5 1.1 %collective-permute-start.11 = (f32[64,512]{1,0:T(8,128)S(1)}, f32[64,512]{1,0:T(8,128)S(1)}, u32[]{:S(2)}, u32[]{:S(2)}) collective-permute-start(f32[64,512]{1,0:T(8,128)S(1)} %get-tuple-element.55), channel_id=1, source_target_pairs={{0,1},{1,2},{2,3},{3,0},{4,5},{5,6},{6,7},{7,4},{8,9},{9,10},{10,1... | collective-permute-start | bytes 393224 | tf_op jit(solution)/shard_map/ppermute | solution.py:551
  36.7 2.8 %collective-permute-start.12 = (f32[64,512]{1,0:T(8,128)S(1)}, f32[64,512]{1,0:T(8,128)S(1)}, u32[]{:S(2)}, u32[]{:S(2)}) collective-permute-start(f32[64,512]{1,0:T(8,128)S(1)} %get-tuple-element.56), channel_id=1, source_target_pairs={{0,3},{1,0},{2,1},{3,2},{4,7},{5,4},{6,5},{7,6},{8,11},{9,8},{10,9... | collective-permute-start | bytes 393224 | tf_op jit(solution)/shard_map/ppermute | solution.py:551
  39.5 0.0 collective-permute-start.10
  39.5 0.0 collective-permute-done.4.refs_2_.refs_0_.refs_1_
  39.5 0.0 copy-start.3
  39.5 2.1 %attend.4 = (f32[4,8,256]{2,1,0:T(8,128)S(1)}, f32[4,144,256]{2,1,0:T(8,128)S(1)}, f32[8,128]{1,0:T(8,128)S(1)}) custom-call(s32[2]{0:T(128)S(1)} %copy-done.4, bf16[1,256,512]{2,1,0:T(8,128)(2,1)S(1)} %copy-done.2, bf16[1056,256]{1,0:T(8,128)(2,1)S(1)} %collective-permute-done.4.refs_2_.refs_0_.refs_1_, f32[4,8,256]{2,1,0:T(8,128)S(1)} %get-tuple-element.41.refs_3_, ...), custom_call_target="tpu_custom_call" | custom-call | flops 3450000896 | bytes 1024 | tf_op jit(solution)/shard_map/attend/pallas_call | solution.py:72
  41.6 0.0 copy-start.5
  41.6 0.0 collective-permute-done.3.refs_1_.refs_2_
  41.7 0.6 collective-permute-start.8
  42.2 1.5 %collective-permute-start.9 = (bf16[528,256]{1,0:T(8,128)(2,1)S(1)}, bf16[528,256]{1,0:T(8,128)(2,1)S(1)}, u32[]{:S(2)}, u32[]{:S(2)}) collective-permute-start(bf16[528,256]{1,0:T(8,128)(2,1)S(1)} %get-tuple-element.50), channel_id=1, source_target_pairs={{0,96},{32,0},{64,32},{96,64},{128,224},{160,128},{192,160},{224,1... | collective-permute-start | bytes 811016 | tf_op jit(solution)/shard_map/ppermute | solution.py:543
  43.8 2.3 %collective-permute-done.10.refs_2_ = bf16[64,512]{1,0:T(8,128)(2,1)S(1)} collective-permute-done((bf16[64,512]{1,0:T(8,128)(2,1)S(1)}, bf16[64,512]{1,0:T(8,128)(2,1)S(1)}, u32[]{:S(2)}, u32[]{:S(2)}) %collective-permute-start.10) | collective-permute-done | bytes 65568 | tf_op jit(solution)/shard_map/ppermute | solution.py:551
  46.1 0.0 collective-permute-done.11.refs_3_
  46.1 0.0 collective-permute-done.12.refs_4_
  46.1 0.0 copy-done.3
  46.1 0.8 %hidden.1 = (f32[64,512]{1,0:T(8,128)S(1)}, f32[16,8,128]{2,1,0:T(8,128)}, f32[8,128]{1,0:T(8,128)S(1)}) custom-call(bf16[1,4,16,512]{3,2,1,0:T(8,128)(2,1)S(1)} %copy-done.3, f32[64,512]{1,0:T(8,128)S(1)} %get-tuple-element.53.refs_1_, bf16[64,512]{1,0:T(8,128)(2,1)S(1)} %collective-permute-done.10.refs_2_, f32[64,512]{1,0:T(8,128)S(1)} %collective-permute-done.11.refs_3_, ...), custom_call_target="tpu_custom_call" | custom-call | flops 4600001024 | bytes 1024 | tf_op jit(solution)/shard_map/hidden/pallas_call | solution.py:72
  46.8 0.0 copy-done.5
  46.9 0.0 copy-start.1
  46.9 4.1 %all-to-all-start = ((f32[16,8,128]{2,1,0:T(8,128)}), f32[16,8,128]{2,1,0:T(8,128)S(1)}, u32[]{:S(2)}, u32[]{:S(2)}) async-start(f32[16,8,128]{2,1,0:T(8,128)} %get-tuple-element.66), calls=%async_computation | async-start | bytes 131072 | tf_op jit(solution)/shard_map/all_to_all | solution.py:600
  51.0 0.0 collective-permute-done.8.refs_3_
  51.0 0.0 collective-permute-done.9.refs_4_
  51.0 0.5 pages.1
  51.5 0.1 collective-permute-start.13
  51.6 0.0 copy-start.6
  51.6 1.1 %copy-done.6 = f32[4,144,256]{2,1,0:T(8,128)S(1)} copy-done((f32[4,144,256]{2,1,0:T(8,128)S(1)}, f32[4,144,256]{2,1,0:T(8,128)}, u32[]{:S(2)}) %copy-start.6) | copy-done | bytes 589848
  52.7 4.2 %attend.5 = (bf16[1,256,512]{2,1,0:T(8,128)(2,1)}, f32[8,128]{1,0:T(8,128)S(1)}) custom-call(s32[2]{0:T(128)S(1)} %copy-done.4, bf16[1,256,512]{2,1,0:T(8,128)(2,1)S(1)} %copy-done.2, bf16[1056,256]{1,0:T(8,128)(2,1)S(1)} %collective-permute-done.3.refs_1_.refs_2_, bf16[528,256]{1,0:T(8,128)(2,1)S(1)} %collective-permute-done.8.refs_3_, ...), custom_call_target="tpu_custom_call" | custom-call | flops 3450000896 | bytes 1024 | tf_op jit(solution)/shard_map/attend/pallas_call | solution.py:72
  56.9 0.0 collective-permute-done.13.refs_1_
  56.9 0.7 %pool.1 = (bf16[8,2,2,2,16,128]{5,4,3,2,1,0:T(8,128)(2,1)}, f32[8,128]{1,0:T(8,128)S(1)}) custom-call(bf16[8,2,2,16,128]{4,3,2,1,0:T(8,128)(2,1)S(1)} %get-tuple-element.61.refs_0_, bf16[8,2,2,16,128]{4,3,2,1,0:T(8,128)(2,1)S(1)} %collective-permute-done.13.refs_1_, f32[8,128]{1,0:T(8,128)S(1)} %get-tuple-element.63.refs_2_), custom_call_target="tpu_custom_call" | custom-call | flops 1024 | bytes 1024 | tf_op jit(solution)/shard_map/pool/pallas_call | solution.py:72
  57.6 1.5 %all-to-all-done.refs_2_ = f32[16,8,128]{2,1,0:T(8,128)S(1)} async-done(((f32[16,8,128]{2,1,0:T(8,128)}), f32[16,8,128]{2,1,0:T(8,128)S(1)}, u32[]{:S(2)}, u32[]{:S(2)}) %all-to-all-start) | async-done | bytes 65568 | tf_op jit(solution)/shard_map/all_to_all | solution.py:600
  59.1 0.0 copy-done.1
  59.1 0.7 %finish.1 = (bf16[1,4,16,512]{3,2,1,0:T(8,128)(2,1)}, f32[8,128]{1,0:T(8,128)}) custom-call(f32[64,512]{1,0:T(8,128)S(1)} %get-tuple-element.65.refs_0_, bf16[512]{0:T(512)(128)(2,1)S(1)} %copy-done.1, f32[16,8,128]{2,1,0:T(8,128)S(1)} %all-to-all-done.refs_2_, f32[8,128]{1,0:T(8,128)S(1)} %get-tuple-element.67.refs_3_), custom_call_target="tpu_custom_call" | custom-call | flops 1024 | bytes 1024 | tf_op jit(solution)/shard_map/finish/pallas_call | solution.py:72
  (2 shorter events, 0.1 us)
Async XLA Ops:
  2.2 23.0 %copy-start = (bf16[272,256]{1,0:T(8,128)(2,1)S(1)}, bf16[272,256]{1,0:T(8,128)(2,1)}, u32[]{:S(2)}) copy-start(bf16[272,256]{1,0:T(8,128)(2,1)} %pack.1.refs_0_) | copy-start | bytes 417796
  2.2 25.1 %copy-start.2 = (bf16[1,256,512]{2,1,0:T(8,128)(2,1)S(1)}, bf16[1,256,512]{2,1,0:T(8,128)(2,1)}, u32[]{:S(2)}) copy-start(bf16[1,256,512]{2,1,0:T(8,128)(2,1)} %refs_1_.8) | copy-start | bytes 786436
  2.2 25.1 %copy-start.4 = (s32[2]{0:T(128)S(1)}, s32[2]{0:T(128)}, u32[]{:S(2)}) copy-start(s32[2]{0:T(128)} %refs_0_.9) | copy-start | bytes 28
  2.3 16.6 %collective-permute-start.1 = (bf16[272,256]{1,0:T(8,128)(2,1)}, bf16[272,256]{1,0:T(8,128)(2,1)S(1)}, u32[]{:S(2)}, u32[]{:S(2)}) collective-permute-start(bf16[272,256]{1,0:T(8,128)(2,1)} %pack.1.refs_0_), channel_id=1, source_target_pairs={{0,128},{32,160},{64,192},{96,224},{128,0},{160,32},{192,64},{224,... | collective-permute-start | bytes 417800 | tf_op jit(solution)/shard_map/ppermute | solution.py:574
  9.5 15.6 %collective-permute-start = (bf16[272,256]{1,0:T(8,128)(2,1)}, bf16[272,256]{1,0:T(8,128)(2,1)S(1)}, u32[]{:S(2)}, u32[]{:S(2)}) collective-permute-start(bf16[272,256]{1,0:T(8,128)(2,1)} %pack.1.refs_0_), channel_id=1, source_target_pairs={{0,1},{1,0},{2,3},{3,2},{4,5},{5,4},{6,7},{7,6},{8,9},{9,8},{10,11... | collective-permute-start | bytes 417800 | tf_op jit(solution)/shard_map/ppermute | solution.py:573
  18.8 16.6 %copy-start.8 = (f32[64,2048]{1,0:T(8,128)S(1)}, f32[64,2048]{1,0:T(8,128)}, u32[]{:S(2)}) copy-start(f32[64,2048]{1,0:T(8,128)} %get-tuple-element.39.refs_3_.refs_0_) | copy-start | bytes 1572868
  18.9 6.3 %collective-permute-start.2 = (bf16[272,256]{1,0:T(8,128)(2,1)S(1)}, bf16[272,256]{1,0:T(8,128)(2,1)S(1)}, u32[]{:S(2)}, u32[]{:S(2)}) collective-permute-start(bf16[272,256]{1,0:T(8,128)(2,1)S(1)} %collective-permute-done.1.refs_2_), channel_id=1, source_target_pairs={{0,1},{1,0},{2,3},{3,2},{4,5},{5,4},{6,7},{7,6},{8,9},{9,8},{10,11... | collective-permute-start | bytes 417800 | tf_op jit(solution)/shard_map/ppermute | solution.py:577
  19.9 10.6 %collective-permute-start.6 = (bf16[64,2048]{1,0:T(8,128)(2,1)}, bf16[64,2048]{1,0:T(8,128)(2,1)S(1)}, u32[]{:S(2)}, u32[]{:S(2)}) collective-permute-start(bf16[64,2048]{1,0:T(8,128)(2,1)} %get-tuple-element.44), channel_id=1, source_target_pairs={{0,4},{1,5},{2,6},{3,7},{4,8},{5,9},{6,10},{7,11},{8,12},{9,13},{1... | collective-permute-start | bytes 786440 | tf_op jit(solution)/shard_map/ppermute | solution.py:547
  21.5 9.5 %collective-permute-start.7 = (bf16[64,2048]{1,0:T(8,128)(2,1)}, bf16[64,2048]{1,0:T(8,128)(2,1)S(1)}, u32[]{:S(2)}, u32[]{:S(2)}) collective-permute-start(bf16[64,2048]{1,0:T(8,128)(2,1)} %get-tuple-element.45), channel_id=1, source_target_pairs={{0,12},{1,13},{2,14},{3,15},{4,0},{5,1},{6,2},{7,3},{8,4},{9,5},{1... | collective-permute-start | bytes 786440 | tf_op jit(solution)/shard_map/ppermute | solution.py:547
  23.2 12.2 %collective-permute-start.5 = (bf16[64,2048]{1,0:T(8,128)(2,1)}, bf16[64,2048]{1,0:T(8,128)(2,1)S(1)}, u32[]{:S(2)}, u32[]{:S(2)}) collective-permute-start(bf16[64,2048]{1,0:T(8,128)(2,1)} %get-tuple-element.43), channel_id=1, source_target_pairs={{0,8},{1,9},{2,10},{3,11},{4,12},{5,13},{6,14},{7,15},{8,0},{9,1},... | collective-permute-start | bytes 786440 | tf_op jit(solution)/shard_map/ppermute | solution.py:547
  25.2 14.2 %collective-permute-start.4 = (bf16[1056,256]{1,0:T(8,128)(2,1)S(1)}, bf16[1056,256]{1,0:T(8,128)(2,1)S(1)}, u32[]{:S(2)}, u32[]{:S(2)}) collective-permute-start(bf16[1056,256]{1,0:T(8,128)(2,1)S(1)} %get-tuple-element.38.refs_2_.refs_0_), channel_id=1, source_target_pairs={{0,32},{32,64},{64,96},{96,0},{128,160},{160,192},{192,224},{224,1... | collective-permute-start | bytes 1622024 | tf_op jit(solution)/shard_map/ppermute | solution.py:543
  25.8 15.8 %collective-permute-start.3 = (bf16[1056,256]{1,0:T(8,128)(2,1)S(1)}, bf16[1056,256]{1,0:T(8,128)(2,1)S(1)}, u32[]{:S(2)}, u32[]{:S(2)}) collective-permute-start(bf16[1056,256]{1,0:T(8,128)(2,1)S(1)} %get-tuple-element.38.refs_2_.refs_0_), channel_id=1, source_target_pairs={{0,96},{32,0},{64,32},{96,64},{128,224},{160,128},{192,160},{224,1... | collective-permute-start | bytes 1622024 | tf_op jit(solution)/shard_map/ppermute | solution.py:543
  27.3 1.0 %copy-start.7 = (f32[64,2048]{1,0:T(8,128)S(1)}, f32[64,2048]{1,0:T(8,128)}, u32[]{:S(2)}) copy-start(f32[64,2048]{1,0:T(8,128)} %get-tuple-element.39.refs_3_.refs_0_) | copy-start | bytes 1572868
  35.5 10.5 %collective-permute-start.11 = (f32[64,512]{1,0:T(8,128)S(1)}, f32[64,512]{1,0:T(8,128)S(1)}, u32[]{:S(2)}, u32[]{:S(2)}) collective-permute-start(f32[64,512]{1,0:T(8,128)S(1)} %get-tuple-element.55), channel_id=1, source_target_pairs={{0,1},{1,2},{2,3},{3,0},{4,5},{5,6},{6,7},{7,4},{8,9},{9,10},{10,1... | collective-permute-start | bytes 393224 | tf_op jit(solution)/shard_map/ppermute | solution.py:551
  36.7 9.4 %collective-permute-start.12 = (f32[64,512]{1,0:T(8,128)S(1)}, f32[64,512]{1,0:T(8,128)S(1)}, u32[]{:S(2)}, u32[]{:S(2)}) collective-permute-start(f32[64,512]{1,0:T(8,128)S(1)} %get-tuple-element.56), channel_id=1, source_target_pairs={{0,3},{1,0},{2,1},{3,2},{4,7},{5,4},{6,5},{7,6},{8,11},{9,8},{10,9... | collective-permute-start | bytes 393224 | tf_op jit(solution)/shard_map/ppermute | solution.py:551
  39.5 6.6 %collective-permute-start.10 = (bf16[64,512]{1,0:T(8,128)(2,1)S(1)}, bf16[64,512]{1,0:T(8,128)(2,1)S(1)}, u32[]{:S(2)}, u32[]{:S(2)}) collective-permute-start(bf16[64,512]{1,0:T(8,128)(2,1)S(1)} %get-tuple-element.54), channel_id=1, source_target_pairs={{0,2},{1,3},{2,0},{3,1},{4,6},{5,7},{6,4},{7,5},{8,10},{9,11},{10,... | collective-permute-start | bytes 196616 | tf_op jit(solution)/shard_map/ppermute | solution.py:551
  39.5 6.6 %copy-start.3 = (bf16[1,4,16,512]{3,2,1,0:T(8,128)(2,1)S(1)}, bf16[1,4,16,512]{3,2,1,0:T(8,128)(2,1)}, u32[]{:S(2)}) copy-start(bf16[1,4,16,512]{3,2,1,0:T(8,128)(2,1)} %refs_0_.8) | copy-start | bytes 196612
  41.6 5.2 %copy-start.5 = (f32[4,144,256]{2,1,0:T(8,128)}, f32[4,144,256]{2,1,0:T(8,128)S(1)}, u32[]{:S(2)}) copy-start(f32[4,144,256]{2,1,0:T(8,128)S(1)} %get-tuple-element.52.refs_6_) | copy-start | bytes 1769476
  41.7 9.3 %collective-permute-start.8 = (bf16[528,256]{1,0:T(8,128)(2,1)S(1)}, bf16[528,256]{1,0:T(8,128)(2,1)S(1)}, u32[]{:S(2)}, u32[]{:S(2)}) collective-permute-start(bf16[528,256]{1,0:T(8,128)(2,1)S(1)} %get-tuple-element.49), channel_id=1, source_target_pairs={{0,32},{32,64},{64,96},{96,0},{128,160},{160,192},{192,224},{224,1... | collective-permute-start | bytes 811016 | tf_op jit(solution)/shard_map/ppermute | solution.py:543
  42.2 8.8 %collective-permute-start.9 = (bf16[528,256]{1,0:T(8,128)(2,1)S(1)}, bf16[528,256]{1,0:T(8,128)(2,1)S(1)}, u32[]{:S(2)}, u32[]{:S(2)}) collective-permute-start(bf16[528,256]{1,0:T(8,128)(2,1)S(1)} %get-tuple-element.50), channel_id=1, source_target_pairs={{0,96},{32,0},{64,32},{96,64},{128,224},{160,128},{192,160},{224,1... | collective-permute-start | bytes 811016 | tf_op jit(solution)/shard_map/ppermute | solution.py:543
  46.9 12.3 %copy-start.1 = (bf16[512]{0:T(512)(128)(2,1)S(1)}, bf16[512]{0:T(512)(128)(2,1)}, u32[]{:S(2)}) copy-start(bf16[512]{0:T(512)(128)(2,1)} %refs_1_.9) | copy-start | bytes 3076
  46.9 12.3 %all-to-all-start = ((f32[16,8,128]{2,1,0:T(8,128)}), f32[16,8,128]{2,1,0:T(8,128)S(1)}, u32[]{:S(2)}, u32[]{:S(2)}) async-start(f32[16,8,128]{2,1,0:T(8,128)} %get-tuple-element.66), calls=%async_computation | async-start | bytes 131072 | tf_op jit(solution)/shard_map/all_to_all | solution.py:600
  51.5 5.4 %collective-permute-start.13 = (bf16[8,2,2,16,128]{4,3,2,1,0:T(8,128)(2,1)S(1)}, bf16[8,2,2,16,128]{4,3,2,1,0:T(8,128)(2,1)S(1)}, u32[]{:S(2)}, u32[]{:S(2)}) collective-permute-start(bf16[8,2,2,16,128]{4,3,2,1,0:T(8,128)(2,1)S(1)} %get-tuple-element.62), channel_id=1, source_target_pairs={{0,16},{16,0},{1,17},{17,1},{2,18},{18,2},{3,19},{19,3},{4,20},{20... | collective-permute-start | bytes 393224 | tf_op jit(solution)/shard_map/ppermute | solution.py:604
  51.6 1.1 %copy-start.6 = (f32[4,144,256]{2,1,0:T(8,128)S(1)}, f32[4,144,256]{2,1,0:T(8,128)}, u32[]{:S(2)}) copy-start(f32[4,144,256]{2,1,0:T(8,128)} %copy-done.5) | copy-start | bytes 1769476

commit v6 on v5

--- a/solution.py
+++ b/solution.py
@@ -520,13 +520,13 @@
 
 
 def sum_shares(residual, own, came, token):
-    outs = [shape((STEPS * ROWS, SHARE), F32), shape((16, 8, HEAD_SIZE), F32)]
+    outs = [shape((STEPS * ROWS, SHARE), F32), shape((16, 1, HEAD_SIZE), F32)]
     operands = [(a, VMEM) for a in (residual, own, *came)]
     return run(hidden_kernel, "hidden", 4, token, outs, operands, cost=4)
 
 
 def finish_kernel(hidden_ref, gain_ref, square_ref, out_ref):
-    square = jnp.sum(square_ref[...], axis=0)[0:1]
+    square = jnp.sum(square_ref[...], axis=0)
     square = jnp.sum(jnp.where(diagonal(), square, 0.0), axis=1, keepdims=True)
     scale = lax.rsqrt(square * (1.0 / COLUMNS) + EPSILON)
     out = hidden_ref[...] * scale * gain_ref[...].reshape(1, SHARE).astype(F32)

time: 60.6 us -> 60.6 us (level)
  no operation moved by 1% of the time
where the time goes in v6:
time: 60.6 us; the launch traced here: 59.5 us
  starting transfers between devices  26.9 us (44%)
  Pallas kernels  21.2 us (35%)
  waiting for transfers between devices  8.42 us (14%)
  local copies, waits for them, and re-layouts  2.13 us (4%)
  between operations  0.82 us (1%)
    pallas_call x12, Pallas kernels, run(): pl.pallas_call(with_token, out_shape=(*outs, TOKEN) if emit else tuple(ou...  21.2 us
    ppermute x1, starting transfers between devices, body(): far = lax.ppermute(packed, 'blk', [(i, i ^ 4) for i in range(8)])  7.28 us
    ppermute x3, starting transfers between devices, move_y(): return lax.ppermute(a, 'tp', [(i, (i + 4 * turn) % 16) for i in range(16)])  5.22 us
    ppermute x3, waiting for transfers between devices, move_y(): return lax.ppermute(a, 'tp', [(i, (i + 4 * turn) % 16) for i in range(16)])  4.92 us
    ppermute x4, starting transfers between devices, move_x(): lax.ppermute(a, 'blk', [(i, i // 4 * 4 + (i + turn) % 4) for i in range(8)])  4.21 us
    all_to_all x1, starting transfers between devices, body(): lax.all_to_all(square, 'tp', split_axis=0, concat_axis=0, tiled=True)  4.12 us
    ppermute x3, starting transfers between devices, move_z(): lax.ppermute(a, 'tp', [(i, i // 4 * 4 + (i + turn) % 4) for i in range(16)])  3.9 us
    ppermute x3, waiting for transfers between devices, move_z(): lax.ppermute(a, 'tp', [(i, i // 4 * 4 + (i + turn) % 4) for i in range(16)])  2.29 us
  transfers between devices with their start and end apart: 15, of which 4 were waited for; matrix products, arithmetic and copies ran while one was open for 0% of the time, Pallas kernels for 32%

profile of v6, /device:TPU:6, one launch (start us, length us, event | category | flops | bytes accessed | tf_op | source)
XLA Modules:
  0.0 59.5 jit_solution(5022649220801283252)
XLA Ops:
  0.6 1.6 %pack.1.refs_0_ = bf16[272,256]{1,0:T(8,128)(2,1)} custom-call(s32[1,16]{1,0:T(1,128)} %bitcast.6, bf16[1,2,64,256]{3,2,1,0:T(8,128)(2,1)} %bitcast.4, bf16[1,2,64,256]{3,2,1,0:T(8,128)(2,1)} %bitcast.5), custom_call_target="tpu_custom_call" | custom-call | flops 1024 | bytes 1024 | tf_op jit(solution)/shard_map/pack/pallas_call | solution.py:72
  2.2 0.0 copy-start
  2.2 0.0 copy-start.2
  2.2 0.0 copy-start.4
  2.3 7.3 %collective-permute-start.1 = (bf16[272,256]{1,0:T(8,128)(2,1)}, bf16[272,256]{1,0:T(8,128)(2,1)S(1)}, u32[]{:S(2)}, u32[]{:S(2)}) collective-permute-start(bf16[272,256]{1,0:T(8,128)(2,1)} %pack.1.refs_0_), channel_id=1, source_target_pairs={{0,128},{32,160},{64,192},{96,224},{128,0},{160,32},{192,64},{224,... | collective-permute-start | bytes 417800 | tf_op jit(solution)/shard_map/ppermute | solution.py:574
  9.5 1.0 %collective-permute-start = (bf16[272,256]{1,0:T(8,128)(2,1)}, bf16[272,256]{1,0:T(8,128)(2,1)S(1)}, u32[]{:S(2)}, u32[]{:S(2)}) collective-permute-start(bf16[272,256]{1,0:T(8,128)(2,1)} %pack.1.refs_0_), channel_id=1, source_target_pairs={{0,1},{1,0},{2,3},{3,2},{4,5},{5,4},{6,7},{7,6},{8,9},{9,8},{10,11... | collective-permute-start | bytes 417800 | tf_op jit(solution)/shard_map/ppermute | solution.py:573
  10.5 8.3 %decode.1 = (f32[64,2048]{1,0:T(8,128)}, bf16[64,2048]{1,0:T(8,128)(2,1)}, bf16[64,2048]{1,0:T(8,128)(2,1)}, bf16[64,2048]{1,0:T(8,128)(2,1)}) custom-call(s32[1,16]{1,0:T(1,128)} %refs_0_.5, bf16[1,4,16,512]{3,2,1,0:T(8,128)(2,1)} %refs_1_.5, bf16[1,4,2,16,128]{4,3,2,1,0:T(8,128)(2,1)} %refs_2_.1, bf16[1,2,16,256,128]{4,3,2,1,0:T(8,128)(2,1)} %refs_3_.1, ...), custom_call_target="tpu_custom_call" | custom-call | flops 10350001152 | bytes 1024 | tf_op jit(solution)/shard_map/decode/pallas_call | solution.py:72
  18.8 0.0 copy-start.8
  18.8 0.0 collective-permute-done.1.refs_2_
  18.9 1.1 %collective-permute-start.2 = (bf16[272,256]{1,0:T(8,128)(2,1)S(1)}, bf16[272,256]{1,0:T(8,128)(2,1)S(1)}, u32[]{:S(2)}, u32[]{:S(2)}) collective-permute-start(bf16[272,256]{1,0:T(8,128)(2,1)S(1)} %collective-permute-done.1.refs_2_), channel_id=1, source_target_pairs={{0,1},{1,0},{2,3},{3,2},{4,5},{5,4},{6,7},{7,6},{8,9},{9,8},{10,11... | collective-permute-start | bytes 417800 | tf_op jit(solution)/shard_map/ppermute | solution.py:577
  19.9 1.6 %collective-permute-start.6 = (bf16[64,2048]{1,0:T(8,128)(2,1)}, bf16[64,2048]{1,0:T(8,128)(2,1)S(1)}, u32[]{:S(2)}, u32[]{:S(2)}) collective-permute-start(bf16[64,2048]{1,0:T(8,128)(2,1)} %get-tuple-element.44), channel_id=1, source_target_pairs={{0,4},{1,5},{2,6},{3,7},{4,8},{5,9},{6,10},{7,11},{8,12},{9,13},{1... | collective-permute-start | bytes 786440 | tf_op jit(solution)/shard_map/ppermute | solution.py:547
  21.5 1.7 %collective-permute-start.7 = (bf16[64,2048]{1,0:T(8,128)(2,1)}, bf16[64,2048]{1,0:T(8,128)(2,1)S(1)}, u32[]{:S(2)}, u32[]{:S(2)}) collective-permute-start(bf16[64,2048]{1,0:T(8,128)(2,1)} %get-tuple-element.45), channel_id=1, source_target_pairs={{0,12},{1,13},{2,14},{3,15},{4,0},{5,1},{6,2},{7,3},{8,4},{9,5},{1... | collective-permute-start | bytes 786440 | tf_op jit(solution)/shard_map/ppermute | solution.py:547
  23.2 2.0 %collective-permute-start.5 = (bf16[64,2048]{1,0:T(8,128)(2,1)}, bf16[64,2048]{1,0:T(8,128)(2,1)S(1)}, u32[]{:S(2)}, u32[]{:S(2)}) collective-permute-start(bf16[64,2048]{1,0:T(8,128)(2,1)} %get-tuple-element.43), channel_id=1, source_target_pairs={{0,8},{1,9},{2,10},{3,11},{4,12},{5,13},{6,14},{7,15},{8,0},{9,1},... | collective-permute-start | bytes 786440 | tf_op jit(solution)/shard_map/ppermute | solution.py:547
  25.2 0.0 collective-permute-done.refs_1_
  25.2 0.0 collective-permute-done.2.refs_3_
  25.2 0.0 copy-done
  25.2 0.6 collective-permute-start.4
  25.8 1.5 %collective-permute-start.3 = (bf16[1056,256]{1,0:T(8,128)(2,1)S(1)}, bf16[1056,256]{1,0:T(8,128)(2,1)S(1)}, u32[]{:S(2)}, u32[]{:S(2)}) collective-permute-start(bf16[1056,256]{1,0:T(8,128)(2,1)S(1)} %get-tuple-element.38.refs_2_.refs_0_), channel_id=1, source_target_pairs={{0,96},{32,0},{64,32},{96,64},{128,224},{160,128},{192,160},{224,1... | collective-permute-start | bytes 1622024 | tf_op jit(solution)/shard_map/ppermute | solution.py:543
  27.3 0.0 copy-done.2
  27.3 0.0 copy-done.4
  27.3 0.0 copy-start.7
  27.4 1.0 %copy-done.7 = f32[64,2048]{1,0:T(8,128)S(1)} copy-done((f32[64,2048]{1,0:T(8,128)S(1)}, f32[64,2048]{1,0:T(8,128)}, u32[]{:S(2)}) %copy-start.7) | copy-done | bytes 524312
  28.4 2.1 %attend.3 = (f32[4,8,256]{2,1,0:T(8,128)S(1)}, f32[4,144,256]{2,1,0:T(8,128)S(1)}, f32[8,128]{1,0:T(8,128)S(1)}) custom-call(s32[2]{0:T(128)S(1)} %copy-done.4, bf16[1,256,512]{2,1,0:T(8,128)(2,1)S(1)} %copy-done.2, bf16[1056,256]{1,0:T(8,128)(2,1)S(1)} %get-tuple-element.38.refs_2_.refs_0_, f32[64,2048]{1,0:T(8,128)S(1)} %copy-done.7, ...), custom_call_target="tpu_custom_call" | custom-call | flops 3450000896 | bytes 1024 | tf_op jit(solution)/shard_map/attend/pallas_call | solution.py:72
  30.5 0.0 collective-permute-done.6.refs_2_
  30.5 0.5 collective-permute-done.7.refs_3_
  31.0 4.5 %collective-permute-done.5.refs_1_ = bf16[64,2048]{1,0:T(8,128)(2,1)S(1)} collective-permute-done((bf16[64,2048]{1,0:T(8,128)(2,1)}, bf16[64,2048]{1,0:T(8,128)(2,1)S(1)}, u32[]{:S(2)}, u32[]{:S(2)}) %collective-permute-start.5) | collective-permute-done | bytes 262176 | tf_op jit(solution)/shard_map/ppermute | solution.py:547
  35.4 0.0 copy-done.8
  35.4 0.1 quarters.1
  35.5 1.1 %collective-permute-start.11 = (f32[64,512]{1,0:T(8,128)S(1)}, f32[64,512]{1,0:T(8,128)S(1)}, u32[]{:S(2)}, u32[]{:S(2)}) collective-permute-start(f32[64,512]{1,0:T(8,128)S(1)} %get-tuple-element.55), channel_id=1, source_target_pairs={{0,1},{1,2},{2,3},{3,0},{4,5},{5,6},{6,7},{7,4},{8,9},{9,10},{10,1... | collective-permute-start | bytes 393224 | tf_op jit(solution)/shard_map/ppermute | solution.py:551
  36.7 2.8 %collective-permute-start.12 = (f32[64,512]{1,0:T(8,128)S(1)}, f32[64,512]{1,0:T(8,128)S(1)}, u32[]{:S(2)}, u32[]{:S(2)}) collective-permute-start(f32[64,512]{1,0:T(8,128)S(1)} %get-tuple-element.56), channel_id=1, source_target_pairs={{0,3},{1,0},{2,1},{3,2},{4,7},{5,4},{6,5},{7,6},{8,11},{9,8},{10,9... | collective-permute-start | bytes 393224 | tf_op jit(solution)/shard_map/ppermute | solution.py:551
  39.5 0.0 collective-permute-start.10
  39.5 0.0 collective-permute-done.4.refs_2_.refs_0_.refs_1_
  39.5 0.0 copy-start.3
  39.5 2.1 %attend.4 = (f32[4,8,256]{2,1,0:T(8,128)S(1)}, f32[4,144,256]{2,1,0:T(8,128)S(1)}, f32[8,128]{1,0:T(8,128)S(1)}) custom-call(s32[2]{0:T(128)S(1)} %copy-done.4, bf16[1,256,512]{2,1,0:T(8,128)(2,1)S(1)} %copy-done.2, bf16[1056,256]{1,0:T(8,128)(2,1)S(1)} %collective-permute-done.4.refs_2_.refs_0_.refs_1_, f32[4,8,256]{2,1,0:T(8,128)S(1)} %get-tuple-element.41.refs_3_, ...), custom_call_target="tpu_custom_call" | custom-call | flops 3450000896 | bytes 1024 | tf_op jit(solution)/shard_map/attend/pallas_call | solution.py:72
  41.6 0.0 copy-start.5
  41.6 0.0 collective-permute-done.3.refs_1_.refs_2_
  41.7 0.6 collective-permute-start.8
  42.2 1.5 %collective-permute-start.9 = (bf16[528,256]{1,0:T(8,128)(2,1)S(1)}, bf16[528,256]{1,0:T(8,128)(2,1)S(1)}, u32[]{:S(2)}, u32[]{:S(2)}) collective-permute-start(bf16[528,256]{1,0:T(8,128)(2,1)S(1)} %get-tuple-element.50), channel_id=1, source_target_pairs={{0,96},{32,0},{64,32},{96,64},{128,224},{160,128},{192,160},{224,1... | collective-permute-start | bytes 811016 | tf_op jit(solution)/shard_map/ppermute | solution.py:543
  43.8 2.3 %collective-permute-done.10.refs_2_ = bf16[64,512]{1,0:T(8,128)(2,1)S(1)} collective-permute-done((bf16[64,512]{1,0:T(8,128)(2,1)S(1)}, bf16[64,512]{1,0:T(8,128)(2,1)S(1)}, u32[]{:S(2)}, u32[]{:S(2)}) %collective-permute-start.10) | collective-permute-done | bytes 65568 | tf_op jit(solution)/shard_map/ppermute | solution.py:551
  46.1 0.0 collective-permute-done.11.refs_3_
  46.1 0.0 collective-permute-done.12.refs_4_
  46.1 0.0 copy-done.3
  46.1 0.7 %hidden.1 = (f32[64,512]{1,0:T(8,128)S(1)}, f32[16,1,128]{2,1,0:T(1,128)}, f32[8,128]{1,0:T(8,128)S(1)}) custom-call(bf16[1,4,16,512]{3,2,1,0:T(8,128)(2,1)S(1)} %copy-done.3, f32[64,512]{1,0:T(8,128)S(1)} %get-tuple-element.53.refs_1_, bf16[64,512]{1,0:T(8,128)(2,1)S(1)} %collective-permute-done.10.refs_2_, f32[64,512]{1,0:T(8,128)S(1)} %collective-permute-done.11.refs_3_, ...), custom_call_target="tpu_custom_call" | custom-call | flops 4600001024 | bytes 1024 | tf_op jit(solution)/shard_map/hidden/pallas_call | solution.py:72
  46.8 0.0 copy-done.5
  46.8 0.0 copy-start.1
  46.8 4.1 %all-to-all-start = ((f32[16,1,128]{2,1,0:T(1,128)}), f32[16,1,128]{2,1,0:T(1,128)S(1)}, u32[]{:S(2)}, u32[]{:S(2)}) async-start(f32[16,1,128]{2,1,0:T(1,128)} %get-tuple-element.66), calls=%async_computation | async-start | bytes 16384 | tf_op jit(solution)/shard_map/all_to_all | solution.py:600
  51.0 0.0 collective-permute-done.8.refs_3_
  51.0 0.0 collective-permute-done.9.refs_4_
  51.0 0.5 pages.1
  51.5 0.1 collective-permute-start.13
  51.6 0.0 copy-start.6
  51.6 1.1 %copy-done.6 = f32[4,144,256]{2,1,0:T(8,128)S(1)} copy-done((f32[4,144,256]{2,1,0:T(8,128)S(1)}, f32[4,144,256]{2,1,0:T(8,128)}, u32[]{:S(2)}) %copy-start.6) | copy-done | bytes 589848
  52.6 4.2 %attend.5 = (bf16[1,256,512]{2,1,0:T(8,128)(2,1)}, f32[8,128]{1,0:T(8,128)S(1)}) custom-call(s32[2]{0:T(128)S(1)} %copy-done.4, bf16[1,256,512]{2,1,0:T(8,128)(2,1)S(1)} %copy-done.2, bf16[1056,256]{1,0:T(8,128)(2,1)S(1)} %collective-permute-done.3.refs_1_.refs_2_, bf16[528,256]{1,0:T(8,128)(2,1)S(1)} %collective-permute-done.8.refs_3_, ...), custom_call_target="tpu_custom_call" | custom-call | flops 3450000896 | bytes 1024 | tf_op jit(solution)/shard_map/attend/pallas_call | solution.py:72
  56.8 0.0 collective-permute-done.13.refs_1_
  56.8 0.7 %pool.1 = (bf16[8,2,2,2,16,128]{5,4,3,2,1,0:T(8,128)(2,1)}, f32[8,128]{1,0:T(8,128)S(1)}) custom-call(bf16[8,2,2,16,128]{4,3,2,1,0:T(8,128)(2,1)S(1)} %get-tuple-element.61.refs_0_, bf16[8,2,2,16,128]{4,3,2,1,0:T(8,128)(2,1)S(1)} %collective-permute-done.13.refs_1_, f32[8,128]{1,0:T(8,128)S(1)} %get-tuple-element.63.refs_2_), custom_call_target="tpu_custom_call" | custom-call | flops 1024 | bytes 1024 | tf_op jit(solution)/shard_map/pool/pallas_call | solution.py:72
  57.6 1.2 %all-to-all-done.refs_2_ = f32[16,1,128]{2,1,0:T(1,128)S(1)} async-done(((f32[16,1,128]{2,1,0:T(1,128)}), f32[16,1,128]{2,1,0:T(1,128)S(1)}, u32[]{:S(2)}, u32[]{:S(2)}) %all-to-all-start) | async-done | bytes 8224 | tf_op jit(solution)/shard_map/all_to_all | solution.py:600
  58.8 0.0 copy-done.1
  58.8 0.7 %finish.1 = (bf16[1,4,16,512]{3,2,1,0:T(8,128)(2,1)}, f32[8,128]{1,0:T(8,128)}) custom-call(f32[64,512]{1,0:T(8,128)S(1)} %get-tuple-element.65.refs_0_, bf16[512]{0:T(512)(128)(2,1)S(1)} %copy-done.1, f32[16,1,128]{2,1,0:T(1,128)S(1)} %all-to-all-done.refs_2_, f32[8,128]{1,0:T(8,128)S(1)} %get-tuple-element.67.refs_3_), custom_call_target="tpu_custom_call" | custom-call | flops 1024 | bytes 1024 | tf_op jit(solution)/shard_map/finish/pallas_call | solution.py:72
  (2 shorter events, 0.1 us)
Async XLA Ops:
  2.2 23.0 %copy-start = (bf16[272,256]{1,0:T(8,128)(2,1)S(1)}, bf16[272,256]{1,0:T(8,128)(2,1)}, u32[]{:S(2)}) copy-start(bf16[272,256]{1,0:T(8,128)(2,1)} %pack.1.refs_0_) | copy-start | bytes 417796
  2.2 25.1 %copy-start.2 = (bf16[1,256,512]{2,1,0:T(8,128)(2,1)S(1)}, bf16[1,256,512]{2,1,0:T(8,128)(2,1)}, u32[]{:S(2)}) copy-start(bf16[1,256,512]{2,1,0:T(8,128)(2,1)} %refs_1_.8) | copy-start | bytes 786436
  2.2 25.1 %copy-start.4 = (s32[2]{0:T(128)S(1)}, s32[2]{0:T(128)}, u32[]{:S(2)}) copy-start(s32[2]{0:T(128)} %refs_0_.9) | copy-start | bytes 28
  2.3 16.6 %collective-permute-start.1 = (bf16[272,256]{1,0:T(8,128)(2,1)}, bf16[272,256]{1,0:T(8,128)(2,1)S(1)}, u32[]{:S(2)}, u32[]{:S(2)}) collective-permute-start(bf16[272,256]{1,0:T(8,128)(2,1)} %pack.1.refs_0_), channel_id=1, source_target_pairs={{0,128},{32,160},{64,192},{96,224},{128,0},{160,32},{192,64},{224,... | collective-permute-start | bytes 417800 | tf_op jit(solution)/shard_map/ppermute | solution.py:574
  9.5 15.6 %collective-permute-start = (bf16[272,256]{1,0:T(8,128)(2,1)}, bf16[272,256]{1,0:T(8,128)(2,1)S(1)}, u32[]{:S(2)}, u32[]{:S(2)}) collective-permute-start(bf16[272,256]{1,0:T(8,128)(2,1)} %pack.1.refs_0_), channel_id=1, source_target_pairs={{0,1},{1,0},{2,3},{3,2},{4,5},{5,4},{6,7},{7,6},{8,9},{9,8},{10,11... | collective-permute-start | bytes 417800 | tf_op jit(solution)/shard_map/ppermute | solution.py:573
  18.8 16.6 %copy-start.8 = (f32[64,2048]{1,0:T(8,128)S(1)}, f32[64,2048]{1,0:T(8,128)}, u32[]{:S(2)}) copy-start(f32[64,2048]{1,0:T(8,128)} %get-tuple-element.39.refs_3_.refs_0_) | copy-start | bytes 1572868
  18.9 6.3 %collective-permute-start.2 = (bf16[272,256]{1,0:T(8,128)(2,1)S(1)}, bf16[272,256]{1,0:T(8,128)(2,1)S(1)}, u32[]{:S(2)}, u32[]{:S(2)}) collective-permute-start(bf16[272,256]{1,0:T(8,128)(2,1)S(1)} %collective-permute-done.1.refs_2_), channel_id=1, source_target_pairs={{0,1},{1,0},{2,3},{3,2},{4,5},{5,4},{6,7},{7,6},{8,9},{9,8},{10,11... | collective-permute-start | bytes 417800 | tf_op jit(solution)/shard_map/ppermute | solution.py:577
  19.9 10.6 %collective-permute-start.6 = (bf16[64,2048]{1,0:T(8,128)(2,1)}, bf16[64,2048]{1,0:T(8,128)(2,1)S(1)}, u32[]{:S(2)}, u32[]{:S(2)}) collective-permute-start(bf16[64,2048]{1,0:T(8,128)(2,1)} %get-tuple-element.44), channel_id=1, source_target_pairs={{0,4},{1,5},{2,6},{3,7},{4,8},{5,9},{6,10},{7,11},{8,12},{9,13},{1... | collective-permute-start | bytes 786440 | tf_op jit(solution)/shard_map/ppermute | solution.py:547
  21.5 9.5 %collective-permute-start.7 = (bf16[64,2048]{1,0:T(8,128)(2,1)}, bf16[64,2048]{1,0:T(8,128)(2,1)S(1)}, u32[]{:S(2)}, u32[]{:S(2)}) collective-permute-start(bf16[64,2048]{1,0:T(8,128)(2,1)} %get-tuple-element.45), channel_id=1, source_target_pairs={{0,12},{1,13},{2,14},{3,15},{4,0},{5,1},{6,2},{7,3},{8,4},{9,5},{1... | collective-permute-start | bytes 786440 | tf_op jit(solution)/shard_map/ppermute | solution.py:547
  23.2 12.2 %collective-permute-start.5 = (bf16[64,2048]{1,0:T(8,128)(2,1)}, bf16[64,2048]{1,0:T(8,128)(2,1)S(1)}, u32[]{:S(2)}, u32[]{:S(2)}) collective-permute-start(bf16[64,2048]{1,0:T(8,128)(2,1)} %get-tuple-element.43), channel_id=1, source_target_pairs={{0,8},{1,9},{2,10},{3,11},{4,12},{5,13},{6,14},{7,15},{8,0},{9,1},... | collective-permute-start | bytes 786440 | tf_op jit(solution)/shard_map/ppermute | solution.py:547
  25.2 14.2 %collective-permute-start.4 = (bf16[1056,256]{1,0:T(8,128)(2,1)S(1)}, bf16[1056,256]{1,0:T(8,128)(2,1)S(1)}, u32[]{:S(2)}, u32[]{:S(2)}) collective-permute-start(bf16[1056,256]{1,0:T(8,128)(2,1)S(1)} %get-tuple-element.38.refs_2_.refs_0_), channel_id=1, source_target_pairs={{0,32},{32,64},{64,96},{96,0},{128,160},{160,192},{192,224},{224,1... | collective-permute-start | bytes 1622024 | tf_op jit(solution)/shard_map/ppermute | solution.py:543
  25.8 15.8 %collective-permute-start.3 = (bf16[1056,256]{1,0:T(8,128)(2,1)S(1)}, bf16[1056,256]{1,0:T(8,128)(2,1)S(1)}, u32[]{:S(2)}, u32[]{:S(2)}) collective-permute-start(bf16[1056,256]{1,0:T(8,128)(2,1)S(1)} %get-tuple-element.38.refs_2_.refs_0_), channel_id=1, source_target_pairs={{0,96},{32,0},{64,32},{96,64},{128,224},{160,128},{192,160},{224,1... | collective-permute-start | bytes 1622024 | tf_op jit(solution)/shard_map/ppermute | solution.py:543
  27.3 1.0 %copy-start.7 = (f32[64,2048]{1,0:T(8,128)S(1)}, f32[64,2048]{1,0:T(8,128)}, u32[]{:S(2)}) copy-start(f32[64,2048]{1,0:T(8,128)} %get-tuple-element.39.refs_3_.refs_0_) | copy-start | bytes 1572868
  35.5 10.5 %collective-permute-start.11 = (f32[64,512]{1,0:T(8,128)S(1)}, f32[64,512]{1,0:T(8,128)S(1)}, u32[]{:S(2)}, u32[]{:S(2)}) collective-permute-start(f32[64,512]{1,0:T(8,128)S(1)} %get-tuple-element.55), channel_id=1, source_target_pairs={{0,1},{1,2},{2,3},{3,0},{4,5},{5,6},{6,7},{7,4},{8,9},{9,10},{10,1... | collective-permute-start | bytes 393224 | tf_op jit(solution)/shard_map/ppermute | solution.py:551
  36.7 9.4 %collective-permute-start.12 = (f32[64,512]{1,0:T(8,128)S(1)}, f32[64,512]{1,0:T(8,128)S(1)}, u32[]{:S(2)}, u32[]{:S(2)}) collective-permute-start(f32[64,512]{1,0:T(8,128)S(1)} %get-tuple-element.56), channel_id=1, source_target_pairs={{0,3},{1,0},{2,1},{3,2},{4,7},{5,4},{6,5},{7,6},{8,11},{9,8},{10,9... | collective-permute-start | bytes 393224 | tf_op jit(solution)/shard_map/ppermute | solution.py:551
  39.5 6.6 %collective-permute-start.10 = (bf16[64,512]{1,0:T(8,128)(2,1)S(1)}, bf16[64,512]{1,0:T(8,128)(2,1)S(1)}, u32[]{:S(2)}, u32[]{:S(2)}) collective-permute-start(bf16[64,512]{1,0:T(8,128)(2,1)S(1)} %get-tuple-element.54), channel_id=1, source_target_pairs={{0,2},{1,3},{2,0},{3,1},{4,6},{5,7},{6,4},{7,5},{8,10},{9,11},{10,... | collective-permute-start | bytes 196616 | tf_op jit(solution)/shard_map/ppermute | solution.py:551
  39.5 6.6 %copy-start.3 = (bf16[1,4,16,512]{3,2,1,0:T(8,128)(2,1)S(1)}, bf16[1,4,16,512]{3,2,1,0:T(8,128)(2,1)}, u32[]{:S(2)}) copy-start(bf16[1,4,16,512]{3,2,1,0:T(8,128)(2,1)} %refs_0_.8) | copy-start | bytes 196612
  41.6 5.2 %copy-start.5 = (f32[4,144,256]{2,1,0:T(8,128)}, f32[4,144,256]{2,1,0:T(8,128)S(1)}, u32[]{:S(2)}) copy-start(f32[4,144,256]{2,1,0:T(8,128)S(1)} %get-tuple-element.52.refs_6_) | copy-start | bytes 1769476
  41.7 9.3 %collective-permute-start.8 = (bf16[528,256]{1,0:T(8,128)(2,1)S(1)}, bf16[528,256]{1,0:T(8,128)(2,1)S(1)}, u32[]{:S(2)}, u32[]{:S(2)}) collective-permute-start(bf16[528,256]{1,0:T(8,128)(2,1)S(1)} %get-tuple-element.49), channel_id=1, source_target_pairs={{0,32},{32,64},{64,96},{96,0},{128,160},{160,192},{192,224},{224,1... | collective-permute-start | bytes 811016 | tf_op jit(solution)/shard_map/ppermute | solution.py:543
  42.2 8.7 %collective-permute-start.9 = (bf16[528,256]{1,0:T(8,128)(2,1)S(1)}, bf16[528,256]{1,0:T(8,128)(2,1)S(1)}, u32[]{:S(2)}, u32[]{:S(2)}) collective-permute-start(bf16[528,256]{1,0:T(8,128)(2,1)S(1)} %get-tuple-element.50), channel_id=1, source_target_pairs={{0,96},{32,0},{64,32},{96,64},{128,224},{160,128},{192,160},{224,1... | collective-permute-start | bytes 811016 | tf_op jit(solution)/shard_map/ppermute | solution.py:543
  46.8 11.9 %copy-start.1 = (bf16[512]{0:T(512)(128)(2,1)S(1)}, bf16[512]{0:T(512)(128)(2,1)}, u32[]{:S(2)}) copy-start(bf16[512]{0:T(512)(128)(2,1)} %refs_1_.9) | copy-start | bytes 3076
  46.8 11.9 %all-to-all-start = ((f32[16,1,128]{2,1,0:T(1,128)}), f32[16,1,128]{2,1,0:T(1,128)S(1)}, u32[]{:S(2)}, u32[]{:S(2)}) async-start(f32[16,1,128]{2,1,0:T(1,128)} %get-tuple-element.66), calls=%async_computation | async-start | bytes 16384 | tf_op jit(solution)/shard_map/all_to_all | solution.py:600
  51.5 5.4 %collective-permute-start.13 = (bf16[8,2,2,16,128]{4,3,2,1,0:T(8,128)(2,1)S(1)}, bf16[8,2,2,16,128]{4,3,2,1,0:T(8,128)(2,1)S(1)}, u32[]{:S(2)}, u32[]{:S(2)}) collective-permute-start(bf16[8,2,2,16,128]{4,3,2,1,0:T(8,128)(2,1)S(1)} %get-tuple-element.62), channel_id=1, source_target_pairs={{0,16},{16,0},{1,17},{17,1},{2,18},{18,2},{3,19},{19,3},{4,20},{20... | collective-permute-start | bytes 393224 | tf_op jit(solution)/shard_map/ppermute | solution.py:604
  51.6 1.1 %copy-start.6 = (f32[4,144,256]{2,1,0:T(8,128)S(1)}, f32[4,144,256]{2,1,0:T(8,128)}, u32[]{:S(2)}) copy-start(f32[4,144,256]{2,1,0:T(8,128)} %copy-done.5) | copy-start | bytes 1769476
